TPU v7x, 32 devices: a whole 2x2x4 slice. The times are simulated.
32 devices in a mesh: lat: 4 (over z), lon: 8 (over y, x, core).
Axes of the slice: x: 2, y: 2, z: 4, core: 2. Of those that a mesh axis runs over, the one named last changes fastest.
Arguments:
- state_field: bfloat16 [96, 512, 640], P('lat', 'lon'), may hold values from -6 to 6
- filters: float32 [96, 5, 5, 9], P('lat'), may hold values from -0.9 to 0.9
- band_edges: int32 [96, 2], P('lat'), may hold values from 0 to 96, as said below
- basis_mask: int32 [96, 5], P('lat'), may hold values 0 or 1
- weights_one: float32 [5, 640], replicated, may hold values from -2.5 to 2.5
- weights_two: float32 [5, 640], replicated, may hold values from -2.5 to 2.5
Outputs:
- mixed_field: bfloat16 [96, 512, 640], P('lat', 'lon')
Inputs may be any that keep to these rules, and one draw needn't show every extreme that they name: For each row y, max(y - 2, 0) <= band_edges[y,0] <= max(y - 1, 0) and min(y + 2, 96) <= band_edges[y,1] <= min(y + 3, 96); some row's band spans from y - 2 to y + 3.
All inputs are finite; a program needn't handle non-finite values. No bound on the sum of `basis_mask` on one device may be relied on, other than what follows from the above.
Results may differ from a plain program's by a relative error of at most 0.0049.
Values may be sent and summed in bfloat16 or wider, within the bound.
No kernel may reach another device: no remote copies, remote signals or barrier semaphores. Data moves between devices by JAX's collectives and lax.ppermute only.
A program may use at most 64 MiB of HBM per device.

v0:
```python
import jax
import jax.numpy as jnp
from jax import lax
from jax.sharding import PartitionSpec as P

LAT_REACH = 2
LON_REACH = 4


def with_halo(x, sides, width, wrap):
    for axis, dim in sides:
        peers, length = (lax.axis_size(axis), x.shape[dim])
        up = [(i, (i + 1) % peers) for i in range(peers if wrap else peers - 1)]
        down = [(j, i) for i, j in up]
        last = lax.slice_in_dim(x, length - width, length, axis=dim)
        leading = lax.slice_in_dim(x, 0, width, axis=dim)
        before = lax.ppermute(last, axis, up)
        after = lax.ppermute(leading, axis, down)
        x = jnp.concatenate([before, x, after], axis=dim)
    return x


def build_filter(filters, band_edges, basis_mask):
    first_row = lax.axis_index("lat") * filters.shape[0]
    latitude = first_row + jnp.arange(filters.shape[0], dtype=jnp.int32)
    source = latitude[:, None] + jnp.arange(2 * LAT_REACH + 1, dtype=jnp.int32)[None, :] - LAT_REACH
    inside = (source >= band_edges[:, 0:1]) & (source < band_edges[:, 1:2])
    return (
        filters
        * inside.astype(jnp.float32)[:, None, :, None]
        * basis_mask.astype(jnp.float32)[:, :, None, None]
    )


def widen_rims(values):
    values = with_halo(values, (("lon", 1),), LON_REACH, True)
    values = jnp.pad(values, ((2 * LAT_REACH, 2 * LAT_REACH), (0, 0), (0, 0)))
    return values


def accumulate(extended, coefficients, lon_dim):
    out_rows = coefficients.shape[0]
    span_cells = extended.shape[lon_dim] - 2 * LON_REACH
    running = None
    for offset in range(2 * LAT_REACH + 1):
        for lon_lag in range(2 * LON_REACH + 1):
            window = extended[offset : offset + out_rows, lon_lag : lon_lag + span_cells, :]
            factor = coefficients[:, offset, lon_lag][:, None, :]
            product = factor * window
            running = product if running is None else running + product
    return running


def settle(partial_value):
    own_rows = partial_value.shape[0] - 2 * LAT_REACH
    middle = partial_value[LAT_REACH : LAT_REACH + own_rows]
    both_rims = jnp.concatenate(
        [partial_value[:LAT_REACH], partial_value[own_rows + LAT_REACH :]], axis=0
    )
    widened = with_halo(both_rims, (("lat", 0),), LAT_REACH, False)
    from_below = widened[:LAT_REACH]
    from_above = widened[widened.shape[0] - LAT_REACH :]
    lower_fill = jnp.pad(from_below, ((0, own_rows - LAT_REACH), (0, 0), (0, 0)))
    upper_fill = jnp.pad(from_above, ((own_rows - LAT_REACH, 0), (0, 0), (0, 0)))
    return middle + lower_fill + upper_fill


def convolve(values, kernel, weights, lon_dim):
    coefficients = jnp.einsum("ykdm,kc->ydmc", kernel, weights, precision=lax.Precision.HIGHEST)
    running = accumulate(widen_rims(values), coefficients, lon_dim)
    running = settle(running)
    return running


def per_device(state_field, filters, band_edges, basis_mask, weights_one, weights_two):
    kernel = build_filter(filters, band_edges, basis_mask)
    kernel = with_halo(kernel, (("lat", 0),), LAT_REACH, False)
    lon_dim = 1
    hidden = jax.nn.gelu(
        convolve(state_field, kernel, weights_one, lon_dim), approximate=False
    ).astype(jnp.bfloat16)
    result = convolve(hidden, kernel, weights_two, lon_dim).astype(jnp.bfloat16)
    return result


def solution(mesh):
    placed = (
        P("lat", "lon", None),
        P("lat", None, None, None),
        P("lat", None),
        P("lat", None),
        P(),
        P(),
    )
    return jax.shard_map(
        per_device, mesh=mesh, in_specs=placed, out_specs=P("lat", "lon", None), check_vma=False
    )
```

profile of v0, /device:TPU:0, one launch (start us, length us, event | category | flops | bytes accessed | tf_op | source)
XLA Modules:
  0.0 191.6 jit_solution(5572368350413474291)
XLA Ops:
  0.0 0.0 copy-start
  0.0 0.8 slice_bitcast_fusion.91
  0.8 0.7 convert_element_type.296
  1.5 1.0 fusion.19
  2.4 0.1 fusion.32
  2.5 4.9 %collective-permute-start = (f32[2,5,5,9]{0,1,3,2:T(8,128)S(1)}, f32[2,5,5,9]{0,1,3,2:T(8,128)S(1)}, u32[]{:S(2)}, u32[]{:S(2)}) collective-permute-start(f32[2,5,5,9]{0,1,3,2:T(8,128)S(1)} %get-tuple-element.103), channel_id=1, source_target_pairs={{0,8},{8,16},{16,24},{1,9},{9,17},{17,25},{2,10},{10,18},{18,26},{... | collective-permute-start | bytes 5408 | tf_op jit(solution)/shard_map/ppermute | solution.py:17
  7.5 1.3 collective-permute-start.1
  8.8 1.2 fusion.31
  10.0 0.1 collective-permute-start.2
  10.0 0.0 copy-start.3
  10.0 2.6 %collective-permute-start.3 = (bf16[24,4,640]{2,1,0:T(4,128)(2,1)S(1)}, bf16[24,4,640]{2,1,0:T(4,128)(2,1)S(1)}, u32[]{:S(2)}, u32[]{:S(2)}) collective-permute-start(bf16[24,4,640]{2,1,0:T(4,128)(2,1)S(1)} %get-tuple-element.102), channel_id=1, source_target_pairs={{1,0},{2,1},{3,2},{4,3},{5,4},{6,5},{7,6},{0,7},{9,8},{10,9},{11,1... | collective-permute-start | bytes 368648 | tf_op jit(solution)/shard_map/ppermute | solution.py:18
  12.7 0.0 collective-permute-done
  12.7 2.8 %collective-permute-done.1 = f32[2,5,5,9]{0,1,3,2:T(8,128)S(1)} collective-permute-done((f32[2,5,5,9]{0,1,3,2:T(8,128)S(1)}, f32[2,5,5,9]{0,1,3,2:T(8,128)S(1)}, u32[]{:S(2)}, u32[]{:S(2)}) %collective-permute-start.1) | collective-permute-done | bytes 1832 | tf_op jit(solution)/shard_map/ppermute | solution.py:18
  15.5 0.0 copy-done
  15.5 4.0 %fusion.20 = f32[28,5,9,640]{3,0,2,1:T(8,128)S(1)} fusion(f32[5,640]{1,0:T(8,128)S(1)} %copy-done, f32[2,5,5,9]{0,1,3,2:T(8,128)S(1)} %collective-permute-done.1, f32[24,5,5,9]{0,1,3,2:T(8,128)S(1)} %fusion.19, f32[2,5,5,9]{0,1,3,2:T(8,128)S(1)} %collective-permute-done), kind=kOutput, calls=%fused_computation.129 | convolution fusion | flops 48396600 | bytes 3263600 | tf_op jit(solution)/shard_map/ykdm,kc->ydmc/dot_general | solution.py:69
  19.5 1.0 slice_bitcast_fusion.87
  20.5 0.0 copy-start.2
  20.5 1.1 slice_bitcast_fusion.88
  21.6 0.0 copy-done.3
  21.6 5.8 %fusion.22 = f32[28,5,9,640]{3,0,2,1:T(8,128)} fusion(f32[5,640]{1,0:T(8,128)S(1)} %copy-done.3, f32[2,5,5,9]{0,1,3,2:T(8,128)S(1)} %collective-permute-done.1, f32[24,5,5,9]{0,1,3,2:T(8,128)S(1)} %fusion.19, f32[2,5,5,9]{0,1,3,2:T(8,128)S(1)} %collective-permute-done), kind=kOutput, calls=%fused_computation.131 | convolution fusion | flops 48396600 | bytes 3263600 | tf_op jit(solution)/shard_map/ykdm,kc->ydmc/dot_general | solution.py:69
  27.4 0.8 slice_bitcast_fusion.86
  28.3 0.0 collective-permute-done.2
  28.3 0.0 collective-permute-done.3
  28.3 0.0 copy-done.2
  28.3 3.4 %fusion.18 = bf16[32,72,640]{2,1,0:T(8,128)(2,1)S(1)} fusion(bf16[24,4,640]{2,1,0:T(4,128)(2,1)S(1)} %collective-permute-done.3, bf16[24,64,640]{2,1,0:T(8,128)(2,1)S(1)} %copy-done.2, bf16[24,4,640]{2,1,0:T(4,128)(2,1)S(1)} %collective-permute-done.2), kind=kLoop, calls=%fused_computation.35 | loop fusion | flops 17694720 | bytes 5160960 | tf_op jit(solution)/shard_map/concatenate | solution.py:19
  31.7 53.4 %multiply_add_fusion.1 = f32[28,64,640]{2,1,0:T(8,128)} fusion(bf16[32,72,640]{2,1,0:T(8,128)(2,1)S(1)} %fusion.18, f32[28,640]{1,0:T(8,128)} %get-tuple-element.55, f32[28,640]{1,0:T(8,128)} %get-tuple-element.56, f32[28,640]{1,0:T(8,128)} %get-tuple-element.57, f32[28,640]{1,0:T(8,128)} %get-tuple-element.58, f32[28,640]{1,0:T(8,128)} %get-tuple-element.59, ...), kind=kLoop, calls=%fused_computation.5 | loop fusion | flops 153681920 | bytes 111032320 | tf_op jit(solution)/shard_map/add | solution.py:50
  85.1 0.0 copy-start.1
  85.1 1.3 fusion.29
  86.3 3.6 %collective-permute-start.4 = (f32[2,64,640]{2,1,0:T(8,128)S(1)}, f32[2,64,640]{2,1,0:T(8,128)S(1)}, u32[]{:S(2)}, u32[]{:S(2)}) collective-permute-start(f32[2,64,640]{2,1,0:T(8,128)S(1)} %get-tuple-element.7), channel_id=1, source_target_pairs={{0,8},{8,16},{16,24},{1,9},{9,17},{17,25},{2,10},{10,18},{18,26},{... | collective-permute-start | bytes 983048 | tf_op jit(solution)/shard_map/ppermute | solution.py:17
  90.0 1.3 collective-permute-start.5
  91.3 2.5 %slice_bitcast_fusion.43 = (f32[28,640]{1,0:T(8,128)S(1)}, f32[28,640]{1,0:T(8,128)S(1)}, f32[28,640]{1,0:T(8,128)S(1)}, f32[28,640]{1,0:T(8,128)S(1)}, f32[28,6...) fusion(f32[28,5,9,640]{3,0,2,1:T(8,128)} %fusion.22), kind=kLoop, calls=%fused_computation.82 | loop fusion | bytes 2723840 | tf_op jit(solution)/shard_map/mul | solution.py:49
  93.7 2.6 %slice_bitcast_fusion.89 = (f32[28,640]{1,0:T(8,128)}, f32[28,640]{1,0:T(8,128)}, f32[28,640]{1,0:T(8,128)}, f32[28,640]{1,0:T(8,128)}, f32[28,640]{1,0:T(8,128)...) fusion(f32[28,5,9,640]{3,0,2,1:T(8,128)} %fusion.22), kind=kLoop, calls=%fused_computation.128 | loop fusion | bytes 2723840 | tf_op jit(solution)/shard_map/mul | solution.py:49
  96.3 0.0 collective-permute-done.4
  96.3 3.5 %collective-permute-done.5 = f32[2,64,640]{2,1,0:T(8,128)S(1)} collective-permute-done((f32[2,64,640]{2,1,0:T(8,128)S(1)}, f32[2,64,640]{2,1,0:T(8,128)S(1)}, u32[]{:S(2)}, u32[]{:S(2)}) %collective-permute-start.5) | collective-permute-done | bytes 327712 | tf_op jit(solution)/shard_map/ppermute | solution.py:18
  99.9 0.0 copy-done.1
  99.9 9.0 %fusion.3 = bf16[24,64,640]{2,1,0:T(8,128)(2,1)S(1)} fusion(f32[2,64,640]{2,1,0:T(8,128)S(1)} %collective-permute-done.5, f32[2,64,640]{2,1,0:T(8,128)S(1)} %collective-permute-done.4, f32[28,64,640]{2,1,0:T(8,128)S(1)} %copy-done.1), kind=kLoop, calls=%fused_computation.8 | loop fusion | flops 65863680 | bytes 6553600 | tf_op jit(solution)/shard_map/convert_element_type | solution.py:81
  108.9 0.1 fusion.30
  109.0 0.1 collective-permute-start.6
  109.1 2.6 %collective-permute-start.7 = (bf16[24,4,640]{2,1,0:T(4,128)(2,1)S(1)}, bf16[24,4,640]{2,1,0:T(4,128)(2,1)S(1)}, u32[]{:S(2)}, u32[]{:S(2)}) collective-permute-start(bf16[24,4,640]{2,1,0:T(4,128)(2,1)S(1)} %get-tuple-element.100), channel_id=1, source_target_pairs={{1,0},{2,1},{3,2},{4,3},{5,4},{6,5},{7,6},{0,7},{9,8},{10,9},{11,1... | collective-permute-start | bytes 368648 | tf_op jit(solution)/shard_map/ppermute | solution.py:18
  111.7 1.9 %slice_bitcast_fusion.42 = (f32[28,640]{1,0:T(8,128)}, f32[28,640]{1,0:T(8,128)}, f32[28,640]{1,0:T(8,128)}, f32[28,640]{1,0:T(8,128)}, f32[28,640]{1,0:T(8,128)}, /*index=5*/f32[28,640]{1,0:T(8,128)}, f32[28,640]{1,0:T(8,128)}) fusion(f32[28,5,9,640]{3,0,2,1:T(8,128)} %fusion.22), kind=kLoop, calls=%fused_computation.81 | loop fusion | bytes 1003520 | tf_op jit(solution)/shard_map/mul | solution.py:49
  113.6 0.6 collective-permute-done.6
  114.3 0.0 collective-permute-done.7
  114.3 3.2 %select_maximum_fusion = bf16[32,72,640]{2,1,0:T(8,128)(2,1)S(1)} fusion(bf16[24,4,640]{2,1,0:T(4,128)(2,1)S(1)} %collective-permute-done.7, bf16[24,64,640]{2,1,0:T(8,128)(2,1)S(1)} %fusion.3, bf16[24,4,640]{2,1,0:T(4,128)(2,1)S(1)} %collective-permute-done.6), kind=kLoop, calls=%fused_computation.29 | loop fusion | flops 17694720 | bytes 5160960 | tf_op jit(solution)/shard_map/concatenate | solution.py:19
  117.4 53.4 %multiply_add_fusion = f32[28,64,640]{2,1,0:T(8,128)} fusion(bf16[32,72,640]{2,1,0:T(8,128)(2,1)S(1)} %select_maximum_fusion, f32[28,640]{1,0:T(8,128)} %get-tuple-element.10, f32[28,640]{1,0:T(8,128)} %get-tuple-element.11, f32[28,640]{1,0:T(8,128)} %get-tuple-element.12, f32[28,640]{1,0:T(8,128)} %get-tuple-element.13, f32[28,640]{1,0:T(8,128)} %get-tuple-element.14, ...), kind=kLoop, calls=%fused_computation.4 | loop fusion | flops 153681920 | bytes 111032320 | tf_op jit(solution)/shard_map/add | solution.py:50
  170.8 1.1 fusion.28
  172.0 3.5 %collective-permute-start.8 = (f32[2,64,640]{2,1,0:T(8,128)S(1)}, f32[2,64,640]{2,1,0:T(8,128)S(1)}, u32[]{:S(2)}, u32[]{:S(2)}) collective-permute-start(f32[2,64,640]{2,1,0:T(8,128)S(1)} %get-tuple-element.5), channel_id=1, source_target_pairs={{0,8},{8,16},{16,24},{1,9},{9,17},{17,25},{2,10},{10,18},{18,26},{... | collective-permute-start | bytes 983048 | tf_op jit(solution)/shard_map/ppermute | solution.py:17
  175.4 1.3 collective-permute-start.9
  176.7 6.5 %collective-permute-done.8 = f32[2,64,640]{2,1,0:T(8,128)S(1)} collective-permute-done((f32[2,64,640]{2,1,0:T(8,128)S(1)}, f32[2,64,640]{2,1,0:T(8,128)S(1)}, u32[]{:S(2)}, u32[]{:S(2)}) %collective-permute-start.8) | collective-permute-done | bytes 327712 | tf_op jit(solution)/shard_map/ppermute | solution.py:17
  183.3 4.6 %collective-permute-done.9 = f32[2,64,640]{2,1,0:T(8,128)S(1)} collective-permute-done((f32[2,64,640]{2,1,0:T(8,128)S(1)}, f32[2,64,640]{2,1,0:T(8,128)S(1)}, u32[]{:S(2)}, u32[]{:S(2)}) %collective-permute-start.9) | collective-permute-done | bytes 327712 | tf_op jit(solution)/shard_map/ppermute | solution.py:18
  187.9 3.7 %fusion.5 = bf16[24,64,640]{2,1,0:T(8,128)(2,1)} fusion(f32[28,64,640]{2,1,0:T(8,128)} %multiply_add_fusion, f32[2,64,640]{2,1,0:T(8,128)S(1)} %collective-permute-done.9, f32[2,64,640]{2,1,0:T(8,128)S(1)} %collective-permute-done.8), kind=kLoop, calls=%fused_computation.11 | loop fusion | flops 2949120 | bytes 6553600 | tf_op jit(solution)/shard_map/convert_element_type | solution.py:82
  (2 shorter events, 0.0 us)
Async XLA Ops:
  0.0 15.5 %copy-start = (f32[5,640]{1,0:T(8,128)S(1)}, f32[5,640]{1,0:T(8,128)}, u32[]{:S(2)}) copy-start(f32[5,640]{1,0:T(8,128)} %param.10) | copy-start | bytes 38404
  2.5 10.1 %collective-permute-start = (f32[2,5,5,9]{0,1,3,2:T(8,128)S(1)}, f32[2,5,5,9]{0,1,3,2:T(8,128)S(1)}, u32[]{:S(2)}, u32[]{:S(2)}) collective-permute-start(f32[2,5,5,9]{0,1,3,2:T(8,128)S(1)} %get-tuple-element.103), channel_id=1, source_target_pairs={{0,8},{8,16},{16,24},{1,9},{9,17},{17,25},{2,10},{10,18},{18,26},{... | collective-permute-start | bytes 5408 | tf_op jit(solution)/shard_map/ppermute | solution.py:17
  7.5 8.0 %collective-permute-start.1 = (f32[2,5,5,9]{0,1,3,2:T(8,128)S(1)}, f32[2,5,5,9]{0,1,3,2:T(8,128)S(1)}, u32[]{:S(2)}, u32[]{:S(2)}) collective-permute-start(f32[2,5,5,9]{0,1,3,2:T(8,128)S(1)} %get-tuple-element.104), channel_id=1, source_target_pairs={{8,0},{16,8},{24,16},{9,1},{17,9},{25,17},{10,2},{18,10},{26,18},{... | collective-permute-start | bytes 5408 | tf_op jit(solution)/shard_map/ppermute | solution.py:18
  10.0 18.3 %collective-permute-start.2 = (bf16[24,4,640]{2,1,0:T(4,128)(2,1)S(1)}, bf16[24,4,640]{2,1,0:T(4,128)(2,1)S(1)}, u32[]{:S(2)}, u32[]{:S(2)}) collective-permute-start(bf16[24,4,640]{2,1,0:T(4,128)(2,1)S(1)} %get-tuple-element.101), channel_id=1, source_target_pairs={{0,1},{1,2},{2,3},{3,4},{4,5},{5,6},{6,7},{7,0},{8,9},{9,10},{10,1... | collective-permute-start | bytes 368648 | tf_op jit(solution)/shard_map/ppermute | solution.py:17
  10.0 11.6 %copy-start.3 = (f32[5,640]{1,0:T(8,128)S(1)}, f32[5,640]{1,0:T(8,128)}, u32[]{:S(2)}) copy-start(f32[5,640]{1,0:T(8,128)} %param.11) | copy-start | bytes 38404
  10.0 18.2 %collective-permute-start.3 = (bf16[24,4,640]{2,1,0:T(4,128)(2,1)S(1)}, bf16[24,4,640]{2,1,0:T(4,128)(2,1)S(1)}, u32[]{:S(2)}, u32[]{:S(2)}) collective-permute-start(bf16[24,4,640]{2,1,0:T(4,128)(2,1)S(1)} %get-tuple-element.102), channel_id=1, source_target_pairs={{1,0},{2,1},{3,2},{4,3},{5,4},{6,5},{7,6},{0,7},{9,8},{10,9},{11,1... | collective-permute-start | bytes 368648 | tf_op jit(solution)/shard_map/ppermute | solution.py:18
  20.5 7.8 %copy-start.2 = (bf16[24,64,640]{2,1,0:T(8,128)(2,1)S(1)}, bf16[24,64,640]{2,1,0:T(8,128)(2,1)}, u32[]{:S(2)}) copy-start(bf16[24,64,640]{2,1,0:T(8,128)(2,1)} %param.6) | copy-start | bytes 5898244
  85.1 14.8 %copy-start.1 = (f32[28,64,640]{2,1,0:T(8,128)S(1)}, f32[28,64,640]{2,1,0:T(8,128)}, u32[]{:S(2)}) copy-start(f32[28,64,640]{2,1,0:T(8,128)} %multiply_add_fusion.1) | copy-start | bytes 13762564
  86.3 10.0 %collective-permute-start.4 = (f32[2,64,640]{2,1,0:T(8,128)S(1)}, f32[2,64,640]{2,1,0:T(8,128)S(1)}, u32[]{:S(2)}, u32[]{:S(2)}) collective-permute-start(f32[2,64,640]{2,1,0:T(8,128)S(1)} %get-tuple-element.7), channel_id=1, source_target_pairs={{0,8},{8,16},{16,24},{1,9},{9,17},{17,25},{2,10},{10,18},{18,26},{... | collective-permute-start | bytes 983048 | tf_op jit(solution)/shard_map/ppermute | solution.py:17
  90.0 9.9 %collective-permute-start.5 = (f32[2,64,640]{2,1,0:T(8,128)S(1)}, f32[2,64,640]{2,1,0:T(8,128)S(1)}, u32[]{:S(2)}, u32[]{:S(2)}) collective-permute-start(f32[2,64,640]{2,1,0:T(8,128)S(1)} %get-tuple-element.8), channel_id=1, source_target_pairs={{8,0},{16,8},{24,16},{9,1},{17,9},{25,17},{10,2},{18,10},{26,18},{... | collective-permute-start | bytes 983048 | tf_op jit(solution)/shard_map/ppermute | solution.py:18
  109.0 5.3 %collective-permute-start.6 = (bf16[24,4,640]{2,1,0:T(4,128)(2,1)S(1)}, bf16[24,4,640]{2,1,0:T(4,128)(2,1)S(1)}, u32[]{:S(2)}, u32[]{:S(2)}) collective-permute-start(bf16[24,4,640]{2,1,0:T(4,128)(2,1)S(1)} %get-tuple-element.99), channel_id=1, source_target_pairs={{0,1},{1,2},{2,3},{3,4},{4,5},{5,6},{6,7},{7,0},{8,9},{9,10},{10,1... | collective-permute-start | bytes 368648 | tf_op jit(solution)/shard_map/ppermute | solution.py:17
  109.1 5.2 %collective-permute-start.7 = (bf16[24,4,640]{2,1,0:T(4,128)(2,1)S(1)}, bf16[24,4,640]{2,1,0:T(4,128)(2,1)S(1)}, u32[]{:S(2)}, u32[]{:S(2)}) collective-permute-start(bf16[24,4,640]{2,1,0:T(4,128)(2,1)S(1)} %get-tuple-element.100), channel_id=1, source_target_pairs={{1,0},{2,1},{3,2},{4,3},{5,4},{6,5},{7,6},{0,7},{9,8},{10,9},{11,1... | collective-permute-start | bytes 368648 | tf_op jit(solution)/shard_map/ppermute | solution.py:18
  172.0 11.3 %collective-permute-start.8 = (f32[2,64,640]{2,1,0:T(8,128)S(1)}, f32[2,64,640]{2,1,0:T(8,128)S(1)}, u32[]{:S(2)}, u32[]{:S(2)}) collective-permute-start(f32[2,64,640]{2,1,0:T(8,128)S(1)} %get-tuple-element.5), channel_id=1, source_target_pairs={{0,8},{8,16},{16,24},{1,9},{9,17},{17,25},{2,10},{10,18},{18,26},{... | collective-permute-start | bytes 983048 | tf_op jit(solution)/shard_map/ppermute | solution.py:17
  175.4 12.4 %collective-permute-start.9 = (f32[2,64,640]{2,1,0:T(8,128)S(1)}, f32[2,64,640]{2,1,0:T(8,128)S(1)}, u32[]{:S(2)}, u32[]{:S(2)}) collective-permute-start(f32[2,64,640]{2,1,0:T(8,128)S(1)} %get-tuple-element.6), channel_id=1, source_target_pairs={{8,0},{16,8},{24,16},{9,1},{17,9},{25,17},{10,2},{18,10},{26,18},{... | collective-permute-start | bytes 983048 | tf_op jit(solution)/shard_map/ppermute | solution.py:18
where the time goes:
time: 192 us
  other arithmetic  128 us (67%)
  starting transfers between devices  21.3 us (11%)
  waiting for transfers between devices  18.1 us (9%)
  local copies, waits for them, and re-layouts  14.5 us (8%)
  matrix products  9.82 us (5%)
    add x2, other arithmetic, accumulate(): running = product if running is None else running + product  107 us
    ppermute x5, starting transfers between devices, with_halo(): before = lax.ppermute(last, axis, up)  12.2 us
    ppermute x5, waiting for transfers between devices, with_halo(): after = lax.ppermute(leading, axis, down)  10.9 us
    mul x6, local copies, waits for them, and re-layouts, accumulate(): product = factor * window  9.94 us
    dot_general x2, matrix products, convolve(): jnp.einsum('ykdm,kc->ydmc', kernel, weights, precision=lax.Precision.HIGH...  9.82 us
    ppermute x5, starting transfers between devices, with_halo(): after = lax.ppermute(leading, axis, down)  9.13 us
    convert_element_type x1, other arithmetic, per_device(): hidden = jax.nn.gelu(convolve(state_field, kernel, weights_one, lon_dim),...  9.03 us
    ppermute x5, waiting for transfers between devices, with_halo(): before = lax.ppermute(last, axis, up)  7.16 us
  transfers between devices with their start and end apart: 10, of which 5 were waited for; matrix products, arithmetic and copies ran while one was open for 11% of the time, Pallas kernels for 0%

commit v1 on v0

v1 whole, which is shorter than its diff:
```python
import functools

import jax
import jax.numpy as jnp
from jax import lax
from jax.experimental import pallas as pl
from jax.experimental.pallas import tpu as pltpu
from jax.sharding import PartitionSpec as P

LAT_REACH = 2
LON_REACH = 4
CELLS = 8
WINDOW = CELLS + 2 * LON_REACH
LANES = 128
BANDS = 2 * LAT_REACH + 1

ERF_SERIES = (
    1.5957685368174537,
    0.2906731929485398,
    -0.0010568544789619305,
    -0.007074993444558666,
    0.0020347241919514126,
    -0.00027398798106634774,
    1.4859691157006145e-05,
)


def shift_pair(axis, wrap):
    peers = lax.axis_size(axis)
    up = [(i, (i + 1) % peers) for i in range(peers if wrap else peers - 1)]
    return up, [(j, i) for i, j in up]


def masked_filter(filters, band_edges, basis_mask):
    rows = filters.shape[0]
    latitude = lax.axis_index("lat") * rows + jnp.arange(rows, dtype=jnp.int32)
    source = latitude[:, None] + jnp.arange(BANDS, dtype=jnp.int32)[None, :] - LAT_REACH
    inside = (source >= band_edges[:, 0:1]) & (source < band_edges[:, 1:2])
    keep = inside[:, None, :] & (basis_mask != 0)[:, :, None]
    return jnp.where(keep[..., None], filters, 0.0)


def band_rows(kernel):
    rows, bases, bands, lags = kernel.shape
    spaced = jnp.pad(kernel, ((0, 0), (0, 0), (0, 0), (0, WINDOW - lags)))
    spaced = spaced.reshape(rows, bases, bands * WINDOW)
    return jnp.pad(spaced, ((0, 0), (0, 8 - bases), (0, 2 * LANES - bands * WINDOW)))


def erf_gelu(half):
    square = half * half
    series = jnp.full_like(square, ERF_SERIES[-1])
    for term in ERF_SERIES[-2::-1]:
        series = series * square + term
    return half + half * jnp.tanh(half * series)


def block_kernel(
    block, x_ref, low_ref, high_ref, left_ref, right_ref, band_ref, one_ref, two_ref,
    out_ref, toeplitz, rim_toeplitz, extended, hidden,
):
    rows, cells = x_ref.shape[0], x_ref.shape[1]
    bases = one_ref.shape[0]
    group = bases * CELLS
    reach = 2 * LAT_REACH
    blocks = rows // block
    depth = (block + reach) * WINDOW
    rim_rows = LAT_REACH + reach

    def toeplitz_rows(row, place):
        parts = []
        for basis in range(bases):
            line = jnp.broadcast_to(band_ref[row, basis : basis + 1, :], (CELLS, 2 * LANES))
            parts.append(pltpu.roll(line, place * WINDOW, 1, stride=1, stride_axis=0))
        return parts

    @pl.when(pl.program_id(0) == 0)
    def _():
        for row in range(0, rows, 2):
            inner = row % block
            parts = toeplitz_rows(row + LAT_REACH, inner) + toeplitz_rows(row + LAT_REACH + 1, inner + 1)
            toeplitz[row * group : (row + 2) * group, :] = jnp.concatenate(parts, 0).astype(jnp.bfloat16)
        for side in range(2):
            row = side * (rows + LAT_REACH)
            place = side * rim_rows
            parts = toeplitz_rows(row, place) + toeplitz_rows(row + 1, place + 1)
            at = side * LAT_REACH * group
            rim_toeplitz[at : at + LAT_REACH * group, :] = jnp.concatenate(parts, 0).astype(jnp.bfloat16)

    f32 = jnp.float32
    extended[reach : reach + rows, CELLS : CELLS + cells, :] = x_ref[...].astype(f32)
    extended[:reach, CELLS : CELLS + cells, :] = low_ref[...].astype(f32)
    extended[reach + rows :, CELLS : CELLS + cells, :] = high_ref[...].astype(f32)
    extended[:, :CELLS, :] = left_ref[...].astype(f32)
    extended[:, CELLS + cells :, :] = right_ref[...].astype(f32)

    def pair_lanes(value):
        return jnp.concatenate([value, value], axis=-1)

    one = [pair_lanes(one_ref[k : k + 1, :]) * 0.5 for k in range(bases)]
    two = [pair_lanes(two_ref[k : k + 1, :]) for k in range(bases)]

    def window(ref, spans, at):
        tall = [ref[a:b, at : at + WINDOW, :].astype(jnp.bfloat16) for a, b in spans]
        tall = tall[0] if len(tall) == 1 else jnp.concatenate(tall, 0)
        return tall.reshape(tall.shape[0] * WINDOW, LANES)

    def product(matrix, ref, spans, at, weights):
        wide = jnp.concatenate([window(ref, spans, a) for a in at], axis=1)
        result = jnp.dot(matrix, wide, preferred_element_type=f32)
        result = result.reshape(result.shape[0] // group, bases, CELLS, wide.shape[1])
        total = result[:, 0] * weights[0][:, : wide.shape[1]]
        for k in range(1, bases):
            total = total + result[:, k] * weights[k][:, : wide.shape[1]]
        return total

    columns = cells // CELLS + 1
    for first in range(0, columns, 2):
        at = [c * CELLS for c in range(first, min(first + 2, columns))]
        for part in range(blocks + 1):
            if part < blocks:
                matrix = toeplitz[part * block * group : (part + 1) * block * group, :depth]
                start = LAT_REACH + part * block
                spans = [(start, start + block + reach)]
            else:
                matrix = rim_toeplitz[:, : 2 * rim_rows * WINDOW]
                spans = [(0, rim_rows), (rows + 2 * reach - rim_rows, rows + 2 * reach)]
            value = erf_gelu(product(matrix, extended, spans, at, one))
            for i, a in enumerate(at):
                piece = value[:, :, i * LANES : (i + 1) * LANES]
                if part < blocks:
                    hidden[start : start + block, a : a + CELLS, :] = piece
                else:
                    hidden[:LAT_REACH, a : a + CELLS, :] = piece[:LAT_REACH]
                    hidden[rows + LAT_REACH :, a : a + CELLS, :] = piece[LAT_REACH:]
    for first in range(0, cells // CELLS, 2):
        at = [first * CELLS, (first + 1) * CELLS]
        for part in range(blocks):
            matrix = toeplitz[part * block * group : (part + 1) * block * group, :depth]
            start = part * block
            value = product(matrix, hidden, [(start, start + block + reach)], at, two)
            value = jnp.concatenate([value[:, :, :LANES], value[:, :, LANES:]], axis=1)
            out_ref[start : start + block, at[0] : at[0] + 2 * CELLS, :] = value.astype(out_ref.dtype)


def per_device(state_field, filters, band_edges, basis_mask, weights_one, weights_two):
    rows, cells, channels = state_field.shape
    bases = filters.shape[1]
    reach = 2 * LAT_REACH
    group = bases * CELLS
    block = max(
        b for b in range(2, rows + 1, 2) if rows % b == 0 and (b + reach) * WINDOW <= 2 * LANES
    )

    north, south = shift_pair("lat", False)
    east, west = shift_pair("lon", True)
    low = lax.ppermute(state_field[-reach:], "lat", north)
    high = lax.ppermute(state_field[:reach], "lat", south)
    kernel = masked_filter(filters, band_edges, basis_mask).astype(jnp.bfloat16)
    kernel_low = lax.ppermute(kernel[-LAT_REACH:], "lat", north)
    kernel_high = lax.ppermute(kernel[:LAT_REACH], "lat", south)
    bands = band_rows(jnp.concatenate([kernel_low, kernel, kernel_high], 0).astype(jnp.float32))

    width = 2 * LON_REACH
    left = jnp.concatenate([low[:, -width:], state_field[:, -width:], high[:, -width:]], 0)
    right = jnp.concatenate([low[:, :width], state_field[:, :width], high[:, :width]], 0)
    left = lax.ppermute(left, "lon", east)
    right = lax.ppermute(right, "lon", west)

    def chunked(array):
        lead = array.shape[:-1]
        return pl.BlockSpec(lead + (LANES,), lambda c: (0,) * len(lead) + (c,))

    operands = (state_field, low, high, left, right)
    flops = 2 * (rows * 2 + 2 * reach) * (cells + CELLS) * bases * (block + reach) * WINDOW * channels
    return pl.pallas_call(
        functools.partial(block_kernel, block),
        grid=(channels // LANES,),
        out_shape=jax.ShapeDtypeStruct(state_field.shape, jnp.bfloat16),
        in_specs=[chunked(a) for a in operands]
        + [pl.BlockSpec(bands.shape, lambda c: (0, 0, 0)), chunked(weights_one), chunked(weights_two)],
        out_specs=chunked(state_field),
        scratch_shapes=[
            pltpu.VMEM((rows * group, 2 * LANES), jnp.bfloat16),
            pltpu.VMEM((2 * LAT_REACH * group, 2 * LANES), jnp.bfloat16),
            pltpu.VMEM((rows + 2 * reach, cells + 2 * CELLS, LANES), jnp.float32),
            pltpu.VMEM((rows + reach, cells + CELLS, LANES), jnp.float32),
        ],
        compiler_params=pltpu.CompilerParams(vmem_limit_bytes=48 * 1024 * 1024),
        cost_estimate=pl.CostEstimate(flops=flops, bytes_accessed=4 * state_field.size, transcendentals=0),
    )(*operands, bands, weights_one, weights_two)


def solution(mesh):
    placed = (
        P("lat", "lon", None),
        P("lat", None, None, None),
        P("lat", None),
        P("lat", None),
        P(),
        P(),
    )
    return jax.shard_map(
        per_device, mesh=mesh, in_specs=placed, out_specs=P("lat", "lon", None), check_vma=False
    )
```

time: 192 us -> 41.9 us (0.22)
  other arithmetic: 128 us -> 1.74 us
  local copies, waits for them, and re-layouts: 14.5 us -> 3.45 us
  Pallas kernels: 0 us -> 10.1 us
  matrix products: 9.82 us -> 0 us
  waiting for transfers between devices: 18.1 us -> 11.1 us
  starting transfers between devices: 21.3 us -> 15.1 us
    add x3 -> x1, other arithmetic: 107 us -> 0.01 us  [masked_filter(): latitude = lax.axis_index('lat') * rows + jnp.arange(rows, dtype=jnp.int32)]
    convert_element_type x4 -> x1, other arithmetic: 13.4 us -> 0.02 us  [per_device(): kernel = masked_filter(filters, band_edges, basis_mask).astype(jnp.bfloat16)]
    pallas_call x0 -> x1, Pallas kernels: none -> 10.1 us  [per_device(): pl.pallas_call(functools.partial(block_kernel, block), grid=(channels //...]
    mul x6 -> x0, local copies, waits for them, and re-layouts: 9.94 us -> none  [accumulate(): product = factor * window]
    dot_general x2 -> x0, matrix products: 9.82 us -> none  [convolve(): jnp.einsum('ykdm,kc->ydmc', kernel, weights, precision=lax.Precision.HIGH...]
    ppermute x10 -> x6, waiting for transfers between devices: 18.1 us -> 11.1 us  [the longest x1 4.68 us: per_device(): high = lax.ppermute(state_field[:reach], 'lat', south)]
    ppermute x10 -> x6, starting transfers between devices: 21.3 us -> 15.1 us  [the longest x1 5.58 us: per_device(): low = lax.ppermute(state_field[-reach:], 'lat', north)]
    concatenate x2 -> x3, other arithmetic: 6.57 us -> 1.68 us  [the longest x1 0.77 us: per_device(): jnp.concatenate([low[:, -width:], state_field[:, -width:], high[:, -width...]
  transfers between devices with their start and end apart: 10 -> 6, of which waited for: 5 -> 4; matrix products, arithmetic and copies ran while one was open for 11% -> 6% of each run, Pallas kernels for 0% -> 0%
where the time goes in v1:
time: 41.9 us; the launch traced here: 41.7 us
  starting transfers between devices  15.1 us (36%)
  waiting for transfers between devices  11.1 us (26%)
  Pallas kernels  10.1 us (24%)
  local copies, waits for them, and re-layouts  3.45 us (8%)
  other arithmetic  1.74 us (4%)
    pallas_call x1, Pallas kernels, per_device(): pl.pallas_call(functools.partial(block_kernel, block), grid=(channels //...  10.1 us
    ppermute x1, starting transfers between devices, per_device(): low = lax.ppermute(state_field[-reach:], 'lat', north)  5.58 us
    ppermute x1, waiting for transfers between devices, per_device(): high = lax.ppermute(state_field[:reach], 'lat', south)  4.68 us
    ppermute x1, waiting for transfers between devices, per_device(): kernel_high = lax.ppermute(kernel[:LAT_REACH], 'lat', south)  4.31 us
    ppermute x1, starting transfers between devices, per_device(): kernel_low = lax.ppermute(kernel[-LAT_REACH:], 'lat', north)  4.29 us
    ppermute x1, starting transfers between devices, per_device(): right = lax.ppermute(right, 'lon', west)  2.64 us
    slice x1, local copies, waits for them, and re-layouts, per_device(): high = lax.ppermute(state_field[:reach], 'lat', south)  2 us
    ppermute x1, starting transfers between devices, per_device(): kernel_high = lax.ppermute(kernel[:LAT_REACH], 'lat', south)  1.29 us
  transfers between devices with their start and end apart: 6, of which 4 were waited for; matrix products, arithmetic and copies ran while one was open for 6% of the time, Pallas kernels for 0%

profile of v1, /device:TPU:0, one launch (start us, length us, event | category | flops | bytes accessed | tf_op | source)
XLA Modules:
  0.0 41.7 jit_solution(17159493153956414304)
XLA Ops:
  0.0 0.0 copy-start.5
  0.0 0.0 copy-start.4
  0.0 0.0 copy-start.3
  0.0 2.0 %fusion.4 = (bf16[4,64,640]{2,1,0:T(8,128)(2,1)}, bf16[4,64,640]{2,1,0:T(8,128)(2,1)}) fusion(bf16[24,64,640]{2,1,0:T(8,128)(2,1)} %x_ref.1), kind=kLoop, calls=%fused_computation.15 | loop fusion | bytes 1310720 | tf_op jit(solution)/shard_map/slice | solution.py:158
  2.0 1.3 %collective-permute-start.1 = (bf16[4,64,640]{2,1,0:T(8,128)(2,1)}, bf16[4,64,640]{2,1,0:T(8,128)(2,1)S(1)}, u32[]{:S(2)}, u32[]{:S(2)}) collective-permute-start(bf16[4,64,640]{2,1,0:T(8,128)(2,1)} %get-tuple-element.7), channel_id=1, source_target_pairs={{8,0},{16,8},{24,16},{9,1},{17,9},{25,17},{10,2},{18,10},{26,18},{... | collective-permute-start | bytes 983048 | tf_op jit(solution)/shard_map/ppermute | solution.py:158
  3.3 5.6 %collective-permute-start = (bf16[4,64,640]{2,1,0:T(8,128)(2,1)}, bf16[4,64,640]{2,1,0:T(8,128)(2,1)S(1)}, u32[]{:S(2)}, u32[]{:S(2)}) collective-permute-start(bf16[4,64,640]{2,1,0:T(8,128)(2,1)} %get-tuple-element.8), channel_id=1, source_target_pairs={{0,8},{8,16},{16,24},{1,9},{9,17},{17,25},{2,10},{10,18},{18,26},{... | collective-permute-start | bytes 983048 | tf_op jit(solution)/shard_map/ppermute | solution.py:157
  8.9 1.1 %fusion.3 = (bf16[24,8,640]{2,1,0:T(8,128)(2,1)S(1)}, bf16[24,8,640]{2,1,0:T(8,128)(2,1)S(1)}) fusion(bf16[24,64,640]{2,1,0:T(8,128)(2,1)} %x_ref.1), kind=kLoop, calls=%fused_computation.14 | loop fusion | bytes 983040 | tf_op jit(solution)/shard_map/slice | solution.py:166
  10.0 0.0 copy-start
  10.0 0.0 copy-start.1
  10.0 0.0 copy-start.2
  10.1 0.0 copy-done.5
  10.1 0.0 copy-done.4
  10.1 0.0 copy-done.3
  10.2 4.7 %collective-permute-done.1.high_ref = bf16[4,64,640]{2,1,0:T(8,128)(2,1)S(1)} collective-permute-done((bf16[4,64,640]{2,1,0:T(8,128)(2,1)}, bf16[4,64,640]{2,1,0:T(8,128)(2,1)S(1)}, u32[]{:S(2)}, u32[]{:S(2)}) %collective-permute-start.1) | collective-permute-done | bytes 327712 | tf_op jit(solution)/shard_map/ppermute | solution.py:158
  14.9 1.3 %collective-permute-done.low_ref = bf16[4,64,640]{2,1,0:T(8,128)(2,1)S(1)} collective-permute-done((bf16[4,64,640]{2,1,0:T(8,128)(2,1)}, bf16[4,64,640]{2,1,0:T(8,128)(2,1)S(1)}, u32[]{:S(2)}, u32[]{:S(2)}) %collective-permute-start) | collective-permute-done | bytes 327712 | tf_op jit(solution)/shard_map/ppermute | solution.py:157
  16.1 0.8 %pad_maximum_fusion = bf16[32,8,640]{2,1,0:T(8,128)(2,1)} fusion(bf16[4,8,640]{2,1,0:T(8,128)(2,1)S(1)} %get-tuple-element.12, bf16[24,8,640]{2,1,0:T(8,128)(2,1)S(1)} %get-tuple-element.6, bf16[4,8,640]{2,1,0:T(8,128)(2,1)S(1)} %get-tuple-element.10), kind=kLoop, calls=%fused_computation | loop fusion | flops 327680 | bytes 655360 | tf_op jit(solution)/shard_map/concatenate | solution.py:165
  16.9 0.0 collective-permute-start.2
  16.9 0.8 %pad_maximum_fusion.1 = bf16[32,8,640]{2,1,0:T(8,128)(2,1)} fusion(bf16[4,8,640]{2,1,0:T(8,128)(2,1)S(1)} %get-tuple-element.11, bf16[24,8,640]{2,1,0:T(8,128)(2,1)S(1)} %get-tuple-element.5, bf16[4,8,640]{2,1,0:T(8,128)(2,1)S(1)} %get-tuple-element.9), kind=kLoop, calls=%fused_computation.1 | loop fusion | flops 327680 | bytes 655360 | tf_op jit(solution)/shard_map/concatenate | solution.py:166
  17.7 2.6 %collective-permute-start.3 = (bf16[32,8,640]{2,1,0:T(8,128)(2,1)}, bf16[32,8,640]{2,1,0:T(8,128)(2,1)S(1)}, u32[]{:S(2)}, u32[]{:S(2)}) collective-permute-start(bf16[32,8,640]{2,1,0:T(8,128)(2,1)} %pad_maximum_fusion.1), channel_id=1, source_target_pairs={{1,0},{2,1},{3,2},{4,3},{5,4},{6,5},{7,6},{0,7},{9,8},{10,9},{11,1... | collective-permute-start | bytes 983048 | tf_op jit(solution)/shard_map/ppermute | solution.py:168
  20.3 0.1 fusion.7
  20.4 4.3 %collective-permute-start.4 = (bf16[2,5,5,9]{0,2,3,1:T(8,128)(2,1)S(1)}, bf16[2,5,5,9]{0,2,3,1:T(8,128)(2,1)S(1)}, u32[]{:S(2)}, u32[]{:S(2)}) collective-permute-start(bf16[2,5,5,9]{0,2,3,1:T(8,128)(2,1)S(1)} %get-tuple-element.13), channel_id=1, source_target_pairs={{0,8},{8,16},{16,24},{1,9},{9,17},{17,25},{2,10},{10,18},{18,26},{... | collective-permute-start | bytes 2708 | tf_op jit(solution)/shard_map/ppermute | solution.py:160
  24.7 1.3 %collective-permute-start.5 = (bf16[2,5,5,9]{0,2,3,1:T(8,128)(2,1)S(1)}, bf16[2,5,5,9]{0,2,3,1:T(8,128)(2,1)S(1)}, u32[]{:S(2)}, u32[]{:S(2)}) collective-permute-start(bf16[2,5,5,9]{0,2,3,1:T(8,128)(2,1)S(1)} %get-tuple-element.14), channel_id=1, source_target_pairs={{8,0},{16,8},{24,16},{9,1},{17,9},{25,17},{10,2},{18,10},{26,18},{... | collective-permute-start | bytes 2708 | tf_op jit(solution)/shard_map/ppermute | solution.py:161
  26.0 0.8 %collective-permute-done.4 = bf16[2,5,5,9]{0,2,3,1:T(8,128)(2,1)S(1)} collective-permute-done((bf16[2,5,5,9]{0,2,3,1:T(8,128)(2,1)S(1)}, bf16[2,5,5,9]{0,2,3,1:T(8,128)(2,1)S(1)}, u32[]{:S(2)}, u32[]{:S(2)}) %collective-permute-start.4) | collective-permute-done | bytes 932 | tf_op jit(solution)/shard_map/ppermute | solution.py:160
  26.9 4.3 %collective-permute-done.5 = bf16[2,5,5,9]{0,2,3,1:T(8,128)(2,1)S(1)} collective-permute-done((bf16[2,5,5,9]{0,2,3,1:T(8,128)(2,1)S(1)}, bf16[2,5,5,9]{0,2,3,1:T(8,128)(2,1)S(1)}, u32[]{:S(2)}, u32[]{:S(2)}) %collective-permute-start.5) | collective-permute-done | bytes 932 | tf_op jit(solution)/shard_map/ppermute | solution.py:161
  31.2 0.1 pad_maximum_fusion.2
  31.4 0.1 copy.9
  31.5 0.0 collective-permute-done.2.left_ref
  31.6 0.0 collective-permute-done.3.right_ref
  31.6 0.0 copy-done
  31.6 0.0 copy-done.1
  31.6 0.0 copy-done.2
  31.6 10.1 %shard_map.64 = bf16[24,64,640]{2,1,0:T(8,128)(2,1)} custom-call(bf16[24,64,640]{2,1,0:T(8,128)(2,1)S(1)} %copy-done, bf16[4,64,640]{2,1,0:T(8,128)(2,1)S(1)} %collective-permute-done.low_ref, bf16[4,64,640]{2,1,0:T(8,128)(2,1)S(1)} %collective-permute-done.1.high_ref, bf16[32,8,640]{2,1,0:T(8,128)(2,1)S(1)} %collective-permute-done.2.left_ref, ...), custom_call_target="tpu_custom_call" | custom-call | flops 6606028800 | bytes 3932160 | tf_op jit(solution)/shard_map/pallas_call | solution.py:176
  (10 shorter events, 0.1 us)
Async XLA Ops:
  0.0 10.1 %copy-start.5 = (s32[24,2]{0,1:T(2,128)S(1)}, s32[24,2]{0,1:T(2,128)}, u32[]{:S(2)}) copy-start(s32[24,2]{0,1:T(2,128)} %param.8) | copy-start | bytes 580
  0.0 10.1 %copy-start.4 = (s32[24,5]{0,1:T(8,128)S(1)}, s32[24,5]{0,1:T(8,128)}, u32[]{:S(2)}) copy-start(s32[24,5]{0,1:T(8,128)} %param.9) | copy-start | bytes 1444
  0.0 10.1 %copy-start.3 = (f32[24,5,5,9]{0,2,3,1:T(8,128)S(1)}, f32[24,5,5,9]{0,2,3,1:T(8,128)}, u32[]{:S(2)}) copy-start(f32[24,5,5,9]{0,2,3,1:T(8,128)} %param.7) | copy-start | bytes 64804
  2.0 12.8 %collective-permute-start.1 = (bf16[4,64,640]{2,1,0:T(8,128)(2,1)}, bf16[4,64,640]{2,1,0:T(8,128)(2,1)S(1)}, u32[]{:S(2)}, u32[]{:S(2)}) collective-permute-start(bf16[4,64,640]{2,1,0:T(8,128)(2,1)} %get-tuple-element.7), channel_id=1, source_target_pairs={{8,0},{16,8},{24,16},{9,1},{17,9},{25,17},{10,2},{18,10},{26,18},{... | collective-permute-start | bytes 983048 | tf_op jit(solution)/shard_map/ppermute | solution.py:158
  3.3 12.8 %collective-permute-start = (bf16[4,64,640]{2,1,0:T(8,128)(2,1)}, bf16[4,64,640]{2,1,0:T(8,128)(2,1)S(1)}, u32[]{:S(2)}, u32[]{:S(2)}) collective-permute-start(bf16[4,64,640]{2,1,0:T(8,128)(2,1)} %get-tuple-element.8), channel_id=1, source_target_pairs={{0,8},{8,16},{16,24},{1,9},{9,17},{17,25},{2,10},{10,18},{18,26},{... | collective-permute-start | bytes 983048 | tf_op jit(solution)/shard_map/ppermute | solution.py:157
  10.0 21.6 %copy-start = (bf16[24,64,640]{2,1,0:T(8,128)(2,1)S(1)}, bf16[24,64,640]{2,1,0:T(8,128)(2,1)}, u32[]{:S(2)}) copy-start(bf16[24,64,640]{2,1,0:T(8,128)(2,1)} %x_ref.1) | copy-start | bytes 5898244
  10.0 21.6 %copy-start.1 = (f32[5,640]{1,0:T(8,128)S(1)}, f32[5,640]{1,0:T(8,128)}, u32[]{:S(2)}) copy-start(f32[5,640]{1,0:T(8,128)} %one_ref.1) | copy-start | bytes 38404
  10.0 21.6 %copy-start.2 = (f32[5,640]{1,0:T(8,128)S(1)}, f32[5,640]{1,0:T(8,128)}, u32[]{:S(2)}) copy-start(f32[5,640]{1,0:T(8,128)} %two_ref.1) | copy-start | bytes 38404
  16.9 14.6 %collective-permute-start.2 = (bf16[32,8,640]{2,1,0:T(8,128)(2,1)}, bf16[32,8,640]{2,1,0:T(8,128)(2,1)S(1)}, u32[]{:S(2)}, u32[]{:S(2)}) collective-permute-start(bf16[32,8,640]{2,1,0:T(8,128)(2,1)} %pad_maximum_fusion), channel_id=1, source_target_pairs={{0,1},{1,2},{2,3},{3,4},{4,5},{5,6},{6,7},{7,0},{8,9},{9,10},{10,1... | collective-permute-start | bytes 983048 | tf_op jit(solution)/shard_map/ppermute | solution.py:167
  17.7 13.9 %collective-permute-start.3 = (bf16[32,8,640]{2,1,0:T(8,128)(2,1)}, bf16[32,8,640]{2,1,0:T(8,128)(2,1)S(1)}, u32[]{:S(2)}, u32[]{:S(2)}) collective-permute-start(bf16[32,8,640]{2,1,0:T(8,128)(2,1)} %pad_maximum_fusion.1), channel_id=1, source_target_pairs={{1,0},{2,1},{3,2},{4,3},{5,4},{6,5},{7,6},{0,7},{9,8},{10,9},{11,1... | collective-permute-start | bytes 983048 | tf_op jit(solution)/shard_map/ppermute | solution.py:168
  20.4 6.4 %collective-permute-start.4 = (bf16[2,5,5,9]{0,2,3,1:T(8,128)(2,1)S(1)}, bf16[2,5,5,9]{0,2,3,1:T(8,128)(2,1)S(1)}, u32[]{:S(2)}, u32[]{:S(2)}) collective-permute-start(bf16[2,5,5,9]{0,2,3,1:T(8,128)(2,1)S(1)} %get-tuple-element.13), channel_id=1, source_target_pairs={{0,8},{8,16},{16,24},{1,9},{9,17},{17,25},{2,10},{10,18},{18,26},{... | collective-permute-start | bytes 2708 | tf_op jit(solution)/shard_map/ppermute | solution.py:160
  24.7 6.4 %collective-permute-start.5 = (bf16[2,5,5,9]{0,2,3,1:T(8,128)(2,1)S(1)}, bf16[2,5,5,9]{0,2,3,1:T(8,128)(2,1)S(1)}, u32[]{:S(2)}, u32[]{:S(2)}) collective-permute-start(bf16[2,5,5,9]{0,2,3,1:T(8,128)(2,1)S(1)} %get-tuple-element.14), channel_id=1, source_target_pairs={{8,0},{16,8},{24,16},{9,1},{17,9},{25,17},{10,2},{18,10},{26,18},{... | collective-permute-start | bytes 2708 | tf_op jit(solution)/shard_map/ppermute | solution.py:161

commit v2 on v0

v2 whole, which is shorter than its diff:
```python
import functools

import jax
import jax.numpy as jnp
from jax import lax
from jax.experimental import pallas as pl
from jax.experimental.pallas import tpu as pltpu
from jax.sharding import PartitionSpec as P

LAT_REACH = 2
LON_REACH = 4
REACH = 2 * LAT_REACH
CELLS = 8
WINDOW = CELLS + 2 * LON_REACH
LANES = 128
DEPTH = 2 * LANES
BANDS = 2 * LAT_REACH + 1
VMEM_BYTES = 56 * 1024 * 1024

ERF_SERIES = (
    1.5956562720156744,
    0.2917503271976864,
    -0.003995570947534282,
    -0.003914369984884403,
    0.0005729703632347449,
)


def erf_gelu(half):
    square = half * half
    series = ERF_SERIES[-1] * square + ERF_SERIES[-2]
    for term in ERF_SERIES[-3::-1]:
        series = series * square + term
    return half + half * jnp.tanh(half * series)


def swaps(peers, second, wrap):
    pairs = [(i, i + 1) for i in range(1 if second else 0, peers - 1, 2)]
    if second and wrap:
        pairs.append((peers - 1, 0))
    return pairs + [(j, i) for i, j in pairs]


def masked_filter(filters, band_edges, basis_mask):
    rows = filters.shape[0]
    latitude = lax.axis_index("lat") * rows + jnp.arange(rows, dtype=jnp.int32)
    source = latitude[:, None] + jnp.arange(BANDS, dtype=jnp.int32)[None, :] - LAT_REACH
    inside = (source >= band_edges[:, 0:1]) & (source < band_edges[:, 1:2])
    keep = inside[:, None, :] & (basis_mask != 0)[:, :, None]
    return jnp.where(keep[..., None], filters, 0.0).astype(jnp.bfloat16)


def band_rows(kernel):
    rows, bases, bands, lags = kernel.shape
    spaced = jnp.pad(kernel.astype(jnp.float32), ((0, 0), (0, 0), (0, 0), (0, WINDOW - lags)))
    spaced = spaced.reshape(rows, bases, bands * WINDOW)
    return jnp.pad(spaced, ((0, 0), (0, 8 - bases), (0, DEPTH - bands * WINDOW)))


def fill_toeplitz(toeplitz, band_ref, bases, places):
    group = bases * CELLS
    for row in range(0, len(places), 2):
        parts = []
        for r in (row, row + 1):
            for basis in range(bases):
                line = jnp.broadcast_to(band_ref[r, basis : basis + 1, :], (CELLS, DEPTH))
                parts.append(pltpu.roll(line, places[r] * WINDOW, 1, stride=1, stride_axis=0))
        toeplitz[row * group : (row + 2) * group, :] = jnp.concatenate(parts, 0).astype(jnp.bfloat16)


def pairs_of(items):
    return [items[i : i + 2] for i in range(0, len(items), 2)]


def lane_weights(ref, scale=1.0):
    bases, channels = ref.shape
    return [
        [ref[k : k + 1, c * LANES : (c + 1) * LANES] * scale for k in range(bases)]
        for c in range(channels // LANES)
    ]


def product(matrix, windows, weights):
    wide = [w.astype(jnp.bfloat16).reshape(DEPTH, LANES) for w in windows]
    result = jnp.dot(matrix, jnp.concatenate(wide, 1), preferred_element_type=jnp.float32)
    bases = len(weights[0])
    result = result.reshape(-1, bases, CELLS, len(windows) * LANES)
    total = None
    for k in range(bases):
        term = result[:, k] * jnp.concatenate([w[k] for w in weights], 1)
        total = term if total is None else total + term
    return [total[:, :, i * LANES : (i + 1) * LANES] for i in range(len(windows))]


def inner_kernel(
    block, x_ref, band_ref, one_ref, two_ref, toeplitz, edge_rows, edge_cells, out_ref, field, hidden
):
    rows, cells, channels = x_ref.shape
    bases = one_ref.shape[0]
    group = bases * CELLS
    chunks = channels // LANES
    fill_toeplitz(toeplitz, band_ref, bases, [r % block for r in range(rows)])
    one, two = lane_weights(one_ref, 0.5), lane_weights(two_ref)

    for c in range(chunks):
        lanes = slice(c * LANES, (c + 1) * LANES)
        field[c, LAT_REACH : LAT_REACH + rows] = x_ref[:, :, lanes].astype(jnp.float32)
        field[c, :LAT_REACH] = jnp.zeros((LAT_REACH, cells, LANES), jnp.float32)
        field[c, LAT_REACH + rows :] = jnp.zeros((LAT_REACH, cells, LANES), jnp.float32)

    windows = (cells - WINDOW) // CELLS + 1
    for start in range(0, rows, block):
        low = max(start, LAT_REACH)
        high = min(start + block, rows - LAT_REACH)
        for items in pairs_of([(c, w) for c in range(chunks) for w in range(windows)]):
            values = product(
                toeplitz[low * group : high * group, :],
                [field[c, start : start + block + REACH, w * CELLS : w * CELLS + WINDOW] for c, w in items],
                [one[c] for c, w in items],
            )
            for (c, w), value in zip(items, values):
                hidden[c, low : high, w * CELLS : (w + 1) * CELLS] = erf_gelu(value)
    for c in range(chunks):
        lanes = slice(c * LANES, (c + 1) * LANES)
        hidden[c, :LAT_REACH] = jnp.zeros((LAT_REACH,) + hidden.shape[2:], jnp.float32)
        hidden[c, rows - LAT_REACH :] = jnp.zeros((LAT_REACH,) + hidden.shape[2:], jnp.float32)
        span = windows * CELLS
        for i in range(2):
            at = LAT_REACH if i == 0 else rows - REACH - LAT_REACH
            edge_rows[i * REACH : (i + 1) * REACH, :span, lanes] = hidden[c, at : at + REACH].astype(jnp.bfloat16)
            edge_rows[i * REACH : (i + 1) * REACH, span:, lanes] = jnp.zeros((REACH, CELLS, LANES), jnp.bfloat16)
        edge = jnp.concatenate([hidden[c, :, :CELLS], hidden[c, :, span - CELLS :]], axis=1)
        edge_cells[:, :, lanes] = edge.astype(jnp.bfloat16)

    for start in range(0, rows, block):
        low = max(start, REACH)
        high = min(start + block, rows - REACH)
        first = min(max(start - LAT_REACH, 0), rows - block - REACH)
        shift = start - LAT_REACH - first
        for c in range(chunks):
            lanes = slice(c * LANES, (c + 1) * LANES)
            for pair in pairs_of(list(range(windows - 1))):
                tall = []
                for w in pair:
                    at = slice(w * CELLS, w * CELLS + WINDOW)
                    if shift < 0:
                        zero = jnp.zeros((-shift, WINDOW, LANES), jnp.float32)
                        tall.append(jnp.concatenate([zero, hidden[c, : block + REACH + shift, at]], 0))
                    elif shift > 0:
                        zero = jnp.zeros((shift, WINDOW, LANES), jnp.float32)
                        tall.append(jnp.concatenate([hidden[c, rows - block - REACH + shift :, at], zero], 0))
                    else:
                        tall.append(hidden[c, first : first + block + REACH, at])
                values = product(toeplitz[low * group : high * group, :], tall, [two[c]] * 2)
                value = jnp.concatenate(values, 1).astype(out_ref.dtype)
                out_ref[low - REACH : high - REACH, pair[0] * CELLS : (pair[0] + 2) * CELLS, lanes] = value


def rim_kernel(
    block, place_ref, x_ref, lat_a, lat_b, lon_a, lon_b, corner_a, corner_b, edge_rows, edge_cells, inner_ref,
    toeplitz, rim_band, wide_band, one_ref, two_ref, out_ref, rim_toeplitz, wide_toeplitz, field, hidden,
):
    rows, cells, channels = x_ref.shape
    bases = one_ref.shape[0]
    group = bases * CELLS
    chunks = channels // LANES
    f32, bf16 = jnp.float32, jnp.bfloat16
    tall = rows + 2 * REACH
    places = list(range(REACH)) + [2 * REACH + r for r in range(REACH)]
    fill_toeplitz(rim_toeplitz, rim_band, bases, places)
    fill_toeplitz(wide_toeplitz, wide_band, bases, places)
    one, two = lane_weights(one_ref, 0.5), lane_weights(two_ref)
    lat_odd, lon_odd = place_ref[0] == 1, place_ref[1] == 1

    def fill_lat(low, high):
        for c in range(chunks):
            lanes = slice(c * LANES, (c + 1) * LANES)
            for ref, at in ((low, 0), (high, REACH + rows)):
                part = ref[: REACH * cells, lanes].reshape(REACH, cells, LANES)
                field[c, at : at + REACH, CELLS : CELLS + cells] = part.astype(f32)

    def fill_lon(left, right, left_corner, right_corner, lat_low):
        for c in range(chunks):
            lanes = slice(c * LANES, (c + 1) * LANES)
            for ref, corner, at in ((left, left_corner, 0), (right, right_corner, CELLS + cells)):
                span = slice(at, at + CELLS)
                field[c, REACH : REACH + rows, span] = ref[:, :, lanes].astype(f32)
                field[c, :REACH, span] = corner[lat_low * REACH : (lat_low + 1) * REACH, :, lanes].astype(f32)
                other = 1 - lat_low
                field[c, REACH + rows :, span] = corner[other * REACH : (other + 1) * REACH, :, lanes].astype(f32)

    @pl.when(lat_odd)
    def _():
        fill_lat(lat_a, lat_b)

    @pl.when(jnp.logical_not(lat_odd))
    def _():
        fill_lat(lat_b, lat_a)

    for lat_low in range(2):
        for lon_is_odd in range(2):
            def fill(lat_low=lat_low, lon_is_odd=lon_is_odd):
                if lon_is_odd:
                    fill_lon(lon_a, lon_b, corner_a, corner_b, lat_low)
                else:
                    fill_lon(lon_b, lon_a, corner_b, corner_a, lat_low)

            pl.when((lat_odd if lat_low == 0 else jnp.logical_not(lat_odd))
                    & (lon_odd if lon_is_odd else jnp.logical_not(lon_odd)))(fill)

    for c in range(chunks):
        lanes = slice(c * LANES, (c + 1) * LANES)
        own = x_ref[:, :, lanes].astype(f32)
        field[c, REACH : 2 * REACH, CELLS : CELLS + cells] = own[:REACH]
        field[c, rows : rows + REACH, CELLS : CELLS + cells] = own[rows - REACH :]
        field[c, 2 * REACH : rows, CELLS : 2 * CELLS] = own[REACH : rows - REACH, :CELLS]
        field[c, 2 * REACH : rows, cells : CELLS + cells] = own[REACH : rows - REACH, cells - CELLS :]
        span = cells - CELLS
        for i, at in ((0, 2 * LAT_REACH), (1, rows - REACH)):
            part = edge_rows[i * REACH : (i + 1) * REACH, :, lanes].astype(f32)
            hidden[c, at : at + REACH, CELLS : CELLS + span] = part[:, :span]
        part = edge_cells[REACH + LAT_REACH : rows - REACH - LAT_REACH, :, lanes].astype(f32)
        at = slice(2 * REACH, rows - REACH)
        hidden[c, at, CELLS : 2 * CELLS] = part[:, :CELLS]
        hidden[c, at, cells - CELLS : cells] = part[:, CELLS:]

    def rims(ref, c, at):
        span = slice(at, at + WINDOW)
        last = ref.shape[1] - 2 * REACH
        return jnp.concatenate([ref[c, : 2 * REACH, span], ref[c, last:, span]], 0)

    columns = cells // CELLS + 1
    for items in pairs_of([(c, w) for c in range(chunks) for w in range(columns)]):
        values = product(rim_toeplitz[...], [rims(field, c, w * CELLS) for c, w in items], [one[c] for c, w in items])
        for (c, w), value in zip(items, values):
            value = erf_gelu(value)
            hidden[c, :REACH, w * CELLS : (w + 1) * CELLS] = value[:REACH]
            hidden[c, rows:, w * CELLS : (w + 1) * CELLS] = value[REACH:]
    sides = (0, cells)
    for c in range(chunks):
        for start in range(0, rows, block):
            low = max(start, LAT_REACH)
            high = min(start + block, rows - LAT_REACH)
            at = slice(start + LAT_REACH, start + LAT_REACH + block + REACH)
            values = product(
                toeplitz[low * group : high * group, :], [field[c, at, s : s + WINDOW] for s in sides], [one[c]] * 2
            )
            for s, value in zip(sides, values):
                hidden[c, low + LAT_REACH : high + LAT_REACH, s : s + CELLS] = erf_gelu(value)

    for c in range(chunks):
        lanes = slice(c * LANES, (c + 1) * LANES)
        for pair in pairs_of([w * CELLS for w in range(columns - 1)]):
            values = product(wide_toeplitz[...], [rims(hidden, c, s) for s in pair], [two[c]] * 2)
            value = jnp.concatenate(values, 1).astype(out_ref.dtype)
            out_ref[:REACH, pair[0] : pair[0] + 2 * CELLS, lanes] = value[:REACH]
            out_ref[rows - REACH :, pair[0] : pair[0] + 2 * CELLS, lanes] = value[REACH:]
        for start in range(0, rows, block):
            low = max(start, REACH)
            high = min(start + block, rows - REACH)
            at = slice(start, start + block + REACH)
            sides = (0, cells - CELLS)
            values = product(
                toeplitz[low * group : high * group, :], [hidden[c, at, s : s + WINDOW] for s in sides], [two[c]] * 2
            )
            inner = inner_ref[low - REACH : high - REACH, :, lanes].astype(f32)
            whole = jnp.concatenate([values[0], inner, values[1]], 1)
            out_ref[low:high, :, lanes] = whole.astype(out_ref.dtype)


def per_device(state_field, filters, band_edges, basis_mask, weights_one, weights_two):
    rows, cells, channels = state_field.shape
    bases = filters.shape[1]
    group = bases * CELLS
    chunks = channels // LANES
    width = 2 * LON_REACH
    block = max(b for b in range(2, rows + 1, 2) if rows % b == 0 and (b + REACH) * WINDOW <= DEPTH)
    bf16 = jnp.bfloat16
    lat_peers, lon_peers = lax.axis_size("lat"), lax.axis_size("lon")
    lat_odd, lon_odd = lax.axis_index("lat") % 2, lax.axis_index("lon") % 2

    kernel = masked_filter(filters, band_edges, basis_mask)
    tags = bases * BANDS * filters.shape[3] * LAT_REACH

    def lat_send(leading, second):
        start = jnp.where(leading, 0, rows - REACH)
        edge = lax.dynamic_slice_in_dim(state_field, start, REACH, 0).reshape(REACH * cells, channels)
        tag = jnp.where(leading, kernel[:LAT_REACH], kernel[rows - LAT_REACH :]).reshape(1, tags)
        tag = jnp.pad(tag, ((0, 15), (0, channels - tags)))
        return lax.ppermute(jnp.concatenate([edge, tag], 0), "lat", swaps(lat_peers, second, False))

    def lon_send(values, leading, second):
        start = jnp.where(leading, 0, cells - width)
        edge = lax.dynamic_slice_in_dim(values, start, width, 1)
        return lax.ppermute(edge, "lon", swaps(lon_peers, second, True))

    lat_a = lat_send(lat_odd == 1, False)
    lat_b = lat_send(lat_odd == 0, True)
    lon_b = lon_send(state_field, lon_odd == 0, True)
    lon_a = lon_send(state_field, lon_odd == 1, False)

    own_band = band_rows(kernel)
    vmem = pl.BlockSpec(memory_space=pltpu.VMEM)
    spread = cells - 2 * CELLS
    flops = 2 * (2 * rows - 3 * REACH) * (cells - 2 * CELLS) * bases * DEPTH * channels
    toeplitz, edge_rows, edge_cells, inner = pl.pallas_call(
        functools.partial(inner_kernel, block),
        out_shape=(
            jax.ShapeDtypeStruct((rows * group, DEPTH), bf16),
            jax.ShapeDtypeStruct((2 * REACH, cells, channels), bf16),
            jax.ShapeDtypeStruct((rows, 2 * CELLS, channels), bf16),
            jax.ShapeDtypeStruct((rows - 2 * REACH, spread, channels), bf16),
        ),
        in_specs=[vmem] * 4,
        out_specs=(vmem,) * 4,
        scratch_shapes=[
            pltpu.VMEM((chunks, rows + REACH, cells, LANES), jnp.float32),
            pltpu.VMEM((chunks, rows, cells - CELLS, LANES), jnp.float32),
        ],
        compiler_params=pltpu.CompilerParams(vmem_limit_bytes=VMEM_BYTES),
        cost_estimate=pl.CostEstimate(flops=flops, bytes_accessed=4 * state_field.size, transcendentals=0),
        name="inner",
    )(state_field, own_band, weights_one, weights_two)

    def rows_of(received):
        return received[: REACH * cells].reshape(REACH, cells, channels)

    def tag_of(received):
        tag = received[REACH * cells, :tags]
        return tag.reshape(LAT_REACH, bases, BANDS, filters.shape[3])

    joined = jnp.concatenate([rows_of(lat_a), rows_of(lat_b)], 0)
    corner_b = lon_send(joined, lon_odd == 0, True)
    corner_a = lon_send(joined, lon_odd == 1, False)
    tag_a, tag_b = tag_of(lat_a), tag_of(lat_b)
    tag_low = jnp.where(lat_odd == 1, tag_a, tag_b)
    tag_high = jnp.where(lat_odd == 1, tag_b, tag_a)
    edge = REACH - LAT_REACH
    rim_band = band_rows(jnp.concatenate([tag_low, kernel[:edge], kernel[rows - edge :], tag_high], 0))
    wide_band = jnp.concatenate([own_band[:REACH], own_band[rows - REACH :]], 0)
    place = jnp.stack([lat_odd, lon_odd]).astype(jnp.int32)
    return pl.pallas_call(
        functools.partial(rim_kernel, block),
        out_shape=jax.ShapeDtypeStruct(state_field.shape, bf16),
        in_specs=[pl.BlockSpec(memory_space=pltpu.SMEM)] + [vmem] * 15,
        out_specs=vmem,
        scratch_shapes=[
            pltpu.VMEM((2 * REACH * group, DEPTH), bf16),
            pltpu.VMEM((2 * REACH * group, DEPTH), bf16),
            pltpu.VMEM((chunks, rows + 2 * REACH, cells + 2 * CELLS, LANES), jnp.float32),
            pltpu.VMEM((chunks, rows + REACH, cells + CELLS, LANES), jnp.float32),
        ],
        compiler_params=pltpu.CompilerParams(vmem_limit_bytes=VMEM_BYTES),
        cost_estimate=pl.CostEstimate(flops=flops, bytes_accessed=4 * state_field.size, transcendentals=0),
        name="rim",
    )(
        place, state_field, lat_a, lat_b, lon_a, lon_b, corner_a, corner_b, edge_rows, edge_cells, inner,
        toeplitz, rim_band, wide_band, weights_one, weights_two,
    )


def solution(mesh):
    placed = (
        P("lat", "lon", None),
        P("lat", None, None, None),
        P("lat", None),
        P("lat", None),
        P(),
        P(),
    )
    return jax.shard_map(
        per_device, mesh=mesh, in_specs=placed, out_specs=P("lat", "lon", None), check_vma=False
    )
```

time: 192 us -> 37.1 us (0.19)
  other arithmetic: 128 us -> 3.05 us
  waiting for transfers between devices: 18.1 us -> 3.37 us
  Pallas kernels: 0 us -> 14.3 us
  starting transfers between devices: 21.3 us -> 9.64 us
  matrix products: 9.82 us -> 0 us
  local copies, waits for them, and re-layouts: 14.5 us -> 6.23 us
    add x3 -> x1, other arithmetic: 107 us -> 0.01 us  [masked_filter(): latitude = lax.axis_index('lat') * rows + jnp.arange(rows, dtype=jnp.int32)]
    ppermute x10 -> x6, waiting for transfers between devices: 18.1 us -> 3.37 us  [the longest x4 3.08 us: lon_send(): return lax.ppermute(edge, 'lon', swaps(lon_peers, second, True))]
    pallas_call x0 -> x2, Pallas kernels: none -> 14.3 us  [the longest x1 7.8 us: per_device(): pl.pallas_call(functools.partial(rim_kernel, block), out_shape=jax.ShapeD...]
    convert_element_type x4 -> x1, other arithmetic: 13.4 us -> 0.19 us  [masked_filter(): return jnp.where(keep[..., None], filters, 0.0).astype(jnp.bfloat16)]
    ppermute x10 -> x6, starting transfers between devices: 21.3 us -> 9.64 us  [the longest x2 5.13 us: lat_send(): lax.ppermute(jnp.concatenate([edge, tag], 0), 'lat', swaps(lat_peers, sec...]
    mul x6 -> x0, local copies, waits for them, and re-layouts: 9.94 us -> none  [accumulate(): product = factor * window]
    dot_general x2 -> x0, matrix products: 9.82 us -> none  [convolve(): jnp.einsum('ykdm,kc->ydmc', kernel, weights, precision=lax.Precision.HIGH...]
    concatenate x2 -> x5, other arithmetic: 6.57 us -> 0.79 us  [the longest x1 0.65 us: per_device(): wide_band = jnp.concatenate([own_band[:REACH], own_band[rows - REACH:]], 0)]
  transfers between devices with their start and end apart: 10 -> 6, of which waited for: 5 -> 2; matrix products, arithmetic and copies ran while one was open for 11% -> 20% of each run, Pallas kernels for 0% -> 18%
where the time goes in v2:
time: 37.1 us; the launch traced here: 36.8 us
  Pallas kernels  14.3 us (39%)
  starting transfers between devices  9.64 us (26%)
  local copies, waits for them, and re-layouts  6.23 us (17%)
  waiting for transfers between devices  3.37 us (9%)
  other arithmetic  3.05 us (8%)
    pallas_call x1, Pallas kernels, per_device(): pl.pallas_call(functools.partial(rim_kernel, block), out_shape=jax.ShapeD...  7.8 us
    pallas_call x1, Pallas kernels, per_device(): pl.pallas_call(functools.partial(inner_kernel, block), out_shape=(jax.Sha...  6.52 us
    ppermute x2, starting transfers between devices, lat_send(): lax.ppermute(jnp.concatenate([edge, tag], 0), 'lat', swaps(lat_peers, sec...  5.13 us
    ppermute x4, starting transfers between devices, lon_send(): return lax.ppermute(edge, 'lon', swaps(lon_peers, second, True))  4.51 us
    ppermute x4, waiting for transfers between devices, lon_send(): return lax.ppermute(edge, 'lon', swaps(lon_peers, second, True))  3.08 us
    unnamed x16, local copies, waits for them, and re-layouts  2.17 us
    dynamic_slice x1, local copies, waits for them, and re-layouts, lat_send(): lax.dynamic_slice_in_dim(state_field, start, REACH, 0)  1.14 us
    dynamic_slice x1, local copies, waits for them, and re-layouts, lon_send(): edge = lax.dynamic_slice_in_dim(values, start, width, 1)  1.11 us
  transfers between devices with their start and end apart: 6, of which 2 were waited for; matrix products, arithmetic and copies ran while one was open for 20% of the time, Pallas kernels for 18%

profile of v2, /device:TPU:0, one launch (start us, length us, event | category | flops | bytes accessed | tf_op | source)
XLA Modules:
  0.0 36.8 jit_solution(17768460153986576388)
XLA Ops:
  0.0 1.1 %constant_dynamic-slice_fusion = (bf16[24,8,640]{2,1,0:T(8,128)(2,1)S(1)}, bf16[24,8,640]{2,1,0:T(8,128)(2,1)S(1)}) fusion(bf16[24,64,640]{2,1,0:T(8,128)(2,1)} %x_ref.3, s32[]{:T(128)S(6)} %select_n.76, s32[]{:T(128)S(6)} %select_n.75), kind=kLoop, calls=%fused_computation.35 | loop fusion | bytes 983048 | tf_op jit(solution)/shard_map/dynamic_slice | solution.py:294
  1.1 3.4 %collective-permute-start.3 = (bf16[24,8,640]{2,1,0:T(8,128)(2,1)S(1)}, bf16[24,8,640]{2,1,0:T(8,128)(2,1)S(1)}, u32[]{:S(2)}, u32[]{:S(2)}) collective-permute-start(bf16[24,8,640]{2,1,0:T(8,128)(2,1)S(1)} %get-tuple-element.15), channel_id=1, source_target_pairs={{1,2},{3,4},{5,6},{7,0},{2,1},{4,3},{6,5},{0,7},{9,10},{11,12},{13... | collective-permute-start | bytes 737288 | tf_op jit(solution)/shard_map/ppermute | solution.py:295
  4.5 0.0 collective-permute-start.2
  4.5 0.7 %broadcast_compare_fusion = pred[24,5]{0,1:T(8,128)(4,1)S(1)} fusion(s32[24,5]{0,1:T(8,128)} %param.9), kind=kLoop, calls=%fused_computation.34 | loop fusion | flops 120 | bytes 600 | tf_op jit(solution)/shard_map/ne | solution.py:49
  5.2 0.8 %slice_bitcast_fusion.1 = (s32[24]{0:T(128)S(1)}, s32[24]{0:T(128)S(1)}) fusion(s32[24,2]{0,1:T(2,128)} %param.8), kind=kLoop, calls=%fused_computation.41 | loop fusion | bytes 384 | tf_op jit(solution)/shard_map/ge | solution.py:48
  6.0 0.1 copy.19
  6.1 0.1 copy.20
  6.2 1.3 %copy.21 = bf16[24,5,5,9]{3,2,1,0:T(8,128)(2,1)S(1)} copy(f32[24,5,5,9]{0,2,3,1:T(8,128)} %param.7) | data formatting | bytes 32400 | tf_op args[1]
  7.4 0.1 broadcast_and_fusion
  7.5 0.2 select_convert_fusion
  7.8 0.1 reshape.84
  7.9 1.1 %constant_dynamic-slice_fusion.2 = (bf16[4,64,640]{2,1,0:T(8,128)(2,1)S(1)}, bf16[4,64,640]{2,1,0:T(8,128)(2,1)S(1)}) fusion(bf16[24,64,640]{2,1,0:T(8,128)(2,1)} %x_ref.3, s32[]{:T(128)S(6)} %select_n.72, s32[]{:T(128)S(6)} %select_n.68), kind=kLoop, calls=%fused_computation.37 | loop fusion | bytes 1310728 | tf_op jit(solution)/shard_map/dynamic_slice | solution.py:287
  9.1 0.7 %collective-permute-start.1 = (bf16[272,640]{1,0:T(8,128)(2,1)S(1)}, bf16[272,640]{1,0:T(8,128)(2,1)S(1)}, u32[]{:S(2)}, u32[]{:S(2)}) collective-permute-start(bf16[272,640]{1,0:T(8,128)(2,1)S(1)} %fusion.3), channel_id=1, source_target_pairs={{8,16},{16,8},{9,17},{17,9},{10,18},{18,10},{11,19},{19,11},{12,20... | collective-permute-start | bytes 1044488 | tf_op jit(solution)/shard_map/ppermute | solution.py:290
  9.8 0.1 reshape.82
  9.9 4.4 %collective-permute-start = (bf16[272,640]{1,0:T(8,128)(2,1)S(1)}, bf16[272,640]{1,0:T(8,128)(2,1)S(1)}, u32[]{:S(2)}, u32[]{:S(2)}) collective-permute-start(bf16[272,640]{1,0:T(8,128)(2,1)S(1)} %fusion.2), channel_id=1, source_target_pairs={{0,8},{16,24},{8,0},{24,16},{1,9},{17,25},{9,1},{25,17},{2,10},{18... | collective-permute-start | bytes 1044488 | tf_op jit(solution)/shard_map/ppermute | solution.py:290
  14.4 0.3 copy.27
  14.7 0.1 copy.23
  14.8 0.0 copy-start
  14.9 0.7 %pad_maximum_fusion.wide_band = f32[8,8,256]{2,1,0:T(8,128)} fusion(f32[4,8,256]{2,1,0:T(8,128)S(1)} %get-tuple-element.26, f32[4,8,256]{2,1,0:T(8,128)S(1)} %get-tuple-element.25), kind=kLoop, calls=%fused_computation.21 | loop fusion | flops 16384 | bytes 131072 | tf_op jit(solution)/shard_map/concatenate | solution.py:340
  15.5 0.6 %pad_add_fusion.place_ref = s32[2]{0:T(128)} fusion(s32[1]{0:T(128)} %bitcast.1, s32[1]{0:T(128)} %bitcast), kind=kLoop, calls=%fused_computation.39 | loop fusion | flops 2 | bytes 16 | tf_op jit(solution)/shard_map/stack | solution.py:341
  16.1 0.0 copy-done
  16.1 6.5 %inner.1 = (bf16[960,256]{1,0:T(8,128)(2,1)}, bf16[8,64,640]{2,1,0:T(8,128)(2,1)}, bf16[24,16,640]{2,1,0:T(8,128)(2,1)}, bf16[16,48,640]{2,1,0:T(8,128)(2,1)}) custom-call(bf16[24,64,640]{2,1,0:T(8,128)(2,1)} %x_ref.3, f32[24,8,256]{2,1,0:T(8,128)} %copy-done, f32[5,640]{1,0:T(8,128)} %one_ref.3, f32[5,640]{1,0:T(8,128)} %two_ref.3), custom_call_target="tpu_custom_call" | custom-call | flops 2831155200 | bytes 3932160 | tf_op jit(solution)/shard_map/inner/pallas_call | solution.py:306
  22.6 0.0 collective-permute-done.1.lat_b
  22.6 0.0 copy-start.1
  22.6 0.3 collective-permute-done.lat_a
  22.9 0.0 copy-start.2
  22.9 0.1 select_n.79
  23.1 0.1 select_n.81
  23.3 0.1 reshape.89
  23.5 0.1 collective-permute-start.5
  23.6 1.0 %collective-permute-start.4 = (bf16[8,8,640]{2,1,0:T(8,128)(2,1)S(1)}, bf16[8,8,640]{2,1,0:T(8,128)(2,1)S(1)}, u32[]{:S(2)}, u32[]{:S(2)}) collective-permute-start(bf16[8,8,640]{2,1,0:T(8,128)(2,1)S(1)} %get-tuple-element.20), channel_id=1, source_target_pairs={{0,1},{2,3},{4,5},{6,7},{1,0},{3,2},{5,4},{7,6},{8,9},{10,11},{12,... | collective-permute-start | bytes 245768 | tf_op jit(solution)/shard_map/ppermute | solution.py:295
  24.6 0.6 %pad_convert_fusion.1.rim_band = f32[8,8,256]{2,1,0:T(8,128)} fusion(bf16[8,5,80]{2,1,0:T(8,128)(2,1)S(1)} %reshape.89), kind=kLoop, calls=%fused_computation.23 | loop fusion | flops 16384 | bytes 71936 | tf_op jit(solution)/shard_map/jit(_pad)/pad | solution.py:57
  25.2 0.0 collective-permute-done.3.lon_b
  25.2 0.0 copy-start.3
  25.2 0.0 collective-permute-done.2.lon_a
  25.2 0.0 copy-start.4
  25.3 3.1 %collective-permute-done.5.corner_b = bf16[8,8,640]{2,1,0:T(8,128)(2,1)S(1)} collective-permute-done((bf16[8,8,640]{2,1,0:T(8,128)(2,1)S(1)}, bf16[8,8,640]{2,1,0:T(8,128)(2,1)S(1)}, u32[]{:S(2)}, u32[]{:S(2)}) %collective-permute-start.5) | collective-permute-done | bytes 81952 | tf_op jit(solution)/shard_map/ppermute | solution.py:295
  28.3 0.0 copy-start.5
  28.3 0.0 collective-permute-done.4.corner_a
  28.3 0.0 copy-start.6
  28.3 0.0 copy-done.1
  28.3 0.0 copy-done.2
  28.4 0.0 copy-done.3
  28.4 0.0 copy-done.4
  28.4 0.6 %copy-done.5 = bf16[8,8,640]{2,1,0:T(8,128)(2,1)} copy-done((bf16[8,8,640]{2,1,0:T(8,128)(2,1)}, bf16[8,8,640]{2,1,0:T(8,128)(2,1)S(1)}, u32[]{:S(2)}) %copy-start.5) | copy-done | bytes 81944
  29.0 0.0 copy-done.6
  29.0 7.8 %rim.1 = bf16[24,64,640]{2,1,0:T(8,128)(2,1)} custom-call(s32[2]{0:T(128)} %pad_add_fusion.place_ref, bf16[24,64,640]{2,1,0:T(8,128)(2,1)} %x_ref.3, bf16[272,640]{1,0:T(8,128)(2,1)} %copy-done.2, bf16[272,640]{1,0:T(8,128)(2,1)} %copy-done.1, bf16[24,8,640]{2,1,0:T(8,128)(2,1)} %copy-done.4, bf16[24,8,640]{2,1,0:T(8,128)(2,1)} %copy-done.3, ...), custom_call_target="tpu_custom_call" | custom-call | flops 2831155200 | bytes 3932160 | tf_op jit(solution)/shard_map/rim/pallas_call | solution.py:342
  (13 shorter events, 0.3 us)
Async XLA Ops:
  1.1 24.1 %collective-permute-start.3 = (bf16[24,8,640]{2,1,0:T(8,128)(2,1)S(1)}, bf16[24,8,640]{2,1,0:T(8,128)(2,1)S(1)}, u32[]{:S(2)}, u32[]{:S(2)}) collective-permute-start(bf16[24,8,640]{2,1,0:T(8,128)(2,1)S(1)} %get-tuple-element.15), channel_id=1, source_target_pairs={{1,2},{3,4},{5,6},{7,0},{2,1},{4,3},{6,5},{0,7},{9,10},{11,12},{13... | collective-permute-start | bytes 737288 | tf_op jit(solution)/shard_map/ppermute | solution.py:295
  4.5 20.7 %collective-permute-start.2 = (bf16[24,8,640]{2,1,0:T(8,128)(2,1)S(1)}, bf16[24,8,640]{2,1,0:T(8,128)(2,1)S(1)}, u32[]{:S(2)}, u32[]{:S(2)}) collective-permute-start(bf16[24,8,640]{2,1,0:T(8,128)(2,1)S(1)} %get-tuple-element.16), channel_id=1, source_target_pairs={{0,1},{2,3},{4,5},{6,7},{1,0},{3,2},{5,4},{7,6},{8,9},{10,11},{12,... | collective-permute-start | bytes 737288 | tf_op jit(solution)/shard_map/ppermute | solution.py:295
  9.1 13.6 %collective-permute-start.1 = (bf16[272,640]{1,0:T(8,128)(2,1)S(1)}, bf16[272,640]{1,0:T(8,128)(2,1)S(1)}, u32[]{:S(2)}, u32[]{:S(2)}) collective-permute-start(bf16[272,640]{1,0:T(8,128)(2,1)S(1)} %fusion.3), channel_id=1, source_target_pairs={{8,16},{16,8},{9,17},{17,9},{10,18},{18,10},{11,19},{19,11},{12,20... | collective-permute-start | bytes 1044488 | tf_op jit(solution)/shard_map/ppermute | solution.py:290
  9.9 13.0 %collective-permute-start = (bf16[272,640]{1,0:T(8,128)(2,1)S(1)}, bf16[272,640]{1,0:T(8,128)(2,1)S(1)}, u32[]{:S(2)}, u32[]{:S(2)}) collective-permute-start(bf16[272,640]{1,0:T(8,128)(2,1)S(1)} %fusion.2), channel_id=1, source_target_pairs={{0,8},{16,24},{8,0},{24,16},{1,9},{17,25},{9,1},{25,17},{2,10},{18... | collective-permute-start | bytes 1044488 | tf_op jit(solution)/shard_map/ppermute | solution.py:290
  14.8 1.3 %copy-start = (f32[24,8,256]{2,1,0:T(8,128)}, f32[24,8,256]{2,1,0:T(8,128)S(1)}, u32[]{:S(2)}) copy-start(f32[24,8,256]{2,1,0:T(8,128)S(1)} %pad_convert_fusion.band_ref) | copy-start | bytes 589828
  22.6 5.7 %copy-start.1 = (bf16[272,640]{1,0:T(8,128)(2,1)}, bf16[272,640]{1,0:T(8,128)(2,1)S(1)}, u32[]{:S(2)}) copy-start(bf16[272,640]{1,0:T(8,128)(2,1)S(1)} %collective-permute-done.1.lat_b) | copy-start | bytes 1044484
  22.9 5.4 %copy-start.2 = (bf16[272,640]{1,0:T(8,128)(2,1)}, bf16[272,640]{1,0:T(8,128)(2,1)S(1)}, u32[]{:S(2)}) copy-start(bf16[272,640]{1,0:T(8,128)(2,1)S(1)} %collective-permute-done.lat_a) | copy-start | bytes 1044484
  23.5 4.8 %collective-permute-start.5 = (bf16[8,8,640]{2,1,0:T(8,128)(2,1)S(1)}, bf16[8,8,640]{2,1,0:T(8,128)(2,1)S(1)}, u32[]{:S(2)}, u32[]{:S(2)}) collective-permute-start(bf16[8,8,640]{2,1,0:T(8,128)(2,1)S(1)} %get-tuple-element.19), channel_id=1, source_target_pairs={{1,2},{3,4},{5,6},{7,0},{2,1},{4,3},{6,5},{0,7},{9,10},{11,12},{13... | collective-permute-start | bytes 245768 | tf_op jit(solution)/shard_map/ppermute | solution.py:295
  23.6 4.8 %collective-permute-start.4 = (bf16[8,8,640]{2,1,0:T(8,128)(2,1)S(1)}, bf16[8,8,640]{2,1,0:T(8,128)(2,1)S(1)}, u32[]{:S(2)}, u32[]{:S(2)}) collective-permute-start(bf16[8,8,640]{2,1,0:T(8,128)(2,1)S(1)} %get-tuple-element.20), channel_id=1, source_target_pairs={{0,1},{2,3},{4,5},{6,7},{1,0},{3,2},{5,4},{7,6},{8,9},{10,11},{12,... | collective-permute-start | bytes 245768 | tf_op jit(solution)/shard_map/ppermute | solution.py:295
  25.2 3.1 %copy-start.3 = (bf16[24,8,640]{2,1,0:T(8,128)(2,1)}, bf16[24,8,640]{2,1,0:T(8,128)(2,1)S(1)}, u32[]{:S(2)}) copy-start(bf16[24,8,640]{2,1,0:T(8,128)(2,1)S(1)} %collective-permute-done.3.lon_b) | copy-start | bytes 737284
  25.2 3.1 %copy-start.4 = (bf16[24,8,640]{2,1,0:T(8,128)(2,1)}, bf16[24,8,640]{2,1,0:T(8,128)(2,1)S(1)}, u32[]{:S(2)}) copy-start(bf16[24,8,640]{2,1,0:T(8,128)(2,1)S(1)} %collective-permute-done.2.lon_a) | copy-start | bytes 737284
  28.3 0.6 %copy-start.5 = (bf16[8,8,640]{2,1,0:T(8,128)(2,1)}, bf16[8,8,640]{2,1,0:T(8,128)(2,1)S(1)}, u32[]{:S(2)}) copy-start(bf16[8,8,640]{2,1,0:T(8,128)(2,1)S(1)} %collective-permute-done.5.corner_b) | copy-start | bytes 245764
  28.3 0.7 %copy-start.6 = (bf16[8,8,640]{2,1,0:T(8,128)(2,1)}, bf16[8,8,640]{2,1,0:T(8,128)(2,1)S(1)}, u32[]{:S(2)}) copy-start(bf16[8,8,640]{2,1,0:T(8,128)(2,1)S(1)} %collective-permute-done.4.corner_a) | copy-start | bytes 245764

commit v3 on v0

v3 whole, which is shorter than its diff:
```python
import functools

import jax
import jax.numpy as jnp
from jax import lax
from jax.experimental import pallas as pl
from jax.experimental.pallas import tpu as pltpu
from jax.sharding import PartitionSpec as P

LAT_REACH = 2
LON_REACH = 4
REACH = 2 * LAT_REACH
BANDS = 2 * LAT_REACH + 1
CELLS = 8
WINDOW = CELLS + 2 * LON_REACH
LANES = 128
DEPTH = 2 * LANES
TILE = 16
VMEM_BYTES = 56 * 1024 * 1024
F32, BF16 = jnp.float32, jnp.bfloat16

ERF_SERIES = (
    1.5956562720156744,
    0.2917503271976864,
    -0.003995570947534282,
    -0.003914369984884403,
    0.0005729703632347449,
)


def erf_gelu(half):
    square = half * half
    series = ERF_SERIES[-1] * square + ERF_SERIES[-2]
    for term in ERF_SERIES[-3::-1]:
        series = series * square + term
    return half + half * jnp.tanh(half * series)


def swaps(peers, second, wrap):
    pairs = [(i, i + 1) for i in range(1 if second else 0, peers - 1, 2)]
    if second and wrap:
        pairs.append((peers - 1, 0))
    return pairs + [(j, i) for i, j in pairs]


def pairs_of(items):
    return [items[i : i + 2] for i in range(0, len(items), 2)]


def lanes_of(chunk):
    return slice(chunk * LANES, (chunk + 1) * LANES)


def fill_toeplitz(toeplitz, line_of, rows, bases, place_of):
    group = bases * CELLS
    blank = jnp.zeros((CELLS, DEPTH - LANES), F32)
    for row in range(0, rows, 2):
        parts = []
        for r in (row, row + 1):
            for basis in range(bases):
                line = jnp.broadcast_to(line_of(r, basis), (CELLS, LANES))
                line = jnp.concatenate([line, blank], 1)
                parts.append(pltpu.roll(line, place_of(r) * WINDOW, 1, stride=1, stride_axis=0))
        toeplitz[row * group : (row + 2) * group, :] = jnp.concatenate(parts, 0).astype(BF16)


def lane_weights(ref, scale=1.0):
    bases, channels = ref.shape
    return [[ref[k : k + 1, lanes_of(c)] * scale for k in range(bases)] for c in range(channels // LANES)]


def product(matrix, windows, weights):
    wide = [w.astype(BF16).reshape(DEPTH, LANES) for w in windows]
    result = jnp.dot(matrix, jnp.concatenate(wide, 1), preferred_element_type=F32)
    bases = len(weights[0])
    result = result.reshape(-1, bases, CELLS, len(windows) * LANES)
    total = None
    for k in range(bases):
        term = result[:, k] * jnp.concatenate([w[k] for w in weights], 1)
        total = term if total is None else total + term
    return [total[:, :, i * LANES : (i + 1) * LANES] for i in range(len(windows))]


def prep_kernel(
    place_ref, rows_ref, tiles_ref, filter_ref, edge_ref, mask_ref,
    lat_a, lat_b, lon_a, lon_b, lines, sides, padded, tags, packed, sems,
):
    bases, lags, bands, rows = filter_ref.shape
    groups = lat_a.shape[0] - 1
    lat_odd, lon_odd = place_ref[0], place_ref[1]
    start_a = (1 - lat_odd) * (rows_ref.shape[0] - groups)
    start_b = lat_odd * (rows_ref.shape[0] - groups)
    copies = [
        pltpu.make_async_copy(tiles_ref.at[:, 0], sides.at[0], sems.at[0]),
        pltpu.make_async_copy(tiles_ref.at[:, tiles_ref.shape[1] - 1], sides.at[1], sems.at[1]),
        pltpu.make_async_copy(rows_ref.at[pl.ds(start_a, groups)], lat_a.at[pl.ds(0, groups)], sems.at[2]),
        pltpu.make_async_copy(rows_ref.at[pl.ds(start_b, groups)], lat_b.at[pl.ds(0, groups)], sems.at[3]),
    ]
    for copy in copies:
        copy.start()

    source = place_ref[2] + lax.broadcasted_iota(jnp.int32, (bands, rows), 1) - LAT_REACH
    source = source + lax.broadcasted_iota(jnp.int32, (bands, rows), 0)
    inside = (source >= edge_ref[0:1, :]) & (source < edge_ref[1:2, :])
    padded[...] = jnp.zeros_like(padded)
    for k in range(bases):
        keep = inside & (mask_ref[k : k + 1, :] != 0)
        for m in range(lags):
            padded[k, m * 8 : m * 8 + bands, :rows] = jnp.where(keep, filter_ref[k, m], 0.0)
    at = lax.broadcasted_iota(jnp.int32, (LANES, LANES), 0)
    lane = lax.broadcasted_iota(jnp.int32, (LANES, LANES), 1)
    chosen = (at // 8 == lane % WINDOW) & (at % 8 == lane // WINDOW) & (at % 8 < bands) & (at // 8 < lags)
    chosen = jnp.where(chosen, 1.0, 0.0).astype(BF16)
    tags[...] = jnp.zeros_like(tags)
    for k in range(bases):
        line = jnp.dot(padded[k].T.astype(BF16), chosen, preferred_element_type=F32)
        lines[k] = line[:rows]
        span = slice(k * LAT_REACH, (k + 1) * LAT_REACH)
        tags[0, span] = line[:LAT_REACH]
        tags[1, span] = line[rows - LAT_REACH : rows]
    blank = jnp.zeros((TILE, packed.shape[2] - LANES), BF16)
    first = jnp.concatenate([tags[0].astype(BF16), blank], 1)
    last = jnp.concatenate([tags[1].astype(BF16), blank], 1)
    packed[0] = jnp.where(lat_odd == 1, first, last)
    packed[1] = jnp.where(lat_odd == 1, last, first)
    tag_copies = [
        pltpu.make_async_copy(packed.at[0], lat_a.at[groups], sems.at[4]),
        pltpu.make_async_copy(packed.at[1], lat_b.at[groups], sems.at[5]),
    ]
    for copy in tag_copies:
        copy.start()
    copies[0].wait()
    copies[1].wait()
    leading = sides[0].astype(F32)[:, :CELLS]
    trailing = sides[1].astype(F32)[:, TILE - CELLS :]
    odd = lon_odd == 1
    lon_a[...] = jnp.where(odd, leading, trailing).reshape(lon_a.shape).astype(BF16)
    lon_b[...] = jnp.where(odd, trailing, leading).reshape(lon_b.shape).astype(BF16)
    for copy in copies[2:] + tag_copies:
        copy.wait()


def inner_kernel(
    block, x_ref, lines_ref, one_ref, two_ref, toeplitz_out, rows_out, cells_out, sides_out, out_ref,
    toeplitz, x_buf, field, hidden, edge_rows, edge_cells, sides, result, in_sems, out_sems,
):
    rows, cells, channels = x_ref.shape
    bases = one_ref.shape[0]
    group = bases * CELLS
    chunks = channels // LANES
    copies = [
        pltpu.make_async_copy(x_ref.at[:, :, pl.ds(c * LANES, LANES)], x_buf.at[c], in_sems.at[c])
        for c in range(chunks)
    ]
    for copy in copies:
        copy.start()
    fill_toeplitz(toeplitz, lambda r, k: lines_ref[k, r : r + 1, :], rows, bases, lambda r: r % block)
    pending = [pltpu.make_async_copy(toeplitz, toeplitz_out, out_sems.at[0])]
    pending[0].start()
    one, two = lane_weights(one_ref, 0.5), lane_weights(two_ref)
    starts = range(0, rows, block)
    windows = (cells - WINDOW) // CELLS + 1
    span = windows * CELLS

    def load(c):
        copies[c].wait()
        blank = jnp.zeros((LAT_REACH, cells, LANES), F32)
        field[c, :LAT_REACH] = blank
        field[c, LAT_REACH : LAT_REACH + rows] = x_buf[c].astype(F32)
        field[c, LAT_REACH + rows :] = blank
        blank = jnp.zeros((REACH, span, LANES), F32)
        hidden[c, :REACH] = blank
        hidden[c, rows:] = blank

    def first(items):
        for start in starts:
            low, high = max(start, LAT_REACH), min(start + block, rows - LAT_REACH)
            values = product(
                toeplitz[low * group : high * group, :],
                [field[c, start : start + block + REACH, w * CELLS : w * CELLS + WINDOW] for c, w in items],
                [one[c] for c, w in items],
            )
            for (c, w), value in zip(items, values):
                hidden[c, low + LAT_REACH : high + LAT_REACH, w * CELLS : (w + 1) * CELLS] = erf_gelu(value)

    def second(c):
        at = LAT_REACH + LAT_REACH
        for i, row in enumerate((at, rows - REACH)):
            edge_rows[c, i * REACH : (i + 1) * REACH, :span] = hidden[c, row : row + REACH].astype(BF16)
            edge_rows[c, i * REACH : (i + 1) * REACH, span:] = jnp.zeros((REACH, cells - span, LANES), BF16)
        part = hidden[c, 2 * REACH : rows - REACH]
        edge_cells[c] = jnp.concatenate([part[:, :CELLS], part[:, span - CELLS :]], 1).astype(BF16)
        for start in starts:
            low, high = max(start, REACH), min(start + block, rows - REACH)
            matrix = toeplitz[low * group : high * group, :]
            values = []
            for pair in pairs_of(list(range(windows - 1))):
                tall = [hidden[c, start : start + block + REACH, w * CELLS : w * CELLS + WINDOW] for w in pair]
                values += product(matrix, tall, [two[c]] * len(pair))
            whole = jnp.concatenate(values[1:-1], 1).astype(BF16)
            result[c, low - REACH : high - REACH] = whole
            ends = jnp.concatenate([values[0], values[-1]], 1).astype(BF16)
            sides[c, low - REACH : high - REACH] = ends
        lanes = pl.ds(c * LANES, LANES)
        moves = [
            (edge_rows.at[c], rows_out.at[:, :, lanes]),
            (edge_cells.at[c], cells_out.at[:, :, lanes]),
            (sides.at[c], sides_out.at[:, :, lanes]),
            (result.at[c], out_ref.at[pl.ds(REACH, rows - 2 * REACH), pl.ds(TILE, cells - 2 * TILE), lanes]),
        ]
        for i, (source, target) in enumerate(moves):
            pending.append(pltpu.make_async_copy(source, target, out_sems.at[1 + len(moves) * c + i]))
            pending[-1].start()

    loaded = done = 0
    work = pairs_of([(c, w) for c in range(chunks) for w in range(windows)])
    for i, items in enumerate(work):
        while loaded <= items[-1][0]:
            load(loaded)
            loaded += 1
        first(items)
        upcoming = work[i + 1][0][0] if i + 1 < len(work) else chunks
        while done < upcoming:
            second(done)
            done += 1
    for copy in pending:
        copy.wait()


def rim_kernel(
    block, place_ref, x_ref, lat_a, lat_b, lon_a, lon_b, corner_a, corner_b, rows_in, cells_in, sides_in, toeplitz_in,
    lines_ref, one_ref, two_ref, begun_ref, out_ref,
    toeplitz, rim_toeplitz, wide_toeplitz, own_rows, own_cells, lat_buf, tag_buf, lon_buf, corner_buf,
    rows_buf, cells_buf, sides_buf, field, hidden, rim_out, side_out, first_sems, in_sems, out_sems,
):
    del begun_ref
    rows, cells, channels = x_ref.shape
    bases = one_ref.shape[0]
    group = bases * CELLS
    chunks = channels // LANES
    lat_odd, lon_odd = place_ref[0], place_ref[1]
    edge, wide = REACH * cells, rows * CELLS
    low_a, low_b = 1 - lat_odd, lat_odd
    left_a, left_b = 1 - lon_odd, lon_odd
    early = [
        pltpu.make_async_copy(lat_a.at[pl.ds(edge, TILE), pl.ds(0, LANES)], tag_buf.at[low_a], first_sems.at[0]),
        pltpu.make_async_copy(lat_b.at[pl.ds(edge, TILE), pl.ds(0, LANES)], tag_buf.at[low_b], first_sems.at[1]),
        pltpu.make_async_copy(toeplitz_in, toeplitz, first_sems.at[2]),
    ]
    for copy in early:
        copy.start()
    copies = []
    for c in range(chunks):
        lanes = pl.ds(c * LANES, LANES)
        half = REACH * CELLS
        moves = [
            (lat_a.at[pl.ds(0, edge), lanes], lat_buf.at[c, low_a]),
            (lat_b.at[pl.ds(0, edge), lanes], lat_buf.at[c, low_b]),
            (lon_a.at[:, lanes], lon_buf.at[c, left_a]),
            (lon_b.at[:, lanes], lon_buf.at[c, left_b]),
            (corner_a.at[pl.ds(0, half), lanes], corner_buf.at[c, left_a, low_a]),
            (corner_a.at[pl.ds(half, half), lanes], corner_buf.at[c, left_a, low_b]),
            (corner_b.at[pl.ds(0, half), lanes], corner_buf.at[c, left_b, low_a]),
            (corner_b.at[pl.ds(half, half), lanes], corner_buf.at[c, left_b, low_b]),
            (x_ref.at[pl.ds(0, REACH), :, lanes], own_rows.at[c, 0]),
            (x_ref.at[pl.ds(rows - REACH, REACH), :, lanes], own_rows.at[c, 1]),
            (x_ref.at[pl.ds(REACH, rows - 2 * REACH), pl.ds(0, TILE), lanes], own_cells.at[c, 0]),
            (x_ref.at[pl.ds(REACH, rows - 2 * REACH), pl.ds(cells - TILE, TILE), lanes], own_cells.at[c, 1]),
            (rows_in.at[:, :, lanes], rows_buf.at[c]),
            (cells_in.at[:, :, lanes], cells_buf.at[c]),
            (sides_in.at[:, :, lanes], sides_buf.at[c]),
        ]
        copies.append([pltpu.make_async_copy(s, t, in_sems.at[c, i]) for i, (s, t) in enumerate(moves)])
        for copy in copies[-1]:
            copy.start()

    one, two = lane_weights(one_ref, 0.5), lane_weights(two_ref)
    ends = list(range(REACH)) + list(range(rows - REACH, rows))

    def place_of(r):
        return r if r < REACH else REACH + r

    fill_toeplitz(
        wide_toeplitz, lambda r, k: lines_ref[k, ends[r] : ends[r] + 1, :], 2 * REACH, bases, place_of
    )
    early[0].wait()
    early[1].wait()
    tags = tag_buf[...].astype(F32)

    def rim_line(r, k):
        if r < LAT_REACH:
            return tags[0, k * LAT_REACH + r : k * LAT_REACH + r + 1, :]
        if r >= 2 * REACH - LAT_REACH:
            at = k * LAT_REACH + r - (2 * REACH - LAT_REACH)
            return tags[1, at : at + 1, :]
        at = r - LAT_REACH if r < REACH else rows - LAT_REACH + r - REACH
        return lines_ref[k, at : at + 1, :]

    fill_toeplitz(rim_toeplitz, rim_line, 2 * REACH, bases, place_of)
    early[2].wait()

    def load(c):
        for copy in copies[c]:
            copy.wait()
        for side in range(2):
            at = slice(side * (rows + REACH), side * (rows + REACH) + REACH)
            field[c, at, CELLS : CELLS + cells] = lat_buf[c, side].astype(F32).reshape(REACH, cells, LANES)
            own = slice(REACH + side * (rows - REACH), 2 * REACH + side * (rows - REACH))
            field[c, own, CELLS : CELLS + cells] = own_rows[c, side].astype(F32)
            middle = slice(2 * REACH, rows)
            field[c, middle, CELLS + side * (cells - TILE) : CELLS + TILE + side * (cells - TILE)] = own_cells[
                c, side
            ].astype(F32)
            span = slice(side * (CELLS + cells), side * (CELLS + cells) + CELLS)
            field[c, REACH : REACH + rows, span] = lon_buf[c, side].astype(F32).reshape(rows, CELLS, LANES)
            for end in range(2):
                part = corner_buf[c, side, end].astype(F32).reshape(REACH, CELLS, LANES)
                field[c, end * (rows + REACH) : end * (rows + REACH) + REACH, span] = part
        span = cells - CELLS
        for i, at in enumerate((REACH, rows - REACH)):
            part = rows_buf[c, i * REACH : (i + 1) * REACH].astype(F32)
            hidden[c, at : at + REACH, CELLS : CELLS + span] = part[:, :span]
        part = cells_buf[c].astype(F32)
        at = slice(2 * REACH, rows - REACH)
        hidden[c, at, CELLS : 2 * CELLS] = part[:, :CELLS]
        hidden[c, at, cells - CELLS : cells] = part[:, CELLS:]

    def rims(ref, c, at):
        span = slice(at, at + WINDOW)
        last = ref.shape[1] - 2 * REACH
        return jnp.concatenate([ref[c, : 2 * REACH, span], ref[c, last:, span]], 0)

    columns = cells // CELLS + 1

    def first_rows(items):
        values = product(rim_toeplitz[...], [rims(field, c, w * CELLS) for c, w in items], [one[c] for c, w in items])
        for (c, w), value in zip(items, values):
            value = erf_gelu(value)
            hidden[c, :REACH, w * CELLS : (w + 1) * CELLS] = value[:REACH]
            hidden[c, rows:, w * CELLS : (w + 1) * CELLS] = value[REACH:]

    def first_sides(c):
        for start in range(0, rows, block):
            low, high = max(start, LAT_REACH), min(start + block, rows - LAT_REACH)
            at = slice(start + LAT_REACH, start + LAT_REACH + block + REACH)
            sides = (0, cells)
            tall = [field[c, at, s : s + WINDOW] for s in sides]
            values = product(toeplitz[low * group : high * group, :], tall, [one[c]] * 2)
            for s, value in zip(sides, values):
                hidden[c, low + LAT_REACH : high + LAT_REACH, s : s + CELLS] = erf_gelu(value)

    pending = []

    def second(c):
        lanes = pl.ds(c * LANES, LANES)
        for pair in pairs_of([w * CELLS for w in range(columns - 1)]):
            values = product(wide_toeplitz[...], [rims(hidden, c, s) for s in pair], [two[c]] * 2)
            rim_out[c, :, pair[0] : pair[0] + 2 * CELLS] = jnp.concatenate(values, 1).astype(BF16)
        for start in range(0, rows, block):
            low, high = max(start, REACH), min(start + block, rows - REACH)
            at = slice(start, start + block + REACH)
            tall = [hidden[c, at, s : s + WINDOW] for s in (0, cells - CELLS)]
            values = product(toeplitz[low * group : high * group, :], tall, [two[c]] * 2)
            inner = sides_buf[c, low - REACH : high - REACH].astype(F32)
            side_out[c, 0, low - REACH : high - REACH] = jnp.concatenate([values[0], inner[:, :CELLS]], 1).astype(BF16)
            side_out[c, 1, low - REACH : high - REACH] = jnp.concatenate([inner[:, CELLS:], values[1]], 1).astype(BF16)
        middle = pl.ds(REACH, rows - 2 * REACH)
        moves = [
            (rim_out.at[c, pl.ds(0, REACH)], out_ref.at[pl.ds(0, REACH), :, lanes]),
            (rim_out.at[c, pl.ds(REACH, REACH)], out_ref.at[pl.ds(rows - REACH, REACH), :, lanes]),
            (side_out.at[c, 0], out_ref.at[middle, pl.ds(0, TILE), lanes]),
            (side_out.at[c, 1], out_ref.at[middle, pl.ds(cells - TILE, TILE), lanes]),
        ]
        for i, (source, target) in enumerate(moves):
            pending.append(pltpu.make_async_copy(source, target, out_sems.at[c, i]))
            pending[-1].start()

    loaded = done = 0
    work = pairs_of([(c, w) for c in range(chunks) for w in range(columns)])
    for i, items in enumerate(work):
        while loaded <= items[-1][0]:
            load(loaded)
            first_sides(loaded)
            loaded += 1
        first_rows(items)
        upcoming = work[i + 1][0][0] if i + 1 < len(work) else chunks
        while done < upcoming:
            second(done)
            done += 1
    for copy in pending:
        copy.wait()


def per_device(state_field, filters, band_edges, basis_mask, weights_one, weights_two):
    rows, cells, channels = state_field.shape
    bases = filters.shape[1]
    group = bases * CELLS
    chunks = channels // LANES
    tiles = cells // TILE
    edge = REACH * cells
    block = max(b for b in range(2, rows + 1, 2) if rows % b == 0 and (b + REACH) * WINDOW <= DEPTH)
    lat_peers, lon_peers = lax.axis_size("lat"), lax.axis_size("lon")
    lat, lon = lax.axis_index("lat"), lax.axis_index("lon")
    place = jnp.stack([lat % 2, lon % 2, lat * rows]).astype(jnp.int32)

    anywhere = pl.BlockSpec(memory_space=pl.ANY)
    vmem = pl.BlockSpec(memory_space=pltpu.VMEM)
    smem = pl.BlockSpec(memory_space=pltpu.SMEM)
    params = pltpu.CompilerParams(vmem_limit_bytes=VMEM_BYTES)
    dma = pltpu.SemaphoreType.DMA

    def array(*shape, dtype=BF16):
        return jax.ShapeDtypeStruct(shape, dtype)

    def scratch(*shape, dtype=BF16):
        return pltpu.VMEM(shape, dtype)

    groups = REACH * tiles
    lat_a, lat_b, lon_a, lon_b, lines = pl.pallas_call(
        prep_kernel,
        out_shape=(
            array(groups + 1, TILE, channels), array(groups + 1, TILE, channels),
            array(rows * CELLS, channels), array(rows * CELLS, channels),
            array(bases, rows, LANES, dtype=F32),
        ),
        in_specs=[smem, anywhere, anywhere, vmem, vmem, vmem],
        out_specs=(anywhere, anywhere, vmem, vmem, vmem),
        scratch_shapes=[
            scratch(2, rows, TILE, channels), scratch(bases, LANES, LANES, dtype=F32),
            scratch(2, TILE, LANES, dtype=F32), scratch(2, TILE, channels), dma((6,)),
        ],
        compiler_params=params,
        cost_estimate=pl.CostEstimate(flops=0, bytes_accessed=4 * edge * channels, transcendentals=0),
        name="prep",
    )(
        place, state_field.reshape(rows * tiles, TILE, channels), state_field.reshape(rows, tiles, TILE, channels),
        filters.transpose(1, 3, 2, 0), band_edges.T, basis_mask.T,
    )
    lat_a = lax.ppermute(lat_a, "lat", swaps(lat_peers, False, False)).reshape(edge + TILE, channels)
    lat_b = lax.ppermute(lat_b, "lat", swaps(lat_peers, True, False)).reshape(edge + TILE, channels)
    lon_b = lax.ppermute(lon_b, "lon", swaps(lon_peers, True, True))
    lon_a = lax.ppermute(lon_a, "lon", swaps(lon_peers, False, True))

    middle = rows - 2 * REACH
    flops = 2 * (2 * rows - 3 * REACH) * (cells - 2 * CELLS) * bases * DEPTH * channels
    cost = pl.CostEstimate(flops=flops, bytes_accessed=4 * state_field.size, transcendentals=0)
    toeplitz, edge_rows, edge_cells, sides, begun = pl.pallas_call(
        functools.partial(inner_kernel, block),
        out_shape=(
            array(rows * group, DEPTH), array(2 * REACH, cells, channels),
            array(middle - REACH, TILE, channels), array(middle, TILE, channels), array(rows, cells, channels),
        ),
        in_specs=[anywhere, vmem, vmem, vmem],
        out_specs=(anywhere,) * 5,
        scratch_shapes=[
            scratch(rows * group, DEPTH), scratch(chunks, rows, cells, LANES),
            scratch(chunks, rows + REACH, cells, LANES, dtype=F32),
            scratch(chunks, rows + REACH, cells - CELLS, LANES, dtype=F32),
            scratch(chunks, 2 * REACH, cells, LANES), scratch(chunks, middle - REACH, TILE, LANES),
            scratch(chunks, middle, TILE, LANES), scratch(chunks, middle, cells - 2 * TILE, LANES),
            dma((chunks,)), dma((1 + 4 * chunks,)),
        ],
        compiler_params=params,
        cost_estimate=cost,
        name="inner",
    )(state_field, lines, weights_one, weights_two)

    def corner_send(leading, second):
        start = jnp.where(leading, 0, cells - CELLS)
        joined = [v[:edge].reshape(REACH, cells, channels) for v in (lat_a, lat_b)]
        parts = [lax.dynamic_slice_in_dim(v, start, CELLS, 1) for v in joined]
        sent = jnp.concatenate(parts, 0).reshape(2 * REACH * CELLS, channels)
        return lax.ppermute(sent, "lon", swaps(lon_peers, second, True))

    corner_b = corner_send(lon % 2 == 0, True)
    corner_a = corner_send(lon % 2 == 1, False)
    return pl.pallas_call(
        functools.partial(rim_kernel, block),
        out_shape=array(rows, cells, channels),
        in_specs=[smem] + [anywhere] * 11 + [vmem] * 3 + [anywhere],
        out_specs=anywhere,
        input_output_aliases={15: 0},
        scratch_shapes=[
            scratch(rows * group, DEPTH), scratch(2 * REACH * group, DEPTH), scratch(2 * REACH * group, DEPTH),
            scratch(chunks, 2, REACH, cells, LANES), scratch(chunks, 2, middle, TILE, LANES),
            scratch(chunks, 2, edge, LANES), scratch(2, TILE, LANES), scratch(chunks, 2, rows * CELLS, LANES),
            scratch(chunks, 2, 2, REACH * CELLS, LANES), scratch(chunks, 2 * REACH, cells, LANES),
            scratch(chunks, middle - REACH, TILE, LANES), scratch(chunks, middle, TILE, LANES),
            scratch(chunks, rows + 2 * REACH, cells + 2 * CELLS, LANES, dtype=F32),
            scratch(chunks, rows + REACH, cells + CELLS, LANES, dtype=F32),
            scratch(chunks, 2 * REACH, cells, LANES), scratch(chunks, 2, middle, TILE, LANES),
            dma((3,)), dma((chunks, 15)), dma((chunks, 4)),
        ],
        compiler_params=params,
        cost_estimate=cost,
        name="rim",
    )(
        place, state_field, lat_a, lat_b, lon_a, lon_b, corner_a, corner_b, edge_rows, edge_cells, sides,
        toeplitz, lines, weights_one, weights_two, begun,
    )


def solution(mesh):
    placed = (
        P("lat", "lon", None),
        P("lat", None, None, None),
        P("lat", None),
        P("lat", None),
        P(),
        P(),
    )
    return jax.shard_map(
        per_device, mesh=mesh, in_specs=placed, out_specs=P("lat", "lon", None), check_vma=False
    )
```

time: 192 us -> 56.6 us (0.29)
  the two profiles are of different devices: /device:TPU:0 before, /device:TPU:16 now
where the time goes in v3:
time: 56.6 us; the launch traced here: 56.3 us
  Pallas kernels  38.6 us (68%)
  starting transfers between devices  8.85 us (16%)
  waiting for transfers between devices  7.11 us (13%)
  local copies, waits for them, and re-layouts  0.89 us (2%)
  other arithmetic  0.69 us (1%)
    pallas_call x1, Pallas kernels, per_device(): pl.pallas_call(prep_kernel, out_shape=(array(groups + 1, TILE, channels),...  22.8 us
    pallas_call x1, Pallas kernels, per_device(): pl.pallas_call(functools.partial(rim_kernel, block), out_shape=array(rows...  8.19 us
    pallas_call x1, Pallas kernels, per_device(): pl.pallas_call(functools.partial(inner_kernel, block), out_shape=(array(r...  7.62 us
    ppermute x1, waiting for transfers between devices, per_device(): lax.ppermute(lat_a, 'lat', swaps(lat_peers, False, False))  3.98 us
    ppermute x1, waiting for transfers between devices, per_device(): lax.ppermute(lat_b, 'lat', swaps(lat_peers, True, False))  3.12 us
    ppermute x2, starting transfers between devices, corner_send(): return lax.ppermute(sent, 'lon', swaps(lon_peers, second, True))  2.68 us
    ppermute x1, starting transfers between devices, per_device(): lon_b = lax.ppermute(lon_b, 'lon', swaps(lon_peers, True, True))  2.55 us
    ppermute x1, starting transfers between devices, per_device(): lax.ppermute(lat_b, 'lat', swaps(lat_peers, True, False))  1.91 us
  transfers between devices with their start and end apart: 6, of which 2 were waited for; matrix products, arithmetic and copies ran while one was open for 0% of the time, Pallas kernels for 14%

profile of v3, /device:TPU:16, one launch (start us, length us, event | category | flops | bytes accessed | tf_op | source)
XLA Modules:
  0.0 56.3 jit_solution(11354867574854788260)
XLA Ops:
  0.0 0.7 %pad_add_fusion.place_ref = s32[3]{0:T(128)} fusion(s32[1]{0:T(128)} %bitcast.2, s32[1]{0:T(128)} %bitcast.1, s32[1]{0:T(128)} %bitcast), kind=kLoop, calls=%fused_computation.6 | loop fusion | flops 6 | bytes 24 | tf_op jit(solution)/shard_map/stack | solution.py:404
  0.7 22.8 %prep.1 = (bf16[17,16,640]{2,1,0:T(8,128)(2,1)}, bf16[17,16,640]{2,1,0:T(8,128)(2,1)}, bf16[192,640]{1,0:T(8,128)(2,1)}, bf16[192,640]{1,0:T(8,128)(2,1)}, f32[5,24,128]{2,1,0:T(8,128)}) custom-call(s32[3]{0:T(128)} %pad_add_fusion.place_ref, bf16[96,16,640]{2,1,0:T(8,128)(2,1)} %bitcast.16, bf16[24,4,16,640]{3,2,1,0:T(8,128)(2,1)} %bitcast.17, ...), custom_call_target="tpu_custom_call" | custom-call | bytes 655360 | tf_op jit(solution)/shard_map/prep/pallas_call | solution.py:419
  23.5 1.6 %collective-permute-start = (bf16[17,16,640]{2,1,0:T(8,128)(2,1)}, bf16[17,16,640]{2,1,0:T(8,128)(2,1)S(1)}, u32[]{:S(2)}, u32[]{:S(2)}) collective-permute-start(bf16[17,16,640]{2,1,0:T(8,128)(2,1)} %get-tuple-element.15), channel_id=1, source_target_pairs={{0,8},{16,24},{8,0},{24,16},{1,9},{17,25},{9,1},{25,17},{2,10},{18... | collective-permute-start | bytes 1044488 | tf_op jit(solution)/shard_map/ppermute | solution.py:439
  25.1 1.9 %collective-permute-start.1 = (bf16[17,16,640]{2,1,0:T(8,128)(2,1)}, bf16[17,16,640]{2,1,0:T(8,128)(2,1)S(1)}, u32[]{:S(2)}, u32[]{:S(2)}) collective-permute-start(bf16[17,16,640]{2,1,0:T(8,128)(2,1)} %get-tuple-element.16), channel_id=1, source_target_pairs={{8,16},{16,8},{9,17},{17,9},{10,18},{18,10},{11,19},{19,11},{12,20... | collective-permute-start | bytes 1044488 | tf_op jit(solution)/shard_map/ppermute | solution.py:440
  27.0 0.1 collective-permute-start.2
  27.1 2.5 %collective-permute-start.3 = (bf16[192,640]{1,0:T(8,128)(2,1)}, bf16[192,640]{1,0:T(8,128)(2,1)S(1)}, u32[]{:S(2)}, u32[]{:S(2)}) collective-permute-start(bf16[192,640]{1,0:T(8,128)(2,1)} %get-tuple-element.18), channel_id=1, source_target_pairs={{1,2},{3,4},{5,6},{7,0},{2,1},{4,3},{6,5},{0,7},{9,10},{11,12},{13... | collective-permute-start | bytes 737288 | tf_op jit(solution)/shard_map/ppermute | solution.py:441
  29.7 4.0 %collective-permute-done = bf16[17,16,640]{2,1,0:T(8,128)(2,1)S(1)} collective-permute-done((bf16[17,16,640]{2,1,0:T(8,128)(2,1)}, bf16[17,16,640]{2,1,0:T(8,128)(2,1)S(1)}, u32[]{:S(2)}, u32[]{:S(2)}) %collective-permute-start) | collective-permute-done | bytes 348192 | tf_op jit(solution)/shard_map/ppermute | solution.py:439
  33.6 0.0 copy-start
  33.7 3.1 %collective-permute-done.1 = bf16[17,16,640]{2,1,0:T(8,128)(2,1)S(1)} collective-permute-done((bf16[17,16,640]{2,1,0:T(8,128)(2,1)}, bf16[17,16,640]{2,1,0:T(8,128)(2,1)S(1)}, u32[]{:S(2)}, u32[]{:S(2)}) %collective-permute-start.1) | collective-permute-done | bytes 348192 | tf_op jit(solution)/shard_map/ppermute | solution.py:440
  36.8 0.0 copy-start.1
  36.9 0.1 collective-permute-start.4
  37.0 2.6 %collective-permute-start.5 = (bf16[64,640]{1,0:T(8,128)(2,1)S(1)}, bf16[64,640]{1,0:T(8,128)(2,1)S(1)}, u32[]{:S(2)}, u32[]{:S(2)}) collective-permute-start(bf16[64,640]{1,0:T(8,128)(2,1)S(1)} %maximum_bitcast_fusion.1), channel_id=1, source_target_pairs={{1,2},{3,4},{5,6},{7,0},{2,1},{4,3},{6,5},{0,7},{9,10},{11,12},{13... | collective-permute-start | bytes 245768 | tf_op jit(solution)/shard_map/ppermute | solution.py:473
  39.6 7.6 %inner.1 = (bf16[960,256]{1,0:T(8,128)(2,1)}, bf16[8,64,640]{2,1,0:T(8,128)(2,1)}, bf16[12,16,640]{2,1,0:T(8,128)(2,1)}, bf16[16,16,640]{2,1,0:T(8,128)(2,1)}, bf16[24,64,640]{2,1,0:T(8,128)(2,1)}) custom-call(bf16[24,64,640]{2,1,0:T(8,128)(2,1)} %x_ref.3, f32[5,24,128]{2,1,0:T(8,128)} %get-tuple-element.19.lines_ref, f32[5,640]{1,0:T(8,128)} %one_ref.3, ...), custom_call_target="tpu_custom_call" | custom-call | flops 2831155200 | bytes 3932160 | tf_op jit(solution)/shard_map/inner/pallas_call | solution.py:447
  47.2 0.0 copy-done
  47.2 0.0 copy-done.1
  47.2 0.0 collective-permute-done.2.lon_a
  47.3 0.0 copy-start.2
  47.3 0.0 collective-permute-done.3.lon_b
  47.3 0.0 copy-start.3
  47.3 0.0 collective-permute-done.4.corner_a
  47.3 0.0 copy-start.4
  47.3 0.0 collective-permute-done.5.corner_b
  47.3 0.0 copy-start.5
  47.3 0.6 %copy-done.2 = bf16[192,640]{1,0:T(8,128)(2,1)} copy-done((bf16[192,640]{1,0:T(8,128)(2,1)}, bf16[192,640]{1,0:T(8,128)(2,1)S(1)}, u32[]{:S(2)}) %copy-start.2) | copy-done | bytes 245784
  48.0 0.1 copy-done.3
  48.0 0.0 copy-done.4
  48.1 0.0 copy-done.5
  48.1 8.2 %rim.1 = bf16[24,64,640]{2,1,0:T(8,128)(2,1)} custom-call(s32[3]{0:T(128)} %pad_add_fusion.place_ref, bf16[24,64,640]{2,1,0:T(8,128)(2,1)} %x_ref.3, bf16[272,640]{1,0:T(8,128)(2,1)} %bitcast.20, bf16[272,640]{1,0:T(8,128)(2,1)} %bitcast.21, bf16[192,640]{1,0:T(8,128)(2,1)} %copy-done.2, ...), custom_call_target="tpu_custom_call", output_to_operand_aliasing={{}: (15, {})} | custom-call | flops 2831155200 | bytes 3932160 | tf_op jit(solution)/shard_map/rim/pallas_call | solution.py:477
  (6 shorter events, 0.1 us)
Async XLA Ops:
  23.5 10.2 %collective-permute-start = (bf16[17,16,640]{2,1,0:T(8,128)(2,1)}, bf16[17,16,640]{2,1,0:T(8,128)(2,1)S(1)}, u32[]{:S(2)}, u32[]{:S(2)}) collective-permute-start(bf16[17,16,640]{2,1,0:T(8,128)(2,1)} %get-tuple-element.15), channel_id=1, source_target_pairs={{0,8},{16,24},{8,0},{24,16},{1,9},{17,25},{9,1},{25,17},{2,10},{18... | collective-permute-start | bytes 1044488 | tf_op jit(solution)/shard_map/ppermute | solution.py:439
  25.1 11.7 %collective-permute-start.1 = (bf16[17,16,640]{2,1,0:T(8,128)(2,1)}, bf16[17,16,640]{2,1,0:T(8,128)(2,1)S(1)}, u32[]{:S(2)}, u32[]{:S(2)}) collective-permute-start(bf16[17,16,640]{2,1,0:T(8,128)(2,1)} %get-tuple-element.16), channel_id=1, source_target_pairs={{8,16},{16,8},{9,17},{17,9},{10,18},{18,10},{11,19},{19,11},{12,20... | collective-permute-start | bytes 1044488 | tf_op jit(solution)/shard_map/ppermute | solution.py:440
  27.0 20.2 %collective-permute-start.2 = (bf16[192,640]{1,0:T(8,128)(2,1)}, bf16[192,640]{1,0:T(8,128)(2,1)S(1)}, u32[]{:S(2)}, u32[]{:S(2)}) collective-permute-start(bf16[192,640]{1,0:T(8,128)(2,1)} %get-tuple-element.17), channel_id=1, source_target_pairs={{0,1},{2,3},{4,5},{6,7},{1,0},{3,2},{5,4},{7,6},{8,9},{10,11},{12,... | collective-permute-start | bytes 737288 | tf_op jit(solution)/shard_map/ppermute | solution.py:442
  27.1 20.2 %collective-permute-start.3 = (bf16[192,640]{1,0:T(8,128)(2,1)}, bf16[192,640]{1,0:T(8,128)(2,1)S(1)}, u32[]{:S(2)}, u32[]{:S(2)}) collective-permute-start(bf16[192,640]{1,0:T(8,128)(2,1)} %get-tuple-element.18), channel_id=1, source_target_pairs={{1,2},{3,4},{5,6},{7,0},{2,1},{4,3},{6,5},{0,7},{9,10},{11,12},{13... | collective-permute-start | bytes 737288 | tf_op jit(solution)/shard_map/ppermute | solution.py:441
  33.6 13.6 %copy-start = (bf16[17,16,640]{2,1,0:T(8,128)(2,1)}, bf16[17,16,640]{2,1,0:T(8,128)(2,1)S(1)}, u32[]{:S(2)}) copy-start(bf16[17,16,640]{2,1,0:T(8,128)(2,1)S(1)} %collective-permute-done) | copy-start | bytes 1044484
  36.8 10.4 %copy-start.1 = (bf16[17,16,640]{2,1,0:T(8,128)(2,1)}, bf16[17,16,640]{2,1,0:T(8,128)(2,1)S(1)}, u32[]{:S(2)}) copy-start(bf16[17,16,640]{2,1,0:T(8,128)(2,1)S(1)} %collective-permute-done.1) | copy-start | bytes 1044484
  36.9 10.4 %collective-permute-start.4 = (bf16[64,640]{1,0:T(8,128)(2,1)S(1)}, bf16[64,640]{1,0:T(8,128)(2,1)S(1)}, u32[]{:S(2)}, u32[]{:S(2)}) collective-permute-start(bf16[64,640]{1,0:T(8,128)(2,1)S(1)} %maximum_bitcast_fusion), channel_id=1, source_target_pairs={{0,1},{2,3},{4,5},{6,7},{1,0},{3,2},{5,4},{7,6},{8,9},{10,11},{12,... | collective-permute-start | bytes 245768 | tf_op jit(solution)/shard_map/ppermute | solution.py:473
  37.0 10.3 %collective-permute-start.5 = (bf16[64,640]{1,0:T(8,128)(2,1)S(1)}, bf16[64,640]{1,0:T(8,128)(2,1)S(1)}, u32[]{:S(2)}, u32[]{:S(2)}) collective-permute-start(bf16[64,640]{1,0:T(8,128)(2,1)S(1)} %maximum_bitcast_fusion.1), channel_id=1, source_target_pairs={{1,2},{3,4},{5,6},{7,0},{2,1},{4,3},{6,5},{0,7},{9,10},{11,12},{13... | collective-permute-start | bytes 245768 | tf_op jit(solution)/shard_map/ppermute | solution.py:473
  47.3 0.7 %copy-start.2 = (bf16[192,640]{1,0:T(8,128)(2,1)}, bf16[192,640]{1,0:T(8,128)(2,1)S(1)}, u32[]{:S(2)}) copy-start(bf16[192,640]{1,0:T(8,128)(2,1)S(1)} %collective-permute-done.2.lon_a) | copy-start | bytes 737284
  47.3 0.8 %copy-start.3 = (bf16[192,640]{1,0:T(8,128)(2,1)}, bf16[192,640]{1,0:T(8,128)(2,1)S(1)}, u32[]{:S(2)}) copy-start(bf16[192,640]{1,0:T(8,128)(2,1)S(1)} %collective-permute-done.3.lon_b) | copy-start | bytes 737284
  47.3 0.8 %copy-start.4 = (bf16[64,640]{1,0:T(8,128)(2,1)}, bf16[64,640]{1,0:T(8,128)(2,1)S(1)}, u32[]{:S(2)}) copy-start(bf16[64,640]{1,0:T(8,128)(2,1)S(1)} %collective-permute-done.4.corner_a) | copy-start | bytes 245764
  47.3 0.8 %copy-start.5 = (bf16[64,640]{1,0:T(8,128)(2,1)}, bf16[64,640]{1,0:T(8,128)(2,1)S(1)}, u32[]{:S(2)}) copy-start(bf16[64,640]{1,0:T(8,128)(2,1)S(1)} %collective-permute-done.5.corner_b) | copy-start | bytes 245764

commit v4 on v3

v4 whole, which is shorter than its diff:
```python
import functools

import jax
import jax.numpy as jnp
from jax import lax
from jax.experimental import pallas as pl
from jax.experimental.pallas import tpu as pltpu
from jax.sharding import PartitionSpec as P

LAT_REACH = 2
LON_REACH = 4
REACH = 2 * LAT_REACH
BANDS = 2 * LAT_REACH + 1
CELLS = 8
WINDOW = CELLS + 2 * LON_REACH
LANES = 128
DEPTH = 2 * LANES
TILE = 16
VMEM_BYTES = 24 * 1024 * 1024
PIECE = 4
F32, BF16 = jnp.float32, jnp.bfloat16

ERF_SERIES = (
    1.5956562720156744,
    0.2917503271976864,
    -0.003995570947534282,
    -0.003914369984884403,
    0.0005729703632347449,
)


def erf_gelu(half):
    square = half * half
    series = ERF_SERIES[-1] * square + ERF_SERIES[-2]
    for term in ERF_SERIES[-3::-1]:
        series = series * square + term
    return half + half * jnp.tanh(half * series)


def swaps(peers, second, wrap):
    pairs = [(i, i + 1) for i in range(1 if second else 0, peers - 1, 2)]
    if second and wrap:
        pairs.append((peers - 1, 0))
    return pairs + [(j, i) for i, j in pairs]


def pairs_of(items):
    return [items[i : i + 2] for i in range(0, len(items), 2)]


def lanes_of(chunk):
    return slice(chunk * LANES, (chunk + 1) * LANES)


def fill_toeplitz(toeplitz, line_of, rows, bases, place_of):
    group = bases * CELLS
    blank = jnp.zeros((CELLS, DEPTH - LANES), F32)
    for row in range(0, rows, 2):
        parts = []
        for r in (row, row + 1):
            for basis in range(bases):
                line = jnp.broadcast_to(line_of(r, basis), (CELLS, LANES))
                line = jnp.concatenate([line, blank], 1)
                parts.append(pltpu.roll(line, place_of(r) * WINDOW, 1, stride=1, stride_axis=0))
        toeplitz[row * group : (row + 2) * group, :] = jnp.concatenate(parts, 0).astype(BF16)


def lane_weights(ref, scale=1.0):
    bases, channels = ref.shape
    return [[ref[k : k + 1, lanes_of(c)] * scale for k in range(bases)] for c in range(channels // LANES)]


def product(matrix, low, high, windows, weights):
    wide = [w.astype(BF16).reshape(DEPTH, LANES) for w in windows]
    wide = jnp.concatenate(wide, 1)
    bases = len(weights[0])
    group = bases * CELLS
    scales = [jnp.concatenate([w[k] for w in weights], 1) for k in range(bases)]
    pieces = []
    for at in range(low, high, PIECE):
        to = min(at + PIECE, high)
        result = jnp.dot(matrix[at * group : to * group, :], wide, preferred_element_type=F32)
        result = result.reshape(to - at, bases, CELLS, len(windows) * LANES)
        total = result[:, 0] * scales[0]
        for k in range(1, bases):
            total = total + result[:, k] * scales[k]
        pieces.append(total)
    total = jnp.concatenate(pieces, 0) if len(pieces) > 1 else pieces[0]
    return [total[:, :, i * LANES : (i + 1) * LANES] for i in range(len(windows))]


def run_mixed(steps):
    waiting = []
    for first, second in steps:
        share = -(-len(waiting) // max(len(first), 1))
        for unit in first:
            unit()
            for _ in range(min(share, len(waiting))):
                waiting.pop(0)()
        for unit in waiting:
            unit()
        waiting = list(second)
    for unit in waiting:
        unit()


def prep_kernel(
    rows_ref, tiles_ref, filter_in, edge_in, mask_in,
    lat_a, lat_b, lon_a, lon_b, lines, filter_ref, edge_ref, mask_ref, sides, padded, tags, sems,
):
    bases, lags, bands, rows = filter_in.shape
    groups = lat_a.shape[0] - 1
    lat = lax.axis_index("lat")
    lat_odd, lon_odd = lat % 2, lax.axis_index("lon") % 2
    start_a = (1 - lat_odd) * (rows_ref.shape[0] - groups)
    start_b = lat_odd * (rows_ref.shape[0] - groups)
    small = [
        pltpu.make_async_copy(filter_in, filter_ref, sems.at[4]),
        pltpu.make_async_copy(edge_in, edge_ref, sems.at[5]),
        pltpu.make_async_copy(mask_in, mask_ref, sems.at[6]),
    ]
    copies = [
        pltpu.make_async_copy(tiles_ref.at[:, 0], sides.at[0], sems.at[0]),
        pltpu.make_async_copy(tiles_ref.at[:, tiles_ref.shape[1] - 1], sides.at[1], sems.at[1]),
        pltpu.make_async_copy(rows_ref.at[pl.ds(start_a, groups)], lat_a.at[pl.ds(0, groups)], sems.at[2]),
        pltpu.make_async_copy(rows_ref.at[pl.ds(start_b, groups)], lat_b.at[pl.ds(0, groups)], sems.at[3]),
    ]
    for copy in small + copies:
        copy.start()
    padded[...] = jnp.zeros_like(padded)
    tags[...] = jnp.zeros_like(tags)
    at = lax.broadcasted_iota(jnp.int32, (LANES, LANES), 0)
    lane = lax.broadcasted_iota(jnp.int32, (LANES, LANES), 1)
    chosen = (at // 8 == lane % WINDOW) & (at % 8 == lane // WINDOW) & (at % 8 < bands) & (at // 8 < lags)
    chosen = jnp.where(chosen, 1.0, 0.0).astype(BF16)
    for copy in small:
        copy.wait()

    source = lat * rows + lax.broadcasted_iota(jnp.int32, (bands, rows), 1) - LAT_REACH
    source = source + lax.broadcasted_iota(jnp.int32, (bands, rows), 0)
    inside = (source >= edge_ref[0:1, :]) & (source < edge_ref[1:2, :])
    for k in range(bases):
        keep = inside & (mask_ref[k : k + 1, :] != 0)
        for m in range(lags):
            padded[k, m * 8 : m * 8 + bands, :rows] = jnp.where(keep, filter_ref[k, m], 0.0)
    for k in range(bases):
        line = jnp.dot(padded[k].T.astype(BF16), chosen, preferred_element_type=F32)
        lines[k] = line[:rows]
        span = slice(k * LAT_REACH, (k + 1) * LAT_REACH)
        tags[0, span] = line[:LAT_REACH]
        tags[1, span] = line[rows - LAT_REACH : rows]
    blank = jnp.zeros((TILE, lat_a.shape[2] - LANES), F32)
    first = jnp.concatenate([tags[0], blank], 1)
    last = jnp.concatenate([tags[1], blank], 1)
    lat_a[groups] = jnp.where(lat_odd == 1, first, last).astype(BF16)
    lat_b[groups] = jnp.where(lat_odd == 1, last, first).astype(BF16)
    copies[0].wait()
    copies[1].wait()
    leading = sides[0].astype(F32)[:, :CELLS]
    trailing = sides[1].astype(F32)[:, TILE - CELLS :]
    odd = lon_odd == 1
    lon_a[...] = jnp.where(odd, leading, trailing).reshape(lon_a.shape).astype(BF16)
    lon_b[...] = jnp.where(odd, trailing, leading).reshape(lon_b.shape).astype(BF16)
    for copy in copies[2:]:
        copy.wait()


def inner_kernel(
    block, x_ref, lines_ref, one_ref, two_ref, toeplitz, edge_rows, edge_cells, sides, middle, field, hidden, ends
):
    rows, cells, channels = x_ref.shape
    bases = one_ref.shape[0]
    chunks = channels // LANES
    fill_toeplitz(toeplitz, lambda r, k: lines_ref[k, r : r + 1, :], rows, bases, lambda r: r % block)
    one, two = lane_weights(one_ref, 0.5), lane_weights(two_ref)
    starts = range(0, rows, block)
    windows = (cells - WINDOW) // CELLS + 1
    span = windows * CELLS

    def load(c):
        blank = jnp.zeros((LAT_REACH, cells, LANES), F32)
        field[c, :LAT_REACH] = blank
        field[c, LAT_REACH : LAT_REACH + rows] = x_ref[:, :, lanes_of(c)].astype(F32)
        field[c, LAT_REACH + rows :] = blank
        blank = jnp.zeros((REACH, span, LANES), F32)
        hidden[c, :REACH] = blank
        hidden[c, rows:] = blank

    def first(items, start):
        low, high = max(start, LAT_REACH), min(start + block, rows - LAT_REACH)
        tall = [field[c, start : start + block + REACH, w * CELLS : w * CELLS + WINDOW] for c, w in items]
        values = product(toeplitz, low, high, tall, [one[c] for c, w in items])
        for (c, w), value in zip(items, values):
            hidden[c, low + LAT_REACH : high + LAT_REACH, w * CELLS : (w + 1) * CELLS] = erf_gelu(value)

    def second(c, start, pair):
        low, high = max(start, REACH), min(start + block, rows - REACH)
        tall = [hidden[c, start : start + block + REACH, w * CELLS : w * CELLS + WINDOW] for w in pair]
        values = product(toeplitz, low, high, tall, [two[c]] * len(pair))
        at = slice(low - REACH, high - REACH)
        for w, value in zip(pair, values):
            if w in (0, windows - 2):
                ends[c, at, (w > 0) * CELLS : (w > 0) * CELLS + CELLS] = value
        if len(pair) == 2 and pair[0] > 0:
            span = slice((pair[0] - 1) * CELLS, (pair[0] + 1) * CELLS)
            middle[at, span, lanes_of(c)] = jnp.concatenate(values, 1).astype(BF16)

    def export(c):
        for i, row in enumerate((REACH, rows - REACH)):
            part = jnp.concatenate([hidden[c, row : row + REACH], jnp.zeros((REACH, cells - span, LANES), F32)], 1)
            edge_rows[i * REACH : (i + 1) * REACH, :, lanes_of(c)] = part.astype(BF16)
        part = hidden[c, 2 * REACH : rows - REACH]
        edge_cells[:, :, lanes_of(c)] = jnp.concatenate([part[:, :CELLS], part[:, span - CELLS :]], 1).astype(BF16)
        sides[:, :, lanes_of(c)] = ends[c].astype(BF16)

    part = functools.partial
    steps = [([part(load, c)], []) for c in range(chunks)]
    for items in pairs_of([(c, w) for c in range(chunks) for w in range(windows)]):
        steps[items[-1][0]][0].extend(part(first, items, start) for start in starts)
    for c in range(chunks):
        pairs = [[0, windows - 2]] + pairs_of(list(range(1, windows - 2)))
        steps[c][1].extend(part(second, c, start, pair) for start in starts for pair in pairs)
        steps[c][1].append(part(export, c))
    for c in range(chunks - 1, 0, -1):
        if c * windows % 2:
            straddle = steps[c][0][1 : 1 + len(starts)]
            steps[c][0][1 : 1 + len(starts)] = []
            steps[c - 1][0].extend([steps[c][0].pop(0)] + straddle)
    run_mixed(steps)


def ordered(odd, a, b):
    a, b = a.astype(F32), b.astype(F32)
    return jnp.where(odd, a, b), jnp.where(odd, b, a)


def parities():
    return lax.axis_index("lat") % 2 == 1, lax.axis_index("lon") % 2 == 1


def rim_kernel(
    block, x_ref, lat_a, lat_b, lon_a, lon_b, rows_in, cells_in, sides_in, toeplitz, lines_ref, one_ref, two_ref,
    rim_toeplitz, wide_toeplitz, rim_out, side_out, ends, field, hidden,
):
    rows, cells, channels = x_ref.shape
    bases = one_ref.shape[0]
    chunks = channels // LANES
    edge = REACH * cells
    columns = cells // CELLS + 1
    lat_odd, lon_odd = parities()
    one, two = lane_weights(one_ref, 0.5), lane_weights(two_ref)
    kept = list(range(REACH)) + list(range(rows - REACH, rows))

    def place_of(r):
        return r if r < REACH else REACH + r

    tags = ordered(lat_odd, lat_a[edge:, :LANES], lat_b[edge:, :LANES])

    def rim_line(r, k):
        if r < LAT_REACH:
            return tags[0][k * LAT_REACH + r : k * LAT_REACH + r + 1, :]
        if r >= 2 * REACH - LAT_REACH:
            at = k * LAT_REACH + r - (2 * REACH - LAT_REACH)
            return tags[1][at : at + 1, :]
        at = r - LAT_REACH if r < REACH else rows - LAT_REACH + r - REACH
        return lines_ref[k, at : at + 1, :]

    fill_toeplitz(rim_toeplitz, rim_line, 2 * REACH, bases, place_of)
    fill_toeplitz(wide_toeplitz, lambda r, k: lines_ref[k, kept[r] : kept[r] + 1, :], 2 * REACH, bases, place_of)

    def load(c):
        lanes = lanes_of(c)
        lat = ordered(lat_odd, lat_a[:edge, lanes], lat_b[:edge, lanes])
        lon = ordered(lon_odd, lon_a[:, lanes], lon_b[:, lanes])
        inner = slice(REACH, rows - REACH)
        blank = jnp.zeros((REACH, CELLS, LANES), F32)
        for side in range(2):
            at = slice(side * (rows + REACH), side * (rows + REACH) + REACH)
            field[c, at, CELLS : CELLS + cells] = lat[side].reshape(REACH, cells, LANES)
            own = slice(side * (rows - REACH), side * (rows - REACH) + REACH)
            at = slice(own.start + REACH, own.stop + REACH)
            field[c, at, CELLS : CELLS + cells] = x_ref[own, :, lanes].astype(F32)
            own = slice(side * (cells - TILE), side * (cells - TILE) + TILE)
            at = slice(own.start + CELLS, own.stop + CELLS)
            field[c, 2 * REACH : rows, at] = x_ref[inner, own, lanes].astype(F32)
            span = slice(side * (CELLS + cells), side * (CELLS + cells) + CELLS)
            field[c, REACH : REACH + rows, span] = lon[side].reshape(rows, CELLS, LANES)
            for end in range(2):
                at = slice(end * (rows + REACH), end * (rows + REACH) + REACH)
                field[c, at, span] = blank
                hidden[c, end * rows : end * rows + REACH, side * cells : side * cells + CELLS] = blank
        span = cells - CELLS
        for i, at in enumerate((REACH, rows - REACH)):
            part = rows_in[i * REACH : (i + 1) * REACH, :, lanes].astype(F32)
            hidden[c, at : at + REACH, CELLS : CELLS + span] = part[:, :span]
        part = cells_in[:, :, lanes].astype(F32)
        at = slice(2 * REACH, rows - REACH)
        hidden[c, at, CELLS : 2 * CELLS] = part[:, :CELLS]
        hidden[c, at, cells - CELLS : cells] = part[:, CELLS:]

    def rims(ref, c, span):
        last = ref.shape[1] - 2 * REACH
        return jnp.concatenate([ref[c, : 2 * REACH, span], ref[c, last:, span]], 0)

    def first_rows(items):
        tall = [rims(field, c, slice(w * CELLS, w * CELLS + WINDOW)) for c, w in items]
        values = product(rim_toeplitz, 0, 2 * REACH, tall, [one[c] for c, w in items])
        for (c, w), value in zip(items, values):
            value = erf_gelu(value)
            hidden[c, :REACH, w * CELLS : (w + 1) * CELLS] = value[:REACH]
            hidden[c, rows:, w * CELLS : (w + 1) * CELLS] = value[REACH:]

    def first_sides(c, start):
        low, high = max(start, LAT_REACH), min(start + block, rows - LAT_REACH)
        at = slice(start + LAT_REACH, start + LAT_REACH + block + REACH)
        tall = [field[c, at, s : s + WINDOW] for s in (0, cells)]
        values = product(toeplitz, low, high, tall, [one[c]] * 2)
        for s, value in zip((0, cells), values):
            hidden[c, low + LAT_REACH : high + LAT_REACH, s : s + CELLS] = erf_gelu(value)

    def second_rows(c, pair):
        tall = [rims(hidden, c, slice(w * CELLS, w * CELLS + WINDOW)) for w in pair]
        values = product(wide_toeplitz, 0, 2 * REACH, tall, [two[c]] * 2)
        blank = jnp.zeros((2 * REACH, CELLS, LANES), F32)
        if pair == [1, columns - 3]:
            rim_out[:, :TILE, lanes_of(c)] = jnp.concatenate([blank, values[0]], 1).astype(BF16)
            rim_out[:, cells - TILE :, lanes_of(c)] = jnp.concatenate([values[1], blank], 1).astype(BF16)
        else:
            rim_out[:, pair[0] * CELLS : (pair[0] + 2) * CELLS, lanes_of(c)] = jnp.concatenate(values, 1).astype(BF16)

    def second_sides(c, start):
        low, high = max(start, REACH), min(start + block, rows - REACH)
        tall = [hidden[c, start : start + block + REACH, s : s + WINDOW] for s in (0, cells - CELLS)]
        values = product(toeplitz, low, high, tall, [two[c]] * 2)
        at = slice(low - REACH, high - REACH)
        inner = sides_in[at, :, lanes_of(c)].astype(F32)
        side_out[0, at, :, lanes_of(c)] = jnp.concatenate([values[0], inner[:, :CELLS]], 1).astype(BF16)
        side_out[1, at, :, lanes_of(c)] = jnp.concatenate([inner[:, CELLS:], values[1]], 1).astype(BF16)

    def export(c):
        for side in range(2):
            span = slice(side * (cells - CELLS), side * (cells - CELLS) + WINDOW)
            ends[side, :, :, lanes_of(c)] = rims(hidden, c, span).astype(BF16)

    part = functools.partial
    steps = [([part(load, c)], []) for c in range(chunks)]
    items = [(c, w) for c in range(chunks) for w in range(1, columns - 1)]
    for pair in pairs_of(items):
        steps[pair[-1][0]][0].append(part(first_rows, pair))
    for c in range(chunks - 1, 0, -1):
        if c * (columns - 2) % 2:
            steps[c - 1][0].extend([steps[c][0].pop(0), steps[c][0].pop(0)])
    starts = range(0, rows, block)
    for c, (first, second) in enumerate(steps):
        first.extend(part(first_sides, c, start) for start in starts)
        second.extend(
            part(second_rows, c, pair) for pair in [[1, columns - 3]] + pairs_of(list(range(2, columns - 3)))
        )
        second.extend(part(second_sides, c, start) for start in starts)
        second.append(part(export, c))
    run_mixed(steps)


def corner_kernel(
    x_ref, lat_a, lat_b, lon_a, lon_b, corner_a, corner_b, ends, rim_toeplitz, wide_toeplitz, one_ref, two_ref,
    middle, side_out, rim_out, out_ref, corner_out, sems,
):
    rows, cells, channels = x_ref.shape
    chunks = channels // LANES
    edge = REACH * cells
    inner = pl.ds(REACH, rows - 2 * REACH)
    ends_at = (pl.ds(0, REACH), pl.ds(rows - REACH, REACH))
    sides_at = (pl.ds(0, TILE), pl.ds(cells - TILE, TILE))
    span = pl.ds(TILE, cells - 2 * TILE)
    moves = [(middle, out_ref.at[inner, span])]
    for i in range(2):
        moves.append((side_out.at[i], out_ref.at[inner, sides_at[i]]))
        moves.append((rim_out.at[pl.ds(i * REACH, REACH), span], out_ref.at[ends_at[i], span]))
    copies = [pltpu.make_async_copy(source, target, sems.at[i]) for i, (source, target) in enumerate(moves)]
    for copy in copies:
        copy.start()
    lat_odd, lon_odd = parities()
    one, two = lane_weights(one_ref, 0.5), lane_weights(two_ref)

    def first(c):
        lanes = lanes_of(c)
        lat = ordered(lat_odd, lat_a[:edge, lanes], lat_b[:edge, lanes])
        lon = ordered(lon_odd, lon_a[:, lanes], lon_b[:, lanes])
        corner = ordered(lon_odd, corner_a[:, lanes], corner_b[:, lanes])
        tall = []
        for side in range(2):
            own = slice(side * (cells - CELLS), side * (cells - CELLS) + CELLS)
            above = [v.reshape(REACH, cells, LANES)[:, own] for v in lat]
            tiles = slice(side * (cells - TILE), side * (cells - TILE) + TILE)
            half = slice(side * (TILE - CELLS), side * (TILE - CELLS) + CELLS)
            mine = [x_ref[r : r + REACH, tiles, lanes].astype(F32)[:, half] for r in (0, rows - REACH)]
            near = lon[side].reshape(rows, CELLS, LANES)
            far = ordered(lat_odd, corner[side][: REACH * CELLS], corner[side][REACH * CELLS :])
            far = [v.reshape(REACH, CELLS, LANES) for v in far]
            own = jnp.concatenate([above[0], mine[0], mine[1], above[1]], 0)
            other = jnp.concatenate([far[0], near[:REACH], near[rows - REACH :], far[1]], 0)
            tall.append(jnp.concatenate([own, other] if side else [other, own], 1))
        return [erf_gelu(v) for v in product(rim_toeplitz, 0, 2 * REACH, tall, [one[c]] * 2)]

    def second(c, blocks):
        lanes = lanes_of(c)
        tall = []
        for side in range(2):
            near = ends[side, :, :, lanes].astype(F32)
            own = near[:, side * CELLS : side * CELLS + CELLS]
            own = jnp.concatenate([blocks[side][:REACH], own[REACH : 3 * REACH], blocks[side][REACH:]], 0)
            tall.append(jnp.concatenate([near[:, :CELLS], own] if side else [own, near[:, CELLS:]], 1))
        values = product(wide_toeplitz, 0, 2 * REACH, tall, [two[c]] * 2)
        for side in range(2):
            tiles = slice(side * (cells - TILE), side * (cells - TILE) + TILE)
            near = rim_out[:, tiles, lanes].astype(F32)
            near = near[:, : TILE - CELLS] if side else near[:, CELLS:]
            whole = [near, values[side]] if side else [values[side], near]
            corner_out[side, :, :, lanes] = jnp.concatenate(whole, 1).astype(BF16)

    hidden = [first(c) for c in range(chunks)]
    for c in range(chunks):
        second(c, hidden[c])
    last = []
    for side in range(2):
        for end in range(2):
            source = corner_out.at[side, pl.ds(end * REACH, REACH)]
            target = out_ref.at[ends_at[end], sides_at[side]]
            last.append(pltpu.make_async_copy(source, target, sems.at[len(copies) + len(last)]))
            last[-1].start()
    for copy in copies + last:
        copy.wait()


def per_device(state_field, filters, band_edges, basis_mask, weights_one, weights_two):
    rows, cells, channels = state_field.shape
    bases = filters.shape[1]
    group = bases * CELLS
    chunks = channels // LANES
    tiles = cells // TILE
    edge = REACH * cells
    block = max(b for b in range(2, rows + 1, 2) if rows % b == 0 and (b + REACH) * WINDOW <= DEPTH)
    lat_peers, lon_peers = lax.axis_size("lat"), lax.axis_size("lon")
    lon = lax.axis_index("lon")

    anywhere = pl.BlockSpec(memory_space=pl.ANY)
    vmem = pl.BlockSpec(memory_space=pltpu.VMEM)
    params = pltpu.CompilerParams(vmem_limit_bytes=VMEM_BYTES)
    dma = pltpu.SemaphoreType.DMA

    def array(*shape, dtype=BF16):
        return jax.ShapeDtypeStruct(shape, dtype)

    def scratch(*shape, dtype=BF16):
        return pltpu.VMEM(shape, dtype)

    groups = REACH * tiles
    lat_a, lat_b, lon_a, lon_b, lines = pl.pallas_call(
        prep_kernel,
        out_shape=(
            array(groups + 1, TILE, channels), array(groups + 1, TILE, channels),
            array(rows * CELLS, channels), array(rows * CELLS, channels),
            array(bases, rows, LANES, dtype=F32),
        ),
        in_specs=[anywhere] * 5,
        out_specs=(vmem,) * 5,
        scratch_shapes=[
            scratch(bases, filters.shape[3], BANDS, rows, dtype=F32),
            scratch(2, rows, dtype=jnp.int32), scratch(bases, rows, dtype=jnp.int32),
            scratch(2, rows, TILE, channels), scratch(bases, LANES, LANES, dtype=F32),
            scratch(2, TILE, LANES, dtype=F32), dma((7,)),
        ],
        compiler_params=pltpu.CompilerParams(vmem_limit_bytes=60 * 1024 * 1024),
        cost_estimate=pl.CostEstimate(flops=0, bytes_accessed=4 * edge * channels, transcendentals=0),
        name="prep",
    )(
        state_field.reshape(rows * tiles, TILE, channels), state_field.reshape(rows, tiles, TILE, channels),
        filters.transpose(1, 3, 2, 0), band_edges.T, basis_mask.T,
    )
    lat_a = lax.ppermute(lat_a, "lat", swaps(lat_peers, False, False)).reshape(edge + TILE, channels)
    lat_b = lax.ppermute(lat_b, "lat", swaps(lat_peers, True, False)).reshape(edge + TILE, channels)
    lon_b = lax.ppermute(lon_b, "lon", swaps(lon_peers, True, True))
    lon_a = lax.ppermute(lon_a, "lon", swaps(lon_peers, False, True))

    middle = rows - 2 * REACH
    flops = 2 * (2 * rows - 3 * REACH) * (cells - 2 * CELLS) * bases * DEPTH * channels
    cost = pl.CostEstimate(flops=flops, bytes_accessed=4 * state_field.size, transcendentals=0)
    toeplitz, edge_rows, edge_cells, sides, inner = pl.pallas_call(
        functools.partial(inner_kernel, block),
        out_shape=(
            array(rows * group, DEPTH), array(2 * REACH, cells, channels), array(middle - REACH, TILE, channels),
            array(middle, TILE, channels), array(middle, cells - 2 * TILE, channels),
        ),
        in_specs=[vmem] * 4,
        out_specs=(vmem,) * 5,
        scratch_shapes=[
            scratch(chunks, rows + REACH, cells, LANES, dtype=F32),
            scratch(chunks, rows + REACH, cells - CELLS, LANES, dtype=F32),
            scratch(chunks, middle, TILE, LANES, dtype=F32),
        ],
        compiler_params=params,
        cost_estimate=cost,
        name="inner",
    )(state_field, lines, weights_one, weights_two)

    def corner_send(leading, second):
        start = jnp.where(leading, 0, cells - CELLS)
        joined = [v[:edge].reshape(REACH, cells, channels) for v in (lat_a, lat_b)]
        parts = [lax.dynamic_slice_in_dim(v, start, CELLS, 1) for v in joined]
        sent = jnp.concatenate(parts, 0).reshape(2 * REACH * CELLS, channels)
        return lax.ppermute(sent, "lon", swaps(lon_peers, second, True))

    lat_a, lat_b, inner = lax.optimization_barrier((lat_a, lat_b, inner))
    corner_b = corner_send(lon % 2 == 0, True)
    corner_a = corner_send(lon % 2 == 1, False)
    rim_toeplitz, wide_toeplitz, rim_out, side_out, ends = pl.pallas_call(
        functools.partial(rim_kernel, block),
        out_shape=(
            array(2 * REACH * group, DEPTH), array(2 * REACH * group, DEPTH), array(2 * REACH, cells, channels),
            array(2, middle, TILE, channels), array(2, 4 * REACH, WINDOW, channels),
        ),
        in_specs=[vmem] * 12,
        out_specs=(vmem,) * 5,
        scratch_shapes=[
            scratch(chunks, rows + 2 * REACH, cells + 2 * CELLS, LANES, dtype=F32),
            scratch(chunks, rows + REACH, cells + CELLS, LANES, dtype=F32),
        ],
        compiler_params=params,
        cost_estimate=cost,
        name="rim",
    )(
        state_field, lat_a, lat_b, lon_a, lon_b, edge_rows, edge_cells, sides, toeplitz, lines,
        weights_one, weights_two,
    )
    return pl.pallas_call(
        corner_kernel,
        out_shape=array(rows, cells, channels),
        in_specs=[vmem] * 15,
        out_specs=anywhere,
        scratch_shapes=[scratch(2, 2 * REACH, TILE, channels), dma((9,))],
        compiler_params=params,
        cost_estimate=cost,
        name="corner",
    )(
        state_field, lat_a, lat_b, lon_a, lon_b, corner_a, corner_b, ends, rim_toeplitz, wide_toeplitz,
        weights_one, weights_two, inner, side_out, rim_out,
    )


def solution(mesh):
    placed = (
        P("lat", "lon", None),
        P("lat", None, None, None),
        P("lat", None),
        P("lat", None),
        P(),
        P(),
    )
    return jax.shard_map(
        per_device, mesh=mesh, in_specs=placed, out_specs=P("lat", "lon", None), check_vma=False
    )
```

time: 56.6 us -> 24.2 us (0.43)
  Pallas kernels: 38.6 us -> 12 us
  waiting for transfers between devices: 7.11 us -> 2.06 us
  other arithmetic: 0.69 us -> 0.03 us
    pallas_call x1, Pallas kernels: 22.8 us -> 2.67 us  [per_device(): pl.pallas_call(prep_kernel, out_shape=(array(groups + 1, TILE, channels),...]
    ppermute x1, waiting for transfers between devices: 3.98 us -> 0.01 us  [per_device(): lax.ppermute(lat_a, 'lat', swaps(lat_peers, False, False))]
    pallas_call x1, Pallas kernels: 7.62 us -> 4.24 us  [per_device(): pl.pallas_call(functools.partial(inner_kernel, block), out_shape=(array(r...]
    pallas_call x1 -> x2, Pallas kernels: 8.19 us -> 5.11 us  [the longest x1 3.18 us: per_device(): pl.pallas_call(functools.partial(rim_kernel, block), out_shape=(array(2 *...]
    ppermute x1, waiting for transfers between devices: 3.12 us -> 2.05 us  [per_device(): lax.ppermute(lat_b, 'lat', swaps(lat_peers, True, False))]
    another operation x1 -> x0, other arithmetic: 0.66 us -> none  [per_device(): place = jnp.stack([lat % 2, lon % 2, lat * rows]).astype(jnp.int32)]
  transfers between devices with their start and end apart: 6 -> 6, of which waited for: 2 -> 1; matrix products, arithmetic and copies ran while one was open for 0% -> 0% of each run, Pallas kernels for 14% -> 31%
where the time goes in v4:
time: 24.2 us; the launch traced here: 24 us
  Pallas kernels  12 us (50%)
  starting transfers between devices  8.85 us (37%)
  waiting for transfers between devices  2.06 us (9%)
  local copies, waits for them, and re-layouts  0.93 us (4%)
    pallas_call x1, Pallas kernels, per_device(): pl.pallas_call(functools.partial(inner_kernel, block), out_shape=(array(r...  4.24 us
    pallas_call x1, Pallas kernels, per_device(): pl.pallas_call(functools.partial(rim_kernel, block), out_shape=(array(2 *...  3.18 us
    ppermute x2, starting transfers between devices, corner_send(): return lax.ppermute(sent, 'lon', swaps(lon_peers, second, True))  2.68 us
    pallas_call x1, Pallas kernels, per_device(): pl.pallas_call(prep_kernel, out_shape=(array(groups + 1, TILE, channels),...  2.67 us
    ppermute x1, starting transfers between devices, per_device(): lon_b = lax.ppermute(lon_b, 'lon', swaps(lon_peers, True, True))  2.55 us
    ppermute x1, waiting for transfers between devices, per_device(): lax.ppermute(lat_b, 'lat', swaps(lat_peers, True, False))  2.05 us
    pallas_call x1, Pallas kernels, per_device(): pl.pallas_call(corner_kernel, out_shape=array(rows, cells, channels), in_...  1.93 us
    ppermute x1, starting transfers between devices, per_device(): lax.ppermute(lat_b, 'lat', swaps(lat_peers, True, False))  1.91 us
  transfers between devices with their start and end apart: 6, of which 1 were waited for; matrix products, arithmetic and copies ran while one was open for 0% of the time, Pallas kernels for 31%

profile of v4, /device:TPU:16, one launch (start us, length us, event | category | flops | bytes accessed | tf_op | source)
XLA Modules:
  0.0 24.0 jit_solution(14859775393711862677)
XLA Ops:
  0.0 0.0 copy-start
  0.0 0.0 copy-start.3
  0.0 0.0 copy-start.4
  0.0 2.7 %prep.1 = (bf16[17,16,640]{2,1,0:T(8,128)(2,1)}, bf16[17,16,640]{2,1,0:T(8,128)(2,1)}, bf16[192,640]{1,0:T(8,128)(2,1)}, bf16[192,640]{1,0:T(8,128)(2,1)}, f32[5,24,128]{2,1,0:T(8,128)}) custom-call(bf16[96,16,640]{2,1,0:T(8,128)(2,1)} %bitcast.13, bf16[24,4,16,640]{3,2,1,0:T(8,128)(2,1)} %bitcast.14, f32[5,9,5,24]{3,2,1,0:T(8,128)} %bitcast.23, ...), custom_call_target="tpu_custom_call" | custom-call | bytes 655360 | tf_op jit(solution)/shard_map/prep/pallas_call | solution.py:458
  2.7 1.6 %collective-permute-start = (bf16[17,16,640]{2,1,0:T(8,128)(2,1)}, bf16[17,16,640]{2,1,0:T(8,128)(2,1)S(1)}, u32[]{:S(2)}, u32[]{:S(2)}) collective-permute-start(bf16[17,16,640]{2,1,0:T(8,128)(2,1)} %get-tuple-element.23), channel_id=1, source_target_pairs={{0,8},{16,24},{8,0},{24,16},{1,9},{17,25},{9,1},{25,17},{2,10},{18... | collective-permute-start | bytes 1044488 | tf_op jit(solution)/shard_map/ppermute | solution.py:480
  4.3 1.9 %collective-permute-start.1 = (bf16[17,16,640]{2,1,0:T(8,128)(2,1)}, bf16[17,16,640]{2,1,0:T(8,128)(2,1)S(1)}, u32[]{:S(2)}, u32[]{:S(2)}) collective-permute-start(bf16[17,16,640]{2,1,0:T(8,128)(2,1)} %get-tuple-element.24), channel_id=1, source_target_pairs={{8,16},{16,8},{9,17},{17,9},{10,18},{18,10},{11,19},{19,11},{12,20... | collective-permute-start | bytes 1044488 | tf_op jit(solution)/shard_map/ppermute | solution.py:481
  6.2 0.1 collective-permute-start.2
  6.3 2.5 %collective-permute-start.3 = (bf16[192,640]{1,0:T(8,128)(2,1)}, bf16[192,640]{1,0:T(8,128)(2,1)S(1)}, u32[]{:S(2)}, u32[]{:S(2)}) collective-permute-start(bf16[192,640]{1,0:T(8,128)(2,1)} %get-tuple-element.30), channel_id=1, source_target_pairs={{1,2},{3,4},{5,6},{7,0},{2,1},{4,3},{6,5},{0,7},{9,10},{11,12},{13... | collective-permute-start | bytes 737288 | tf_op jit(solution)/shard_map/ppermute | solution.py:482
  8.9 0.0 copy-done
  8.9 0.0 copy-done.3
  8.9 0.0 copy-done.4
  8.9 0.0 copy-start.1
  8.9 0.8 %copy-done.1 = f32[5,24,128]{2,1,0:T(8,128)S(1)} copy-done((f32[5,24,128]{2,1,0:T(8,128)S(1)}, f32[5,24,128]{2,1,0:T(8,128)}, u32[]{:S(2)}) %copy-start.1) | copy-done | bytes 61464
  9.7 4.2 %inner.1 = (bf16[960,256]{1,0:T(8,128)(2,1)S(1)}, bf16[8,64,640]{2,1,0:T(8,128)(2,1)S(1)}, bf16[12,16,640]{2,1,0:T(8,128)(2,1)S(1)}, bf16[16,16,640]{2,1,0:T(8,128)(2,1)S(1)}, bf16[16,32,640]{2,1,0:T(8,128)(2,1)S(1)}) custom-call(bf16[24,64,640]{2,1,0:T(8,128)(2,1)S(1)} %copy-done, f32[5,24,128]{2,1,0:T(8,128)S(1)} %copy-done.1, f32[5,640]{1,0:T(8,128)S(1)} %copy-done.3, ...), custom_call_target="tpu_custom_call" | custom-call | flops 2831155200 | bytes 3932160 | tf_op jit(solution)/shard_map/inner/pallas_call | solution.py:488
  14.0 0.0 copy-start.2
  14.0 0.0 collective-permute-done
  14.0 2.0 %collective-permute-done.1 = bf16[17,16,640]{2,1,0:T(8,128)(2,1)S(1)} collective-permute-done((bf16[17,16,640]{2,1,0:T(8,128)(2,1)}, bf16[17,16,640]{2,1,0:T(8,128)(2,1)S(1)}, u32[]{:S(2)}, u32[]{:S(2)}) %collective-permute-start.1) | collective-permute-done | bytes 348192 | tf_op jit(solution)/shard_map/ppermute | solution.py:481
  16.2 0.1 collective-permute-start.4
  16.3 2.6 %collective-permute-start.5 = (bf16[64,640]{1,0:T(8,128)(2,1)S(1)}, bf16[64,640]{1,0:T(8,128)(2,1)S(1)}, u32[]{:S(2)}, u32[]{:S(2)}) collective-permute-start(bf16[64,640]{1,0:T(8,128)(2,1)S(1)} %maximum_bitcast_fusion.1), channel_id=1, source_target_pairs={{1,2},{3,4},{5,6},{7,0},{2,1},{4,3},{6,5},{0,7},{9,10},{11,12},{13... | collective-permute-start | bytes 245768 | tf_op jit(solution)/shard_map/ppermute | solution.py:511
  18.9 0.0 collective-permute-done.2.lon_a
  18.9 0.0 collective-permute-done.3.lon_b
  18.9 0.0 copy-done.2
  18.9 3.2 %rim.1 = (bf16[320,256]{1,0:T(8,128)(2,1)S(1)}, bf16[320,256]{1,0:T(8,128)(2,1)S(1)}, bf16[8,64,640]{2,1,0:T(8,128)(2,1)S(1)}, bf16[2,16,16,640]{3,2,1,0:T(8,128)(2,1)S(1)}, bf16[2,16,16,640]{3,2,1,0:T(8,128)(2,1)S(1)}) custom-call(bf16[24,64,640]{2,1,0:T(8,128)(2,1)S(1)} %copy-done, bf16[272,640]{1,0:T(8,128)(2,1)S(1)} %bitcast.16, ...), custom_call_target="tpu_custom_call" | custom-call | flops 2831155200 | bytes 3932160 | tf_op jit(solution)/shard_map/rim/pallas_call | solution.py:516
  22.1 0.0 collective-permute-done.4.corner_a
  22.1 0.0 collective-permute-done.5.corner_b
  22.1 1.9 %corner.1 = bf16[24,64,640]{2,1,0:T(8,128)(2,1)} custom-call(bf16[24,64,640]{2,1,0:T(8,128)(2,1)S(1)} %copy-done, bf16[272,640]{1,0:T(8,128)(2,1)S(1)} %bitcast.17, bf16[272,640]{1,0:T(8,128)(2,1)S(1)} %bitcast.20, bf16[192,640]{1,0:T(8,128)(2,1)S(1)} %collective-permute-done.2.lon_a, bf16[192,640]{1,0:T(8,128)(2,1)S(1)} %collective-permute-done.3.lon_b, ...), custom_call_target="tpu_custom_call" | custom-call | flops 2831155200 | bytes 3932160 | tf_op jit(solution)/shard_map/corner/pallas_call | solution.py:535
  (5 shorter events, 0.1 us)
Async XLA Ops:
  0.0 8.9 %copy-start = (bf16[24,64,640]{2,1,0:T(8,128)(2,1)S(1)}, bf16[24,64,640]{2,1,0:T(8,128)(2,1)}, u32[]{:S(2)}) copy-start(bf16[24,64,640]{2,1,0:T(8,128)(2,1)} %x_ref.5) | copy-start | bytes 5898244
  0.0 8.9 %copy-start.3 = (f32[5,640]{1,0:T(8,128)S(1)}, f32[5,640]{1,0:T(8,128)}, u32[]{:S(2)}) copy-start(f32[5,640]{1,0:T(8,128)} %one_ref.5) | copy-start | bytes 38404
  0.0 8.9 %copy-start.4 = (f32[5,640]{1,0:T(8,128)S(1)}, f32[5,640]{1,0:T(8,128)}, u32[]{:S(2)}) copy-start(f32[5,640]{1,0:T(8,128)} %two_ref.5) | copy-start | bytes 38404
  2.7 11.3 %collective-permute-start = (bf16[17,16,640]{2,1,0:T(8,128)(2,1)}, bf16[17,16,640]{2,1,0:T(8,128)(2,1)S(1)}, u32[]{:S(2)}, u32[]{:S(2)}) collective-permute-start(bf16[17,16,640]{2,1,0:T(8,128)(2,1)} %get-tuple-element.23), channel_id=1, source_target_pairs={{0,8},{16,24},{8,0},{24,16},{1,9},{17,25},{9,1},{25,17},{2,10},{18... | collective-permute-start | bytes 1044488 | tf_op jit(solution)/shard_map/ppermute | solution.py:480
  4.3 11.7 %collective-permute-start.1 = (bf16[17,16,640]{2,1,0:T(8,128)(2,1)}, bf16[17,16,640]{2,1,0:T(8,128)(2,1)S(1)}, u32[]{:S(2)}, u32[]{:S(2)}) collective-permute-start(bf16[17,16,640]{2,1,0:T(8,128)(2,1)} %get-tuple-element.24), channel_id=1, source_target_pairs={{8,16},{16,8},{9,17},{17,9},{10,18},{18,10},{11,19},{19,11},{12,20... | collective-permute-start | bytes 1044488 | tf_op jit(solution)/shard_map/ppermute | solution.py:481
  6.2 12.6 %collective-permute-start.2 = (bf16[192,640]{1,0:T(8,128)(2,1)}, bf16[192,640]{1,0:T(8,128)(2,1)S(1)}, u32[]{:S(2)}, u32[]{:S(2)}) collective-permute-start(bf16[192,640]{1,0:T(8,128)(2,1)} %get-tuple-element.29), channel_id=1, source_target_pairs={{0,1},{2,3},{4,5},{6,7},{1,0},{3,2},{5,4},{7,6},{8,9},{10,11},{12,... | collective-permute-start | bytes 737288 | tf_op jit(solution)/shard_map/ppermute | solution.py:483
  6.3 12.6 %collective-permute-start.3 = (bf16[192,640]{1,0:T(8,128)(2,1)}, bf16[192,640]{1,0:T(8,128)(2,1)S(1)}, u32[]{:S(2)}, u32[]{:S(2)}) collective-permute-start(bf16[192,640]{1,0:T(8,128)(2,1)} %get-tuple-element.30), channel_id=1, source_target_pairs={{1,2},{3,4},{5,6},{7,0},{2,1},{4,3},{6,5},{0,7},{9,10},{11,12},{13... | collective-permute-start | bytes 737288 | tf_op jit(solution)/shard_map/ppermute | solution.py:482
  8.9 0.8 %copy-start.1 = (f32[5,24,128]{2,1,0:T(8,128)S(1)}, f32[5,24,128]{2,1,0:T(8,128)}, u32[]{:S(2)}) copy-start(f32[5,24,128]{2,1,0:T(8,128)} %get-tuple-element.25.lines_ref) | copy-start | bytes 184324
  14.0 4.9 %copy-start.2 = (f32[5,24,128]{2,1,0:T(8,128)S(1)}, f32[5,24,128]{2,1,0:T(8,128)}, u32[]{:S(2)}) copy-start(f32[5,24,128]{2,1,0:T(8,128)} %get-tuple-element.25.lines_ref) | copy-start | bytes 184324
  16.2 5.9 %collective-permute-start.4 = (bf16[64,640]{1,0:T(8,128)(2,1)S(1)}, bf16[64,640]{1,0:T(8,128)(2,1)S(1)}, u32[]{:S(2)}, u32[]{:S(2)}) collective-permute-start(bf16[64,640]{1,0:T(8,128)(2,1)S(1)} %maximum_bitcast_fusion), channel_id=1, source_target_pairs={{0,1},{2,3},{4,5},{6,7},{1,0},{3,2},{5,4},{7,6},{8,9},{10,11},{12,... | collective-permute-start | bytes 245768 | tf_op jit(solution)/shard_map/ppermute | solution.py:511
  16.3 5.8 %collective-permute-start.5 = (bf16[64,640]{1,0:T(8,128)(2,1)S(1)}, bf16[64,640]{1,0:T(8,128)(2,1)S(1)}, u32[]{:S(2)}, u32[]{:S(2)}) collective-permute-start(bf16[64,640]{1,0:T(8,128)(2,1)S(1)} %maximum_bitcast_fusion.1), channel_id=1, source_target_pairs={{1,2},{3,4},{5,6},{7,0},{2,1},{4,3},{6,5},{0,7},{9,10},{11,12},{13... | collective-permute-start | bytes 245768 | tf_op jit(solution)/shard_map/ppermute | solution.py:511

commit v5 on v4

--- a/solution.py
+++ b/solution.py
@@ -16,7 +16,7 @@
 LANES = 128
 DEPTH = 2 * LANES
 TILE = 16
-VMEM_BYTES = 24 * 1024 * 1024
+VMEM_BYTES = 20 * 1024 * 1024
 PIECE = 4
 F32, BF16 = jnp.float32, jnp.bfloat16
 
@@ -37,11 +37,19 @@
     return half + half * jnp.tanh(half * series)
 
 
-def swaps(peers, second, wrap):
+def swaps(peers, second):
     pairs = [(i, i + 1) for i in range(1 if second else 0, peers - 1, 2)]
-    if second and wrap:
+    if second:
         pairs.append((peers - 1, 0))
     return pairs + [(j, i) for i, j in pairs]
+
+
+def lat_swaps(peers, width, second):
+    pairs = [(i, i + 1) for i in range(1 if second else 0, peers - 1, 2)]
+    pairs += [(j, i) for i, j in pairs]
+    alone = set(range(peers)) - {i for i, _ in pairs}
+    result = [(i * width + k, j * width + k) for i, j in pairs for k in range(width)]
+    return result + [(i * width + k, i * width + (k ^ 1)) for i in sorted(alone) for k in range(width)]
 
 
 def pairs_of(items):
@@ -104,14 +112,32 @@
         unit()
 
 
+def line_choice(lags):
+    at = lax.broadcasted_iota(jnp.int32, (LANES, LANES), 0)
+    lane = lax.broadcasted_iota(jnp.int32, (LANES, LANES), 1)
+    chosen = (at // 8 == lane % WINDOW) & (at % 8 == lane // WINDOW) & (at % 8 < BANDS) & (at // 8 < lags)
+    return jnp.where(chosen, 1.0, 0.0).astype(BF16)
+
+
+def filter_lines(filter_ref, edge_ref, mask_ref, padded, chosen):
+    bases, lags, bands, rows = filter_ref.shape
+    source = lax.axis_index("lat") * rows + lax.broadcasted_iota(jnp.int32, (bands, rows), 1) - LAT_REACH
+    source = source + lax.broadcasted_iota(jnp.int32, (bands, rows), 0)
+    inside = (source >= edge_ref[0:1, :]) & (source < edge_ref[1:2, :])
+    for k in range(bases):
+        keep = inside & (mask_ref[k : k + 1, :] != 0)
+        for m in range(lags):
+            padded[k, m * 8 : m * 8 + bands, :rows] = jnp.where(keep, filter_ref[k, m], 0.0)
+    return [jnp.dot(padded[k].T.astype(BF16), chosen, preferred_element_type=F32) for k in range(bases)]
+
+
 def prep_kernel(
     rows_ref, tiles_ref, filter_in, edge_in, mask_in,
-    lat_a, lat_b, lon_a, lon_b, lines, filter_ref, edge_ref, mask_ref, sides, padded, tags, sems,
+    lat_a, lat_b, lon_a, lon_b, filter_ref, edge_ref, mask_ref, sides, padded, tags, sems,
 ):
     bases, lags, bands, rows = filter_in.shape
     groups = lat_a.shape[0] - 1
-    lat = lax.axis_index("lat")
-    lat_odd, lon_odd = lat % 2, lax.axis_index("lon") % 2
+    lat_odd, lon_odd = lax.axis_index("lat") % 2, lax.axis_index("lon") % 2
     start_a = (1 - lat_odd) * (rows_ref.shape[0] - groups)
     start_b = lat_odd * (rows_ref.shape[0] - groups)
     small = [
@@ -129,23 +155,10 @@
         copy.start()
     padded[...] = jnp.zeros_like(padded)
     tags[...] = jnp.zeros_like(tags)
-    at = lax.broadcasted_iota(jnp.int32, (LANES, LANES), 0)
-    lane = lax.broadcasted_iota(jnp.int32, (LANES, LANES), 1)
-    chosen = (at // 8 == lane % WINDOW) & (at % 8 == lane // WINDOW) & (at % 8 < bands) & (at // 8 < lags)
-    chosen = jnp.where(chosen, 1.0, 0.0).astype(BF16)
+    chosen = line_choice(lags)
     for copy in small:
         copy.wait()
-
-    source = lat * rows + lax.broadcasted_iota(jnp.int32, (bands, rows), 1) - LAT_REACH
-    source = source + lax.broadcasted_iota(jnp.int32, (bands, rows), 0)
-    inside = (source >= edge_ref[0:1, :]) & (source < edge_ref[1:2, :])
-    for k in range(bases):
-        keep = inside & (mask_ref[k : k + 1, :] != 0)
-        for m in range(lags):
-            padded[k, m * 8 : m * 8 + bands, :rows] = jnp.where(keep, filter_ref[k, m], 0.0)
-    for k in range(bases):
-        line = jnp.dot(padded[k].T.astype(BF16), chosen, preferred_element_type=F32)
-        lines[k] = line[:rows]
+    for k, line in enumerate(filter_lines(filter_ref, edge_ref, mask_ref, padded, chosen)):
         span = slice(k * LAT_REACH, (k + 1) * LAT_REACH)
         tags[0, span] = line[:LAT_REACH]
         tags[1, span] = line[rows - LAT_REACH : rows]
@@ -166,12 +179,18 @@
 
 
 def inner_kernel(
-    block, x_ref, lines_ref, one_ref, two_ref, toeplitz, edge_rows, edge_cells, sides, middle, field, hidden, ends
+    block, x_ref, filter_ref, edge_ref, mask_ref, one_ref, two_ref,
+    toeplitz, lines_ref, edge_rows, edge_cells, sides, middle, padded, field, hidden, ends,
 ):
     rows, cells, channels = x_ref.shape
     bases = one_ref.shape[0]
     chunks = channels // LANES
-    fill_toeplitz(toeplitz, lambda r, k: lines_ref[k, r : r + 1, :], rows, bases, lambda r: r % block)
+    padded[...] = jnp.zeros_like(padded)
+    chosen = line_choice(filter_ref.shape[1])
+    lines = filter_lines(filter_ref, edge_ref, mask_ref, padded, chosen)
+    for k in range(bases):
+        lines_ref[k] = lines[k][:rows]
+    fill_toeplitz(toeplitz, lambda r, k: lines[k][r : r + 1, :], rows, bases, lambda r: r % block)
     one, two = lane_weights(one_ref, 0.5), lane_weights(two_ref)
     starts = range(0, rows, block)
     windows = (cells - WINDOW) // CELLS + 1
@@ -239,7 +258,7 @@
 
 
 def rim_kernel(
-    block, x_ref, lat_a, lat_b, lon_a, lon_b, rows_in, cells_in, sides_in, toeplitz, lines_ref, one_ref, two_ref,
+    block, x_ref, lat_a, lat_b, lon_b, lon_a, rows_in, cells_in, sides_in, toeplitz, lines_ref, one_ref, two_ref,
     rim_toeplitz, wide_toeplitz, rim_out, side_out, ends, field, hidden,
 ):
     rows, cells, channels = x_ref.shape
@@ -362,7 +381,7 @@
 
 
 def corner_kernel(
-    x_ref, lat_a, lat_b, lon_a, lon_b, corner_a, corner_b, ends, rim_toeplitz, wide_toeplitz, one_ref, two_ref,
+    x_ref, lat_a, lat_b, lon_b, lon_a, corner_b, corner_a, ends, rim_toeplitz, wide_toeplitz, one_ref, two_ref,
     middle, side_out, rim_out, out_ref, corner_out, sems,
 ):
     rows, cells, channels = x_ref.shape
@@ -455,15 +474,15 @@
         return pltpu.VMEM(shape, dtype)
 
     groups = REACH * tiles
-    lat_a, lat_b, lon_a, lon_b, lines = pl.pallas_call(
+    filter_args = (filters.transpose(1, 3, 2, 0), band_edges.T, basis_mask.T)
+    lat_a, lat_b, lon_a, lon_b = pl.pallas_call(
         prep_kernel,
         out_shape=(
             array(groups + 1, TILE, channels), array(groups + 1, TILE, channels),
             array(rows * CELLS, channels), array(rows * CELLS, channels),
-            array(bases, rows, LANES, dtype=F32),
         ),
         in_specs=[anywhere] * 5,
-        out_specs=(vmem,) * 5,
+        out_specs=(vmem,) * 4,
         scratch_shapes=[
             scratch(bases, filters.shape[3], BANDS, rows, dtype=F32),
             scratch(2, rows, dtype=jnp.int32), scratch(bases, rows, dtype=jnp.int32),
@@ -475,25 +494,28 @@
         name="prep",
     )(
         state_field.reshape(rows * tiles, TILE, channels), state_field.reshape(rows, tiles, TILE, channels),
-        filters.transpose(1, 3, 2, 0), band_edges.T, basis_mask.T,
+        *filter_args,
     )
-    lat_a = lax.ppermute(lat_a, "lat", swaps(lat_peers, False, False)).reshape(edge + TILE, channels)
-    lat_b = lax.ppermute(lat_b, "lat", swaps(lat_peers, True, False)).reshape(edge + TILE, channels)
-    lon_b = lax.ppermute(lon_b, "lon", swaps(lon_peers, True, True))
-    lon_a = lax.ppermute(lon_a, "lon", swaps(lon_peers, False, True))
+    both = ("lat", "lon")
+    lat_a = lax.ppermute(lat_a, both, lat_swaps(lat_peers, lon_peers, False)).reshape(edge + TILE, channels)
+    lat_b = lax.ppermute(lat_b, both, lat_swaps(lat_peers, lon_peers, True)).reshape(edge + TILE, channels)
+    lon_b = lax.ppermute(lon_b, "lon", swaps(lon_peers, True))
+    lon_a = lax.ppermute(lon_a, "lon", swaps(lon_peers, False))
 
     middle = rows - 2 * REACH
     flops = 2 * (2 * rows - 3 * REACH) * (cells - 2 * CELLS) * bases * DEPTH * channels
     cost = pl.CostEstimate(flops=flops, bytes_accessed=4 * state_field.size, transcendentals=0)
-    toeplitz, edge_rows, edge_cells, sides, inner = pl.pallas_call(
+    toeplitz, lines, edge_rows, edge_cells, sides, inner = pl.pallas_call(
         functools.partial(inner_kernel, block),
         out_shape=(
-            array(rows * group, DEPTH), array(2 * REACH, cells, channels), array(middle - REACH, TILE, channels),
+            array(rows * group, DEPTH), array(bases, rows, LANES, dtype=F32),
+            array(2 * REACH, cells, channels), array(middle - REACH, TILE, channels),
             array(middle, TILE, channels), array(middle, cells - 2 * TILE, channels),
         ),
-        in_specs=[vmem] * 4,
-        out_specs=(vmem,) * 5,
+        in_specs=[vmem] * 6,
+        out_specs=(vmem,) * 6,
         scratch_shapes=[
+            scratch(bases, LANES, LANES, dtype=F32),
             scratch(chunks, rows + REACH, cells, LANES, dtype=F32),
             scratch(chunks, rows + REACH, cells - CELLS, LANES, dtype=F32),
             scratch(chunks, middle, TILE, LANES, dtype=F32),
@@ -501,14 +523,14 @@
         compiler_params=params,
         cost_estimate=cost,
         name="inner",
-    )(state_field, lines, weights_one, weights_two)
+    )(state_field, *filter_args, weights_one, weights_two)
 
     def corner_send(leading, second):
         start = jnp.where(leading, 0, cells - CELLS)
         joined = [v[:edge].reshape(REACH, cells, channels) for v in (lat_a, lat_b)]
         parts = [lax.dynamic_slice_in_dim(v, start, CELLS, 1) for v in joined]
         sent = jnp.concatenate(parts, 0).reshape(2 * REACH * CELLS, channels)
-        return lax.ppermute(sent, "lon", swaps(lon_peers, second, True))
+        return lax.ppermute(sent, "lon", swaps(lon_peers, second))
 
     lat_a, lat_b, inner = lax.optimization_barrier((lat_a, lat_b, inner))
     corner_b = corner_send(lon % 2 == 0, True)
@@ -529,7 +551,7 @@
         cost_estimate=cost,
         name="rim",
     )(
-        state_field, lat_a, lat_b, lon_a, lon_b, edge_rows, edge_cells, sides, toeplitz, lines,
+        state_field, lat_a, lat_b, lon_b, lon_a, edge_rows, edge_cells, sides, toeplitz, lines,
         weights_one, weights_two,
     )
     return pl.pallas_call(
@@ -542,7 +564,7 @@
         cost_estimate=cost,
         name="corner",
     )(
-        state_field, lat_a, lat_b, lon_a, lon_b, corner_a, corner_b, ends, rim_toeplitz, wide_toeplitz,
+        state_field, lat_a, lat_b, lon_b, lon_a, corner_b, corner_a, ends, rim_toeplitz, wide_toeplitz,
         weights_one, weights_two, inner, side_out, rim_out,
     )
 

time: 24.2 us -> 21.9 us (0.905)
  the two profiles are of different devices: /device:TPU:16 before, /device:TPU:0 now
where the time goes in v5:
time: 21.9 us; the launch traced here: 21.6 us
  Pallas kernels  12.2 us (56%)
  starting transfers between devices  7.57 us (35%)
  waiting for transfers between devices  1.55 us (7%)
    pallas_call x1, Pallas kernels, per_device(): pl.pallas_call(functools.partial(inner_kernel, block), out_shape=(array(r...  4.52 us
    pallas_call x1, Pallas kernels, per_device(): pl.pallas_call(functools.partial(rim_kernel, block), out_shape=(array(2 *...  3.18 us
    ppermute x1, starting transfers between devices, per_device(): lax.ppermute(lat_a, both, lat_swaps(lat_peers, lon_peers, False))  3.1 us
    pallas_call x1, Pallas kernels, per_device(): pl.pallas_call(prep_kernel, out_shape=(array(groups + 1, TILE, channels),...  2.65 us
    ppermute x1, starting transfers between devices, per_device(): lon_b = lax.ppermute(lon_b, 'lon', swaps(lon_peers, True))  2.56 us
    ppermute x2, starting transfers between devices, corner_send(): return lax.ppermute(sent, 'lon', swaps(lon_peers, second))  1.9 us
    pallas_call x1, Pallas kernels, per_device(): pl.pallas_call(corner_kernel, out_shape=array(rows, cells, channels), in_...  1.89 us
    ppermute x1, waiting for transfers between devices, per_device(): lax.ppermute(lat_a, both, lat_swaps(lat_peers, lon_peers, False))  1.21 us
  transfers between devices with their start and end apart: 6, of which 2 were waited for; matrix products, arithmetic and copies ran while one was open for 1% of the time, Pallas kernels for 36%

profile of v5, /device:TPU:0, one launch (start us, length us, event | category | flops | bytes accessed | tf_op | source)
XLA Modules:
  0.0 21.6 jit_solution(6157059047556520752)
XLA Ops:
  0.0 0.0 copy-start
  0.0 0.0 copy-start.1
  0.0 0.0 copy-start.2
  0.0 0.0 copy-start.3
  0.0 0.0 copy-start.4
  0.0 0.0 copy-start.5
  0.0 2.7 %prep.1 = (bf16[17,16,640]{2,1,0:T(8,128)(2,1)}, bf16[17,16,640]{2,1,0:T(8,128)(2,1)}, bf16[192,640]{1,0:T(8,128)(2,1)}, bf16[192,640]{1,0:T(8,128)(2,1)}) custom-call(bf16[96,16,640]{2,1,0:T(8,128)(2,1)} %bitcast.13, bf16[24,4,16,640]{3,2,1,0:T(8,128)(2,1)} %bitcast.14, f32[5,9,5,24]{3,2,1,0:T(8,128)} %bitcast.21, s32[2,24]{1,0:T(2,128)} %bitcast.25, ...), custom_call_target="tpu_custom_call" | custom-call | bytes 655360 | tf_op jit(solution)/shard_map/prep/pallas_call | solution.py:478
  2.7 3.1 %collective-permute-start = (bf16[17,16,640]{2,1,0:T(8,128)(2,1)}, bf16[17,16,640]{2,1,0:T(8,128)(2,1)S(1)}, u32[]{:S(2)}, u32[]{:S(2)}) collective-permute-start(bf16[17,16,640]{2,1,0:T(8,128)(2,1)} %get-tuple-element.23), channel_id=1, source_target_pairs={{0,8},{1,9},{2,10},{3,11},{4,12},{5,13},{6,14},{7,15},{16,24},{17,... | collective-permute-start | bytes 1044488 | tf_op jit(solution)/shard_map/ppermute | solution.py:500
  5.8 0.0 collective-permute-start.1
  5.8 2.6 %collective-permute-start.2 = (bf16[192,640]{1,0:T(8,128)(2,1)}, bf16[192,640]{1,0:T(8,128)(2,1)S(1)}, u32[]{:S(2)}, u32[]{:S(2)}) collective-permute-start(bf16[192,640]{1,0:T(8,128)(2,1)} %get-tuple-element.28), channel_id=1, source_target_pairs={{1,2},{3,4},{5,6},{7,0},{2,1},{4,3},{6,5},{0,7},{9,10},{11,12},{13... | collective-permute-start | bytes 737288 | tf_op jit(solution)/shard_map/ppermute | solution.py:502
  8.3 0.0 collective-permute-start.3
  8.4 0.0 copy-done
  8.4 0.0 copy-done.1
  8.4 0.0 copy-done.2
  8.4 0.0 copy-done.3
  8.4 0.0 copy-done.4
  8.4 0.0 copy-done.5
  8.4 4.5 %inner.1 = (bf16[960,256]{1,0:T(8,128)(2,1)S(1)}, f32[5,24,128]{2,1,0:T(8,128)S(1)}, bf16[8,64,640]{2,1,0:T(8,128)(2,1)S(1)}, bf16[12,16,640]{2,1,0:T(8,128)(2,1...) custom-call(bf16[24,64,640]{2,1,0:T(8,128)(2,1)S(1)} %copy-done, f32[5,9,5,24]{3,2,1,0:T(8,128)S(1)} %bitcast.22, ...), custom_call_target="tpu_custom_call" | custom-call | flops 2831155200 | bytes 3932160 | tf_op jit(solution)/shard_map/inner/pallas_call | solution.py:508
  12.9 1.2 %collective-permute-done = bf16[17,16,640]{2,1,0:T(8,128)(2,1)S(1)} collective-permute-done((bf16[17,16,640]{2,1,0:T(8,128)(2,1)}, bf16[17,16,640]{2,1,0:T(8,128)(2,1)S(1)}, u32[]{:S(2)}, u32[]{:S(2)}) %collective-permute-start) | collective-permute-done | bytes 348192 | tf_op jit(solution)/shard_map/ppermute | solution.py:500
  14.1 0.0 collective-permute-done.1
  14.3 1.2 %collective-permute-start.4 = (bf16[64,640]{1,0:T(8,128)(2,1)S(1)}, bf16[64,640]{1,0:T(8,128)(2,1)S(1)}, u32[]{:S(2)}, u32[]{:S(2)}) collective-permute-start(bf16[64,640]{1,0:T(8,128)(2,1)S(1)} %maximum_bitcast_fusion), channel_id=1, source_target_pairs={{1,2},{3,4},{5,6},{7,0},{2,1},{4,3},{6,5},{0,7},{9,10},{11,12},{13... | collective-permute-start | bytes 245768 | tf_op jit(solution)/shard_map/ppermute | solution.py:533
  15.5 0.7 %collective-permute-start.5 = (bf16[64,640]{1,0:T(8,128)(2,1)S(1)}, bf16[64,640]{1,0:T(8,128)(2,1)S(1)}, u32[]{:S(2)}, u32[]{:S(2)}) collective-permute-start(bf16[64,640]{1,0:T(8,128)(2,1)S(1)} %maximum_bitcast_fusion.1), channel_id=1, source_target_pairs={{0,1},{2,3},{4,5},{6,7},{1,0},{3,2},{5,4},{7,6},{8,9},{10,11},{12,... | collective-permute-start | bytes 245768 | tf_op jit(solution)/shard_map/ppermute | solution.py:533
  16.2 0.0 collective-permute-done.2.lon_b
  16.2 0.0 collective-permute-done.3.lon_a
  16.2 3.2 %rim.1 = (bf16[320,256]{1,0:T(8,128)(2,1)S(1)}, bf16[320,256]{1,0:T(8,128)(2,1)S(1)}, bf16[8,64,640]{2,1,0:T(8,128)(2,1)S(1)}, bf16[2,16,16,640]{3,2,1,0:T(8,128)(2,1)S(1)}, bf16[2,16,16,640]{3,2,1,0:T(8,128)(2,1)S(1)}) custom-call(bf16[24,64,640]{2,1,0:T(8,128)(2,1)S(1)} %copy-done, bf16[272,640]{1,0:T(8,128)(2,1)S(1)} %bitcast.16, ...), custom_call_target="tpu_custom_call" | custom-call | flops 2831155200 | bytes 3932160 | tf_op jit(solution)/shard_map/rim/pallas_call | solution.py:538
  19.4 0.3 %collective-permute-done.4.corner_b = bf16[64,640]{1,0:T(8,128)(2,1)S(1)} collective-permute-done((bf16[64,640]{1,0:T(8,128)(2,1)S(1)}, bf16[64,640]{1,0:T(8,128)(2,1)S(1)}, u32[]{:S(2)}, u32[]{:S(2)}) %collective-permute-start.4) | collective-permute-done | bytes 81952 | tf_op jit(solution)/shard_map/ppermute | solution.py:533
  19.7 0.0 collective-permute-done.5.corner_a
  19.7 1.9 %corner.1 = bf16[24,64,640]{2,1,0:T(8,128)(2,1)} custom-call(bf16[24,64,640]{2,1,0:T(8,128)(2,1)S(1)} %copy-done, bf16[272,640]{1,0:T(8,128)(2,1)S(1)} %bitcast.17, bf16[272,640]{1,0:T(8,128)(2,1)S(1)} %bitcast.20, bf16[192,640]{1,0:T(8,128)(2,1)S(1)} %collective-permute-done.2.lon_b, bf16[192,640]{1,0:T(8,128)(2,1)S(1)} %collective-permute-done.3.lon_a, ...), custom_call_target="tpu_custom_call" | custom-call | flops 2831155200 | bytes 3932160 | tf_op jit(solution)/shard_map/corner/pallas_call | solution.py:557
  (5 shorter events, 0.1 us)
Async XLA Ops:
  0.0 8.4 %copy-start = (bf16[24,64,640]{2,1,0:T(8,128)(2,1)S(1)}, bf16[24,64,640]{2,1,0:T(8,128)(2,1)}, u32[]{:S(2)}) copy-start(bf16[24,64,640]{2,1,0:T(8,128)(2,1)} %x_ref.5) | copy-start | bytes 5898244
  0.0 8.4 %copy-start.1 = (f32[24,5,5,9]{0,2,3,1:T(8,128)S(1)}, f32[24,5,5,9]{0,2,3,1:T(8,128)}, u32[]{:S(2)}) copy-start(f32[24,5,5,9]{0,2,3,1:T(8,128)} %param.7) | copy-start | bytes 64804
  0.0 8.4 %copy-start.2 = (s32[24,5]{0,1:T(8,128)S(1)}, s32[24,5]{0,1:T(8,128)}, u32[]{:S(2)}) copy-start(s32[24,5]{0,1:T(8,128)} %param.9) | copy-start | bytes 1444
  0.0 8.4 %copy-start.3 = (s32[24,2]{0,1:T(2,128)S(1)}, s32[24,2]{0,1:T(2,128)}, u32[]{:S(2)}) copy-start(s32[24,2]{0,1:T(2,128)} %param.8) | copy-start | bytes 580
  0.0 8.4 %copy-start.4 = (f32[5,640]{1,0:T(8,128)S(1)}, f32[5,640]{1,0:T(8,128)}, u32[]{:S(2)}) copy-start(f32[5,640]{1,0:T(8,128)} %one_ref.5) | copy-start | bytes 38404
  0.0 8.4 %copy-start.5 = (f32[5,640]{1,0:T(8,128)S(1)}, f32[5,640]{1,0:T(8,128)}, u32[]{:S(2)}) copy-start(f32[5,640]{1,0:T(8,128)} %two_ref.5) | copy-start | bytes 38404
  2.7 11.5 %collective-permute-start = (bf16[17,16,640]{2,1,0:T(8,128)(2,1)}, bf16[17,16,640]{2,1,0:T(8,128)(2,1)S(1)}, u32[]{:S(2)}, u32[]{:S(2)}) collective-permute-start(bf16[17,16,640]{2,1,0:T(8,128)(2,1)} %get-tuple-element.23), channel_id=1, source_target_pairs={{0,8},{1,9},{2,10},{3,11},{4,12},{5,13},{6,14},{7,15},{16,24},{17,... | collective-permute-start | bytes 1044488 | tf_op jit(solution)/shard_map/ppermute | solution.py:500
  5.8 8.4 %collective-permute-start.1 = (bf16[17,16,640]{2,1,0:T(8,128)(2,1)}, bf16[17,16,640]{2,1,0:T(8,128)(2,1)S(1)}, u32[]{:S(2)}, u32[]{:S(2)}) collective-permute-start(bf16[17,16,640]{2,1,0:T(8,128)(2,1)} %get-tuple-element.24), channel_id=1, source_target_pairs={{8,16},{9,17},{10,18},{11,19},{12,20},{13,21},{14,22},{15,23},{16,... | collective-permute-start | bytes 1044488 | tf_op jit(solution)/shard_map/ppermute | solution.py:501
  5.8 10.4 %collective-permute-start.2 = (bf16[192,640]{1,0:T(8,128)(2,1)}, bf16[192,640]{1,0:T(8,128)(2,1)S(1)}, u32[]{:S(2)}, u32[]{:S(2)}) collective-permute-start(bf16[192,640]{1,0:T(8,128)(2,1)} %get-tuple-element.28), channel_id=1, source_target_pairs={{1,2},{3,4},{5,6},{7,0},{2,1},{4,3},{6,5},{0,7},{9,10},{11,12},{13... | collective-permute-start | bytes 737288 | tf_op jit(solution)/shard_map/ppermute | solution.py:502
  8.3 7.9 %collective-permute-start.3 = (bf16[192,640]{1,0:T(8,128)(2,1)}, bf16[192,640]{1,0:T(8,128)(2,1)S(1)}, u32[]{:S(2)}, u32[]{:S(2)}) collective-permute-start(bf16[192,640]{1,0:T(8,128)(2,1)} %get-tuple-element.29), channel_id=1, source_target_pairs={{0,1},{2,3},{4,5},{6,7},{1,0},{3,2},{5,4},{7,6},{8,9},{10,11},{12,... | collective-permute-start | bytes 737288 | tf_op jit(solution)/shard_map/ppermute | solution.py:503
  14.3 5.4 %collective-permute-start.4 = (bf16[64,640]{1,0:T(8,128)(2,1)S(1)}, bf16[64,640]{1,0:T(8,128)(2,1)S(1)}, u32[]{:S(2)}, u32[]{:S(2)}) collective-permute-start(bf16[64,640]{1,0:T(8,128)(2,1)S(1)} %maximum_bitcast_fusion), channel_id=1, source_target_pairs={{1,2},{3,4},{5,6},{7,0},{2,1},{4,3},{6,5},{0,7},{9,10},{11,12},{13... | collective-permute-start | bytes 245768 | tf_op jit(solution)/shard_map/ppermute | solution.py:533
  15.5 4.2 %collective-permute-start.5 = (bf16[64,640]{1,0:T(8,128)(2,1)S(1)}, bf16[64,640]{1,0:T(8,128)(2,1)S(1)}, u32[]{:S(2)}, u32[]{:S(2)}) collective-permute-start(bf16[64,640]{1,0:T(8,128)(2,1)S(1)} %maximum_bitcast_fusion.1), channel_id=1, source_target_pairs={{0,1},{2,3},{4,5},{6,7},{1,0},{3,2},{5,4},{7,6},{8,9},{10,11},{12,... | collective-permute-start | bytes 245768 | tf_op jit(solution)/shard_map/ppermute | solution.py:533

commit v6 on v5

--- a/solution.py
+++ b/solution.py
@@ -60,10 +60,10 @@
     return slice(chunk * LANES, (chunk + 1) * LANES)
 
 
-def fill_toeplitz(toeplitz, line_of, rows, bases, place_of):
+def fill_toeplitz(toeplitz, line_of, rows, bases, place_of, pairs=None):
     group = bases * CELLS
     blank = jnp.zeros((CELLS, DEPTH - LANES), F32)
-    for row in range(0, rows, 2):
+    for row in pairs or range(0, rows, 2):
         parts = []
         for r in (row, row + 1):
             for basis in range(bases):
@@ -132,55 +132,64 @@
 
 
 def prep_kernel(
-    rows_ref, tiles_ref, filter_in, edge_in, mask_in,
-    lat_a, lat_b, lon_a, lon_b, filter_ref, edge_ref, mask_ref, sides, padded, tags, sems,
+    flat_ref, groups_ref, filter_in, edge_in, mask_in, lat_a, lat_b, lon_a, lon_b,
+    filter_ref, edge_ref, mask_ref, ends, sides, padded, tags, packed, sems, out_sems,
 ):
     bases, lags, bands, rows = filter_in.shape
-    groups = lat_a.shape[0] - 1
+    across = groups_ref.shape[1]
+    edge = REACH * across
     lat_odd, lon_odd = lax.axis_index("lat") % 2, lax.axis_index("lon") % 2
-    start_a = (1 - lat_odd) * (rows_ref.shape[0] - groups)
-    start_b = lat_odd * (rows_ref.shape[0] - groups)
+    firsts = (1 - lat_odd, lat_odd)
     small = [
-        pltpu.make_async_copy(filter_in, filter_ref, sems.at[4]),
-        pltpu.make_async_copy(edge_in, edge_ref, sems.at[5]),
-        pltpu.make_async_copy(mask_in, mask_ref, sems.at[6]),
+        pltpu.make_async_copy(filter_in, filter_ref, sems.at[0]),
+        pltpu.make_async_copy(edge_in, edge_ref, sems.at[1]),
+        pltpu.make_async_copy(mask_in, mask_ref, sems.at[2]),
     ]
-    copies = [
-        pltpu.make_async_copy(tiles_ref.at[:, 0], sides.at[0], sems.at[0]),
-        pltpu.make_async_copy(tiles_ref.at[:, tiles_ref.shape[1] - 1], sides.at[1], sems.at[1]),
-        pltpu.make_async_copy(rows_ref.at[pl.ds(start_a, groups)], lat_a.at[pl.ds(0, groups)], sems.at[2]),
-        pltpu.make_async_copy(rows_ref.at[pl.ds(start_b, groups)], lat_b.at[pl.ds(0, groups)], sems.at[3]),
-    ]
-    for copy in small + copies:
+    rows_in, cells_in = [], []
+    for i in range(2):
+        place = pl.ds(firsts[i] * (rows - REACH) * across, edge)
+        rows_in.append(pltpu.make_async_copy(flat_ref.at[place], ends.at[i], sems.at[3 + i]))
+        place = (1 - lon_odd if i == 0 else lon_odd) * (across - 1)
+        cells_in.append(pltpu.make_async_copy(groups_ref.at[:, place], sides.at[i], sems.at[5 + i]))
+    for copy in rows_in + small + cells_in:
         copy.start()
     padded[...] = jnp.zeros_like(padded)
     tags[...] = jnp.zeros_like(tags)
     chosen = line_choice(lags)
+    pending = []
+
+    def send(source, target):
+        pending.append(pltpu.make_async_copy(source, target, out_sems.at[len(pending)]))
+        pending[-1].start()
+
+    for i, out in enumerate((lat_a, lat_b)):
+        rows_in[i].wait()
+        send(ends.at[i], out.at[pl.ds(0, edge)])
     for copy in small:
         copy.wait()
     for k, line in enumerate(filter_lines(filter_ref, edge_ref, mask_ref, padded, chosen)):
-        span = slice(k * LAT_REACH, (k + 1) * LAT_REACH)
-        tags[0, span] = line[:LAT_REACH]
-        tags[1, span] = line[rows - LAT_REACH : rows]
-    blank = jnp.zeros((TILE, lat_a.shape[2] - LANES), F32)
-    first = jnp.concatenate([tags[0], blank], 1)
-    last = jnp.concatenate([tags[1], blank], 1)
-    lat_a[groups] = jnp.where(lat_odd == 1, first, last).astype(BF16)
-    lat_b[groups] = jnp.where(lat_odd == 1, last, first).astype(BF16)
-    copies[0].wait()
-    copies[1].wait()
-    leading = sides[0].astype(F32)[:, :CELLS]
-    trailing = sides[1].astype(F32)[:, TILE - CELLS :]
-    odd = lon_odd == 1
-    lon_a[...] = jnp.where(odd, leading, trailing).reshape(lon_a.shape).astype(BF16)
-    lon_b[...] = jnp.where(odd, trailing, leading).reshape(lon_b.shape).astype(BF16)
-    for copy in copies[2:]:
+        tags[0, :LAT_REACH, lanes_of(k)] = line[:LAT_REACH]
+        tags[1, :LAT_REACH, lanes_of(k)] = line[rows - LAT_REACH : rows]
+    odd = lat_odd == 1
+    packed[0] = jnp.where(odd, tags[0], tags[1]).astype(BF16)
+    packed[1] = jnp.where(odd, tags[1], tags[0]).astype(BF16)
+    for i, out in enumerate((lat_a, lat_b)):
+        send(packed.at[i], out.at[edge])
+    for i, out in enumerate((lon_a, lon_b)):
+        cells_in[i].wait()
+        send(sides.at[i], out)
+    for copy in pending:
         copy.wait()
+
+
+def place_of(r):
+    return r if r < REACH else REACH + r
 
 
 def inner_kernel(
     block, x_ref, filter_ref, edge_ref, mask_ref, one_ref, two_ref,
-    toeplitz, lines_ref, edge_rows, edge_cells, sides, middle, padded, field, hidden, ends,
+    toeplitz, rim_toeplitz, wide_toeplitz, edge_rows, edge_cells, sides, out_ref,
+    middle, padded, field, hidden, ends, sems,
 ):
     rows, cells, channels = x_ref.shape
     bases = one_ref.shape[0]
@@ -188,9 +197,15 @@
     padded[...] = jnp.zeros_like(padded)
     chosen = line_choice(filter_ref.shape[1])
     lines = filter_lines(filter_ref, edge_ref, mask_ref, padded, chosen)
-    for k in range(bases):
-        lines_ref[k] = lines[k][:rows]
     fill_toeplitz(toeplitz, lambda r, k: lines[k][r : r + 1, :], rows, bases, lambda r: r % block)
+    kept = list(range(REACH)) + list(range(rows - REACH, rows))
+    fill_toeplitz(wide_toeplitz, lambda r, k: lines[k][kept[r] : kept[r] + 1, :], 2 * REACH, bases, place_of)
+    shifted = [r - LAT_REACH for r in range(REACH)] + [rows - LAT_REACH + r for r in range(REACH)]
+    own = range(LAT_REACH, 2 * REACH - LAT_REACH, 2)
+    rim_toeplitz[...] = jnp.zeros_like(rim_toeplitz)
+    fill_toeplitz(
+        rim_toeplitz, lambda r, k: lines[k][shifted[r] : shifted[r] + 1, :], 2 * REACH, bases, place_of, own
+    )
     one, two = lane_weights(one_ref, 0.5), lane_weights(two_ref)
     starts = range(0, rows, block)
     windows = (cells - WINDOW) // CELLS + 1
@@ -246,6 +261,10 @@
             steps[c][0][1 : 1 + len(starts)] = []
             steps[c - 1][0].extend([steps[c][0].pop(0)] + straddle)
     run_mixed(steps)
+    target = out_ref.at[pl.ds(REACH, rows - 2 * REACH), pl.ds(TILE, cells - 2 * TILE)]
+    copy = pltpu.make_async_copy(middle, target, sems.at[0])
+    copy.start()
+    copy.wait()
 
 
 def ordered(odd, a, b):
@@ -258,39 +277,32 @@
 
 
 def rim_kernel(
-    block, x_ref, lat_a, lat_b, lon_b, lon_a, rows_in, cells_in, sides_in, toeplitz, lines_ref, one_ref, two_ref,
-    rim_toeplitz, wide_toeplitz, rim_out, side_out, ends, field, hidden,
+    block, x_ref, lat_a, lat_b, lon_b, lon_a, rows_in, cells_in, sides_in,
+    toeplitz, known_toeplitz, wide_toeplitz, one_ref, two_ref,
+    rim_toeplitz, rim_out, side_out, ends, field, hidden,
 ):
     rows, cells, channels = x_ref.shape
     bases = one_ref.shape[0]
     chunks = channels // LANES
-    edge = REACH * cells
+    group = bases * CELLS
+    edge = REACH * (cells // CELLS)
     columns = cells // CELLS + 1
     lat_odd, lon_odd = parities()
     one, two = lane_weights(one_ref, 0.5), lane_weights(two_ref)
-    kept = list(range(REACH)) + list(range(rows - REACH, rows))
-
-    def place_of(r):
-        return r if r < REACH else REACH + r
-
-    tags = ordered(lat_odd, lat_a[edge:, :LANES], lat_b[edge:, :LANES])
-
-    def rim_line(r, k):
-        if r < LAT_REACH:
-            return tags[0][k * LAT_REACH + r : k * LAT_REACH + r + 1, :]
-        if r >= 2 * REACH - LAT_REACH:
-            at = k * LAT_REACH + r - (2 * REACH - LAT_REACH)
-            return tags[1][at : at + 1, :]
-        at = r - LAT_REACH if r < REACH else rows - LAT_REACH + r - REACH
-        return lines_ref[k, at : at + 1, :]
-
-    fill_toeplitz(rim_toeplitz, rim_line, 2 * REACH, bases, place_of)
-    fill_toeplitz(wide_toeplitz, lambda r, k: lines_ref[k, kept[r] : kept[r] + 1, :], 2 * REACH, bases, place_of)
+    tags = ordered(lat_odd, lat_a[edge], lat_b[edge])
+
+    def tag_line(r, k):
+        at = r % LAT_REACH
+        return tags[0 if r < REACH else 1][at : at + 1, lanes_of(k)]
+
+    own = slice(LAT_REACH * group, (2 * REACH - LAT_REACH) * group)
+    rim_toeplitz[own, :] = known_toeplitz[own, :]
+    fill_toeplitz(rim_toeplitz, tag_line, 2 * REACH, bases, place_of, (0, 2 * REACH - LAT_REACH))
 
     def load(c):
         lanes = lanes_of(c)
-        lat = ordered(lat_odd, lat_a[:edge, lanes], lat_b[:edge, lanes])
-        lon = ordered(lon_odd, lon_a[:, lanes], lon_b[:, lanes])
+        lat = ordered(lat_odd, lat_a[:edge, :, lanes], lat_b[:edge, :, lanes])
+        lon = ordered(lon_odd, lon_a[:, :, lanes], lon_b[:, :, lanes])
         inner = slice(REACH, rows - REACH)
         blank = jnp.zeros((REACH, CELLS, LANES), F32)
         for side in range(2):
@@ -303,7 +315,7 @@
             at = slice(own.start + CELLS, own.stop + CELLS)
             field[c, 2 * REACH : rows, at] = x_ref[inner, own, lanes].astype(F32)
             span = slice(side * (CELLS + cells), side * (CELLS + cells) + CELLS)
-            field[c, REACH : REACH + rows, span] = lon[side].reshape(rows, CELLS, LANES)
+            field[c, REACH : REACH + rows, span] = lon[side]
             for end in range(2):
                 at = slice(end * (rows + REACH), end * (rows + REACH) + REACH)
                 field[c, at, span] = blank
@@ -382,16 +394,17 @@
 
 def corner_kernel(
     x_ref, lat_a, lat_b, lon_b, lon_a, corner_b, corner_a, ends, rim_toeplitz, wide_toeplitz, one_ref, two_ref,
-    middle, side_out, rim_out, out_ref, corner_out, sems,
+    side_out, rim_out, begun_ref, out_ref, corner_out, sems,
 ):
+    del begun_ref
     rows, cells, channels = x_ref.shape
     chunks = channels // LANES
-    edge = REACH * cells
+    edge = REACH * (cells // CELLS)
     inner = pl.ds(REACH, rows - 2 * REACH)
     ends_at = (pl.ds(0, REACH), pl.ds(rows - REACH, REACH))
     sides_at = (pl.ds(0, TILE), pl.ds(cells - TILE, TILE))
     span = pl.ds(TILE, cells - 2 * TILE)
-    moves = [(middle, out_ref.at[inner, span])]
+    moves = []
     for i in range(2):
         moves.append((side_out.at[i], out_ref.at[inner, sides_at[i]]))
         moves.append((rim_out.at[pl.ds(i * REACH, REACH), span], out_ref.at[ends_at[i], span]))
@@ -403,8 +416,8 @@
 
     def first(c):
         lanes = lanes_of(c)
-        lat = ordered(lat_odd, lat_a[:edge, lanes], lat_b[:edge, lanes])
-        lon = ordered(lon_odd, lon_a[:, lanes], lon_b[:, lanes])
+        lat = ordered(lat_odd, lat_a[:edge, :, lanes], lat_b[:edge, :, lanes])
+        lon = ordered(lon_odd, lon_a[:, :, lanes], lon_b[:, :, lanes])
         corner = ordered(lon_odd, corner_a[:, lanes], corner_b[:, lanes])
         tall = []
         for side in range(2):
@@ -413,7 +426,7 @@
             tiles = slice(side * (cells - TILE), side * (cells - TILE) + TILE)
             half = slice(side * (TILE - CELLS), side * (TILE - CELLS) + CELLS)
             mine = [x_ref[r : r + REACH, tiles, lanes].astype(F32)[:, half] for r in (0, rows - REACH)]
-            near = lon[side].reshape(rows, CELLS, LANES)
+            near = lon[side]
             far = ordered(lat_odd, corner[side][: REACH * CELLS], corner[side][REACH * CELLS :])
             far = [v.reshape(REACH, CELLS, LANES) for v in far]
             own = jnp.concatenate([above[0], mine[0], mine[1], above[1]], 0)
@@ -456,8 +469,6 @@
     bases = filters.shape[1]
     group = bases * CELLS
     chunks = channels // LANES
-    tiles = cells // TILE
-    edge = REACH * cells
     block = max(b for b in range(2, rows + 1, 2) if rows % b == 0 and (b + REACH) * WINDOW <= DEPTH)
     lat_peers, lon_peers = lax.axis_size("lat"), lax.axis_size("lon")
     lon = lax.axis_index("lon")
@@ -473,52 +484,51 @@
     def scratch(*shape, dtype=BF16):
         return pltpu.VMEM(shape, dtype)
 
-    groups = REACH * tiles
+    across = cells // CELLS
+    edge = REACH * across
     filter_args = (filters.transpose(1, 3, 2, 0), band_edges.T, basis_mask.T)
     lat_a, lat_b, lon_a, lon_b = pl.pallas_call(
         prep_kernel,
-        out_shape=(
-            array(groups + 1, TILE, channels), array(groups + 1, TILE, channels),
-            array(rows * CELLS, channels), array(rows * CELLS, channels),
-        ),
+        out_shape=(array(edge + 1, CELLS, channels),) * 2 + (array(rows, CELLS, channels),) * 2,
         in_specs=[anywhere] * 5,
-        out_specs=(vmem,) * 4,
+        out_specs=(anywhere,) * 4,
         scratch_shapes=[
             scratch(bases, filters.shape[3], BANDS, rows, dtype=F32),
             scratch(2, rows, dtype=jnp.int32), scratch(bases, rows, dtype=jnp.int32),
-            scratch(2, rows, TILE, channels), scratch(bases, LANES, LANES, dtype=F32),
-            scratch(2, TILE, LANES, dtype=F32), dma((7,)),
+            scratch(2, edge, CELLS, channels), scratch(2, rows, CELLS, channels),
+            scratch(bases, LANES, LANES, dtype=F32), scratch(2, CELLS, channels, dtype=F32),
+            scratch(2, CELLS, channels), dma((7,)), dma((6,)),
         ],
         compiler_params=pltpu.CompilerParams(vmem_limit_bytes=60 * 1024 * 1024),
-        cost_estimate=pl.CostEstimate(flops=0, bytes_accessed=4 * edge * channels, transcendentals=0),
+        cost_estimate=pl.CostEstimate(flops=0, bytes_accessed=8 * REACH * cells * channels, transcendentals=0),
         name="prep",
     )(
-        state_field.reshape(rows * tiles, TILE, channels), state_field.reshape(rows, tiles, TILE, channels),
+        state_field.reshape(rows * across, CELLS, channels), state_field.reshape(rows, across, CELLS, channels),
         *filter_args,
     )
     both = ("lat", "lon")
-    lat_a = lax.ppermute(lat_a, both, lat_swaps(lat_peers, lon_peers, False)).reshape(edge + TILE, channels)
-    lat_b = lax.ppermute(lat_b, both, lat_swaps(lat_peers, lon_peers, True)).reshape(edge + TILE, channels)
+    lat_a = lax.ppermute(lat_a, both, lat_swaps(lat_peers, lon_peers, False))
+    lat_b = lax.ppermute(lat_b, both, lat_swaps(lat_peers, lon_peers, True))
     lon_b = lax.ppermute(lon_b, "lon", swaps(lon_peers, True))
     lon_a = lax.ppermute(lon_a, "lon", swaps(lon_peers, False))
 
     middle = rows - 2 * REACH
     flops = 2 * (2 * rows - 3 * REACH) * (cells - 2 * CELLS) * bases * DEPTH * channels
     cost = pl.CostEstimate(flops=flops, bytes_accessed=4 * state_field.size, transcendentals=0)
-    toeplitz, lines, edge_rows, edge_cells, sides, inner = pl.pallas_call(
+    toeplitz, known, wide, edge_rows, edge_cells, sides, begun = pl.pallas_call(
         functools.partial(inner_kernel, block),
         out_shape=(
-            array(rows * group, DEPTH), array(bases, rows, LANES, dtype=F32),
+            array(rows * group, DEPTH), array(2 * REACH * group, DEPTH), array(2 * REACH * group, DEPTH),
             array(2 * REACH, cells, channels), array(middle - REACH, TILE, channels),
-            array(middle, TILE, channels), array(middle, cells - 2 * TILE, channels),
+            array(middle, TILE, channels), array(rows, cells, channels),
         ),
         in_specs=[vmem] * 6,
-        out_specs=(vmem,) * 6,
+        out_specs=(vmem,) * 6 + (anywhere,),
         scratch_shapes=[
-            scratch(bases, LANES, LANES, dtype=F32),
+            scratch(middle, cells - 2 * TILE, channels), scratch(bases, LANES, LANES, dtype=F32),
             scratch(chunks, rows + REACH, cells, LANES, dtype=F32),
             scratch(chunks, rows + REACH, cells - CELLS, LANES, dtype=F32),
-            scratch(chunks, middle, TILE, LANES, dtype=F32),
+            scratch(chunks, middle, TILE, LANES, dtype=F32), dma((1,)),
         ],
         compiler_params=params,
         cost_estimate=cost,
@@ -532,17 +542,17 @@
         sent = jnp.concatenate(parts, 0).reshape(2 * REACH * CELLS, channels)
         return lax.ppermute(sent, "lon", swaps(lon_peers, second))
 
-    lat_a, lat_b, inner = lax.optimization_barrier((lat_a, lat_b, inner))
+    lat_a, lat_b, sides = lax.optimization_barrier((lat_a, lat_b, sides))
     corner_b = corner_send(lon % 2 == 0, True)
     corner_a = corner_send(lon % 2 == 1, False)
-    rim_toeplitz, wide_toeplitz, rim_out, side_out, ends = pl.pallas_call(
+    rim_toeplitz, rim_out, side_out, ends = pl.pallas_call(
         functools.partial(rim_kernel, block),
         out_shape=(
-            array(2 * REACH * group, DEPTH), array(2 * REACH * group, DEPTH), array(2 * REACH, cells, channels),
-            array(2, middle, TILE, channels), array(2, 4 * REACH, WINDOW, channels),
+            array(2 * REACH * group, DEPTH), array(2 * REACH, cells, channels), array(2, middle, TILE, channels),
+            array(2, 4 * REACH, WINDOW, channels),
         ),
-        in_specs=[vmem] * 12,
-        out_specs=(vmem,) * 5,
+        in_specs=[vmem] * 13,
+        out_specs=(vmem,) * 4,
         scratch_shapes=[
             scratch(chunks, rows + 2 * REACH, cells + 2 * CELLS, LANES, dtype=F32),
             scratch(chunks, rows + REACH, cells + CELLS, LANES, dtype=F32),
@@ -551,21 +561,22 @@
         cost_estimate=cost,
         name="rim",
     )(
-        state_field, lat_a, lat_b, lon_b, lon_a, edge_rows, edge_cells, sides, toeplitz, lines,
-        weights_one, weights_two,
+        state_field, lat_a, lat_b, lon_b, lon_a, edge_rows, edge_cells, sides,
+        toeplitz, known, wide, weights_one, weights_two,
     )
     return pl.pallas_call(
         corner_kernel,
         out_shape=array(rows, cells, channels),
-        in_specs=[vmem] * 15,
+        in_specs=[vmem] * 14 + [anywhere],
         out_specs=anywhere,
-        scratch_shapes=[scratch(2, 2 * REACH, TILE, channels), dma((9,))],
+        input_output_aliases={14: 0},
+        scratch_shapes=[scratch(2, 2 * REACH, TILE, channels), dma((8,))],
         compiler_params=params,
         cost_estimate=cost,
         name="corner",
     )(
-        state_field, lat_a, lat_b, lon_b, lon_a, corner_b, corner_a, ends, rim_toeplitz, wide_toeplitz,
-        weights_one, weights_two, inner, side_out, rim_out,
+        state_field, lat_a, lat_b, lon_b, lon_a, corner_b, corner_a, ends, rim_toeplitz, wide,
+        weights_one, weights_two, side_out, rim_out, begun,
     )
 
 

time: 21.9 us -> 21.3 us (0.973)
  waiting for transfers between devices: 1.55 us -> 0.45 us
  Pallas kernels: 12.2 us -> 12.7 us
    ppermute x2, waiting for transfers between devices: 1.22 us -> 0.16 us  [the longest x1 0.16 us: per_device(): lat_a = lax.ppermute(lat_a, both, lat_swaps(lat_peers, lon_peers, False))]
    pallas_call x1, Pallas kernels: 4.52 us -> 5.36 us  [per_device(): pl.pallas_call(functools.partial(inner_kernel, block), out_shape=(array(r...]
  transfers between devices with their start and end apart: 6 -> 6, of which waited for: 2 -> 2; matrix products, arithmetic and copies ran while one was open for 1% -> 1% of each run, Pallas kernels for 36% -> 41%
where the time goes in v6:
time: 21.3 us; the launch traced here: 21 us
  Pallas kernels  12.7 us (60%)
  starting transfers between devices  7.57 us (36%)
  waiting for transfers between devices  0.45 us (2%)
    pallas_call x1, Pallas kernels, per_device(): pl.pallas_call(functools.partial(inner_kernel, block), out_shape=(array(r...  5.36 us
    pallas_call x1, Pallas kernels, per_device(): pl.pallas_call(functools.partial(rim_kernel, block), out_shape=(array(2 *...  3.23 us
    ppermute x1, starting transfers between devices, per_device(): lat_a = lax.ppermute(lat_a, both, lat_swaps(lat_peers, lon_peers, False))  3.1 us
    ppermute x1, starting transfers between devices, per_device(): lon_b = lax.ppermute(lon_b, 'lon', swaps(lon_peers, True))  2.56 us
    pallas_call x1, Pallas kernels, per_device(): pl.pallas_call(prep_kernel, out_shape=(array(edge + 1, CELLS, channels),)...  2.44 us
    ppermute x2, starting transfers between devices, corner_send(): return lax.ppermute(sent, 'lon', swaps(lon_peers, second))  1.9 us
    pallas_call x1, Pallas kernels, per_device(): pl.pallas_call(corner_kernel, out_shape=array(rows, cells, channels), in_...  1.68 us
  transfers between devices with their start and end apart: 6, of which 2 were waited for; matrix products, arithmetic and copies ran while one was open for 1% of the time, Pallas kernels for 41%

profile of v6, /device:TPU:0, one launch (start us, length us, event | category | flops | bytes accessed | tf_op | source)
XLA Modules:
  0.0 21.0 jit_solution(15553611636212119472)
XLA Ops:
  0.0 0.0 copy-start
  0.0 0.0 copy-start.1
  0.0 0.0 copy-start.2
  0.0 0.0 copy-start.3
  0.0 0.0 copy-start.4
  0.0 0.0 copy-start.5
  0.0 2.4 %prep.1 = (bf16[33,8,640]{2,1,0:T(8,128)(2,1)}, bf16[33,8,640]{2,1,0:T(8,128)(2,1)}, bf16[24,8,640]{2,1,0:T(8,128)(2,1)}, bf16[24,8,640]{2,1,0:T(8,128)(2,1)}) custom-call(bf16[192,8,640]{2,1,0:T(8,128)(2,1)} %bitcast.11, bf16[24,8,8,640]{3,2,1,0:T(8,128)(2,1)} %bitcast.12, f32[5,9,5,24]{3,2,1,0:T(8,128)} %bitcast.13, s32[2,24]{1,0:T(2,128)} %bitcast.17, ...), custom_call_target="tpu_custom_call" | custom-call | bytes 1310720 | tf_op jit(solution)/shard_map/prep/pallas_call | solution.py:490
  2.5 3.1 %collective-permute-start = (bf16[33,8,640]{2,1,0:T(8,128)(2,1)}, bf16[33,8,640]{2,1,0:T(8,128)(2,1)S(1)}, u32[]{:S(2)}, u32[]{:S(2)}) collective-permute-start(bf16[33,8,640]{2,1,0:T(8,128)(2,1)} %get-tuple-element.23), channel_id=1, source_target_pairs={{0,8},{1,9},{2,10},{3,11},{4,12},{5,13},{6,14},{7,15},{16,24},{17,... | collective-permute-start | bytes 1013768 | tf_op jit(solution)/shard_map/ppermute | solution.py:510
  5.6 0.0 collective-permute-start.1
  5.6 2.6 %collective-permute-start.2 = (bf16[24,8,640]{2,1,0:T(8,128)(2,1)}, bf16[24,8,640]{2,1,0:T(8,128)(2,1)S(1)}, u32[]{:S(2)}, u32[]{:S(2)}) collective-permute-start(bf16[24,8,640]{2,1,0:T(8,128)(2,1)} %get-tuple-element.28), channel_id=1, source_target_pairs={{1,2},{3,4},{5,6},{7,0},{2,1},{4,3},{6,5},{0,7},{9,10},{11,12},{13... | collective-permute-start | bytes 737288 | tf_op jit(solution)/shard_map/ppermute | solution.py:512
  8.1 0.0 collective-permute-start.3
  8.1 0.0 copy-done
  8.1 0.0 copy-done.1
  8.2 0.0 copy-done.2
  8.2 0.0 copy-done.3
  8.2 0.0 copy-done.4
  8.2 0.0 copy-done.5
  8.2 5.4 %inner.1 = (bf16[960,256]{1,0:T(8,128)(2,1)S(1)}, bf16[320,256]{1,0:T(8,128)(2,1)S(1)}, bf16[320,256]{1,0:T(8,128)(2,1)S(1)}, bf16[8,64,640]{2,1,0:T(8,128)(2,1)...) custom-call(bf16[24,64,640]{2,1,0:T(8,128)(2,1)S(1)} %copy-done, ...), custom_call_target="tpu_custom_call" | custom-call | flops 2831155200 | bytes 3932160 | tf_op jit(solution)/shard_map/inner/pallas_call | solution.py:518
  13.6 0.2 collective-permute-done.lat_a
  13.7 0.0 collective-permute-done.1.lat_b
  13.9 1.2 %collective-permute-start.4 = (bf16[64,640]{1,0:T(8,128)(2,1)S(1)}, bf16[64,640]{1,0:T(8,128)(2,1)S(1)}, u32[]{:S(2)}, u32[]{:S(2)}) collective-permute-start(bf16[64,640]{1,0:T(8,128)(2,1)S(1)} %maximum_bitcast_fusion), channel_id=1, source_target_pairs={{1,2},{3,4},{5,6},{7,0},{2,1},{4,3},{6,5},{0,7},{9,10},{11,12},{13... | collective-permute-start | bytes 245768 | tf_op jit(solution)/shard_map/ppermute | solution.py:543
  15.1 0.7 %collective-permute-start.5 = (bf16[64,640]{1,0:T(8,128)(2,1)S(1)}, bf16[64,640]{1,0:T(8,128)(2,1)S(1)}, u32[]{:S(2)}, u32[]{:S(2)}) collective-permute-start(bf16[64,640]{1,0:T(8,128)(2,1)S(1)} %maximum_bitcast_fusion.1), channel_id=1, source_target_pairs={{0,1},{2,3},{4,5},{6,7},{1,0},{3,2},{5,4},{7,6},{8,9},{10,11},{12,... | collective-permute-start | bytes 245768 | tf_op jit(solution)/shard_map/ppermute | solution.py:543
  15.8 0.0 collective-permute-done.2.lon_b
  15.8 0.0 collective-permute-done.3.lon_a
  15.8 3.2 %rim.1 = (bf16[320,256]{1,0:T(8,128)(2,1)S(1)}, bf16[8,64,640]{2,1,0:T(8,128)(2,1)S(1)}, bf16[2,16,16,640]{3,2,1,0:T(8,128)(2,1)S(1)}, bf16[2,16,16,640]{3,2,1,0:T(8,128)(2,1)S(1)}) custom-call(bf16[24,64,640]{2,1,0:T(8,128)(2,1)S(1)} %copy-done, bf16[33,8,640]{2,1,0:T(8,128)(2,1)S(1)} %collective-permute-done.lat_a, ...), custom_call_target="tpu_custom_call" | custom-call | flops 2831155200 | bytes 3932160 | tf_op jit(solution)/shard_map/rim/pallas_call | solution.py:548
  19.0 0.3 %collective-permute-done.4.corner_b = bf16[64,640]{1,0:T(8,128)(2,1)S(1)} collective-permute-done((bf16[64,640]{1,0:T(8,128)(2,1)S(1)}, bf16[64,640]{1,0:T(8,128)(2,1)S(1)}, u32[]{:S(2)}, u32[]{:S(2)}) %collective-permute-start.4) | collective-permute-done | bytes 81952 | tf_op jit(solution)/shard_map/ppermute | solution.py:543
  19.3 0.0 collective-permute-done.5.corner_a
  19.3 1.7 %corner.1 = bf16[24,64,640]{2,1,0:T(8,128)(2,1)} custom-call(bf16[24,64,640]{2,1,0:T(8,128)(2,1)S(1)} %copy-done, bf16[33,8,640]{2,1,0:T(8,128)(2,1)S(1)} %collective-permute-done.lat_a, bf16[33,8,640]{2,1,0:T(8,128)(2,1)S(1)} %collective-permute-done.1.lat_b, bf16[24,8,640]{2,1,0:T(8,128)(2,1)S(1)} %collective-permute-done.2.lon_b, ...), custom_call_target="tpu_custom_call", output_to_operand_aliasing={{}: (14, {})} | custom-call | flops 2831155200 | bytes 3932160 | tf_op jit(solution)/shard_map/corner/pallas_call | solution.py:567
  (5 shorter events, 0.1 us)
Async XLA Ops:
  0.0 8.1 %copy-start = (bf16[24,64,640]{2,1,0:T(8,128)(2,1)S(1)}, bf16[24,64,640]{2,1,0:T(8,128)(2,1)}, u32[]{:S(2)}) copy-start(bf16[24,64,640]{2,1,0:T(8,128)(2,1)} %x_ref.5) | copy-start | bytes 5898244
  0.0 8.1 %copy-start.1 = (f32[24,5,5,9]{0,2,3,1:T(8,128)S(1)}, f32[24,5,5,9]{0,2,3,1:T(8,128)}, u32[]{:S(2)}) copy-start(f32[24,5,5,9]{0,2,3,1:T(8,128)} %param.7) | copy-start | bytes 64804
  0.0 8.1 %copy-start.2 = (s32[24,5]{0,1:T(8,128)S(1)}, s32[24,5]{0,1:T(8,128)}, u32[]{:S(2)}) copy-start(s32[24,5]{0,1:T(8,128)} %param.9) | copy-start | bytes 1444
  0.0 8.2 %copy-start.3 = (s32[24,2]{0,1:T(2,128)S(1)}, s32[24,2]{0,1:T(2,128)}, u32[]{:S(2)}) copy-start(s32[24,2]{0,1:T(2,128)} %param.8) | copy-start | bytes 580
  0.0 8.2 %copy-start.4 = (f32[5,640]{1,0:T(8,128)S(1)}, f32[5,640]{1,0:T(8,128)}, u32[]{:S(2)}) copy-start(f32[5,640]{1,0:T(8,128)} %one_ref.5) | copy-start | bytes 38404
  0.0 8.2 %copy-start.5 = (f32[5,640]{1,0:T(8,128)S(1)}, f32[5,640]{1,0:T(8,128)}, u32[]{:S(2)}) copy-start(f32[5,640]{1,0:T(8,128)} %two_ref.5) | copy-start | bytes 38404
  2.5 11.2 %collective-permute-start = (bf16[33,8,640]{2,1,0:T(8,128)(2,1)}, bf16[33,8,640]{2,1,0:T(8,128)(2,1)S(1)}, u32[]{:S(2)}, u32[]{:S(2)}) collective-permute-start(bf16[33,8,640]{2,1,0:T(8,128)(2,1)} %get-tuple-element.23), channel_id=1, source_target_pairs={{0,8},{1,9},{2,10},{3,11},{4,12},{5,13},{6,14},{7,15},{16,24},{17,... | collective-permute-start | bytes 1013768 | tf_op jit(solution)/shard_map/ppermute | solution.py:510
  5.6 8.1 %collective-permute-start.1 = (bf16[33,8,640]{2,1,0:T(8,128)(2,1)}, bf16[33,8,640]{2,1,0:T(8,128)(2,1)S(1)}, u32[]{:S(2)}, u32[]{:S(2)}) collective-permute-start(bf16[33,8,640]{2,1,0:T(8,128)(2,1)} %get-tuple-element.24), channel_id=1, source_target_pairs={{8,16},{9,17},{10,18},{11,19},{12,20},{13,21},{14,22},{15,23},{16,... | collective-permute-start | bytes 1013768 | tf_op jit(solution)/shard_map/ppermute | solution.py:511
  5.6 10.2 %collective-permute-start.2 = (bf16[24,8,640]{2,1,0:T(8,128)(2,1)}, bf16[24,8,640]{2,1,0:T(8,128)(2,1)S(1)}, u32[]{:S(2)}, u32[]{:S(2)}) collective-permute-start(bf16[24,8,640]{2,1,0:T(8,128)(2,1)} %get-tuple-element.28), channel_id=1, source_target_pairs={{1,2},{3,4},{5,6},{7,0},{2,1},{4,3},{6,5},{0,7},{9,10},{11,12},{13... | collective-permute-start | bytes 737288 | tf_op jit(solution)/shard_map/ppermute | solution.py:512
  8.1 7.6 %collective-permute-start.3 = (bf16[24,8,640]{2,1,0:T(8,128)(2,1)}, bf16[24,8,640]{2,1,0:T(8,128)(2,1)S(1)}, u32[]{:S(2)}, u32[]{:S(2)}) collective-permute-start(bf16[24,8,640]{2,1,0:T(8,128)(2,1)} %get-tuple-element.29), channel_id=1, source_target_pairs={{0,1},{2,3},{4,5},{6,7},{1,0},{3,2},{5,4},{7,6},{8,9},{10,11},{12,... | collective-permute-start | bytes 737288 | tf_op jit(solution)/shard_map/ppermute | solution.py:513
  13.9 5.4 %collective-permute-start.4 = (bf16[64,640]{1,0:T(8,128)(2,1)S(1)}, bf16[64,640]{1,0:T(8,128)(2,1)S(1)}, u32[]{:S(2)}, u32[]{:S(2)}) collective-permute-start(bf16[64,640]{1,0:T(8,128)(2,1)S(1)} %maximum_bitcast_fusion), channel_id=1, source_target_pairs={{1,2},{3,4},{5,6},{7,0},{2,1},{4,3},{6,5},{0,7},{9,10},{11,12},{13... | collective-permute-start | bytes 245768 | tf_op jit(solution)/shard_map/ppermute | solution.py:543
  15.1 4.2 %collective-permute-start.5 = (bf16[64,640]{1,0:T(8,128)(2,1)S(1)}, bf16[64,640]{1,0:T(8,128)(2,1)S(1)}, u32[]{:S(2)}, u32[]{:S(2)}) collective-permute-start(bf16[64,640]{1,0:T(8,128)(2,1)S(1)} %maximum_bitcast_fusion.1), channel_id=1, source_target_pairs={{0,1},{2,3},{4,5},{6,7},{1,0},{3,2},{5,4},{7,6},{8,9},{10,11},{12,... | collective-permute-start | bytes 245768 | tf_op jit(solution)/shard_map/ppermute | solution.py:543

commit v7 on v6

--- a/solution.py
+++ b/solution.py
@@ -17,6 +17,7 @@
 DEPTH = 2 * LANES
 TILE = 16
 VMEM_BYTES = 20 * 1024 * 1024
+TURNS = 3
 PIECE = 4
 F32, BF16 = jnp.float32, jnp.bfloat16
 
@@ -44,8 +45,8 @@
     return pairs + [(j, i) for i, j in pairs]
 
 
-def lat_swaps(peers, width, second):
-    pairs = [(i, i + 1) for i in range(1 if second else 0, peers - 1, 2)]
+def turn_swaps(peers, width, turn):
+    pairs = [(i, i + 1) for i in range(peers - 1) if i % TURNS == turn]
     pairs += [(j, i) for i, j in pairs]
     alone = set(range(peers)) - {i for i, _ in pairs}
     result = [(i * width + k, j * width + k) for i, j in pairs for k in range(width)]
@@ -132,29 +133,31 @@
 
 
 def prep_kernel(
-    flat_ref, groups_ref, filter_in, edge_in, mask_in, lat_a, lat_b, lon_a, lon_b,
-    filter_ref, edge_ref, mask_ref, ends, sides, padded, tags, packed, sems, out_sems,
+    flat_ref, groups_ref, filter_in, edge_in, mask_in, turn_0, turn_1, turn_2, lon_b,
+    filter_ref, edge_ref, mask_ref, payloads, far, padded, tags, sems, out_sems,
 ):
     bases, lags, bands, rows = filter_in.shape
     across = groups_ref.shape[1]
     edge = REACH * across
-    lat_odd, lon_odd = lax.axis_index("lat") % 2, lax.axis_index("lon") % 2
-    firsts = (1 - lat_odd, lat_odd)
+    turn, lon_odd = lax.axis_index("lat") % TURNS, lax.axis_index("lon") % 2
     small = [
         pltpu.make_async_copy(filter_in, filter_ref, sems.at[0]),
         pltpu.make_async_copy(edge_in, edge_ref, sems.at[1]),
         pltpu.make_async_copy(mask_in, mask_ref, sems.at[2]),
     ]
-    rows_in, cells_in = [], []
-    for i in range(2):
-        place = pl.ds(firsts[i] * (rows - REACH) * across, edge)
-        rows_in.append(pltpu.make_async_copy(flat_ref.at[place], ends.at[i], sems.at[3 + i]))
-        place = (1 - lon_odd if i == 0 else lon_odd) * (across - 1)
-        cells_in.append(pltpu.make_async_copy(groups_ref.at[:, place], sides.at[i], sems.at[5 + i]))
-    for copy in rows_in + small + cells_in:
+    last, first = pl.ds((rows - REACH) * across, edge), pl.ds(0, edge)
+    near_at, far_at = (1 - lon_odd) * (across - 1), lon_odd * (across - 1)
+    copies = [
+        pltpu.make_async_copy(flat_ref.at[last], payloads.at[0, pl.ds(0, edge)], sems.at[3]),
+        pltpu.make_async_copy(flat_ref.at[first], payloads.at[1, pl.ds(0, edge)], sems.at[4]),
+        pltpu.make_async_copy(groups_ref.at[:, near_at], payloads.at[2, pl.ds(0, rows)], sems.at[5]),
+        pltpu.make_async_copy(groups_ref.at[:, far_at], far, sems.at[6]),
+    ]
+    for copy in copies[:2] + small + copies[2:]:
         copy.start()
     padded[...] = jnp.zeros_like(padded)
     tags[...] = jnp.zeros_like(tags)
+    payloads[2, rows:] = jnp.zeros((edge + 1 - rows,) + payloads.shape[2:], BF16)
     chosen = line_choice(lags)
     pending = []
 
@@ -162,22 +165,22 @@
         pending.append(pltpu.make_async_copy(source, target, out_sems.at[len(pending)]))
         pending[-1].start()
 
-    for i, out in enumerate((lat_a, lat_b)):
-        rows_in[i].wait()
-        send(ends.at[i], out.at[pl.ds(0, edge)])
+    outs = [(out, (turn + TURNS - j) % TURNS) for j, out in enumerate((turn_0, turn_1, turn_2))]
+    for copy in copies[:3]:
+        copy.wait()
+    for out, role in outs:
+        send(payloads.at[role, pl.ds(0, edge)], out.at[pl.ds(0, edge)])
+    copies[3].wait()
+    send(far, lon_b)
     for copy in small:
         copy.wait()
     for k, line in enumerate(filter_lines(filter_ref, edge_ref, mask_ref, padded, chosen)):
-        tags[0, :LAT_REACH, lanes_of(k)] = line[:LAT_REACH]
-        tags[1, :LAT_REACH, lanes_of(k)] = line[rows - LAT_REACH : rows]
-    odd = lat_odd == 1
-    packed[0] = jnp.where(odd, tags[0], tags[1]).astype(BF16)
-    packed[1] = jnp.where(odd, tags[1], tags[0]).astype(BF16)
-    for i, out in enumerate((lat_a, lat_b)):
-        send(packed.at[i], out.at[edge])
-    for i, out in enumerate((lon_a, lon_b)):
-        cells_in[i].wait()
-        send(sides.at[i], out)
+        tags[0, :LAT_REACH, lanes_of(k)] = line[rows - LAT_REACH : rows]
+        tags[1, :LAT_REACH, lanes_of(k)] = line[:LAT_REACH]
+    payloads[0, edge] = tags[0].astype(BF16)
+    payloads[1, edge] = tags[1].astype(BF16)
+    for out, role in outs:
+        send(payloads.at[role, edge], out.at[edge])
     for copy in pending:
         copy.wait()
 
@@ -272,12 +275,24 @@
     return jnp.where(odd, a, b), jnp.where(odd, b, a)
 
 
-def parities():
-    return lax.axis_index("lat") % 2 == 1, lax.axis_index("lon") % 2 == 1
+def pick(received, turn):
+    value = received[-1].astype(F32)
+    for j in range(TURNS - 1):
+        value = jnp.where(turn == j, received[j].astype(F32), value)
+    return value
+
+
+def below_and_above(received):
+    turn = lax.axis_index("lat") % TURNS
+    return pick(received, (turn + TURNS - 1) % TURNS), pick(received, turn)
+
+
+def in_chip(received):
+    return pick(received, (lax.axis_index("lat") + 1) % TURNS)
 
 
 def rim_kernel(
-    block, x_ref, lat_a, lat_b, lon_b, lon_a, rows_in, cells_in, sides_in,
+    block, x_ref, turn_0, turn_1, turn_2, lon_b, rows_in, cells_in, sides_in,
     toeplitz, known_toeplitz, wide_toeplitz, one_ref, two_ref,
     rim_toeplitz, rim_out, side_out, ends, field, hidden,
 ):
@@ -287,9 +302,9 @@
     group = bases * CELLS
     edge = REACH * (cells // CELLS)
     columns = cells // CELLS + 1
-    lat_odd, lon_odd = parities()
+    turns, lon_odd = (turn_0, turn_1, turn_2), lax.axis_index("lon") % 2 == 1
     one, two = lane_weights(one_ref, 0.5), lane_weights(two_ref)
-    tags = ordered(lat_odd, lat_a[edge], lat_b[edge])
+    tags = below_and_above([v[edge] for v in turns])
 
     def tag_line(r, k):
         at = r % LAT_REACH
@@ -301,8 +316,8 @@
 
     def load(c):
         lanes = lanes_of(c)
-        lat = ordered(lat_odd, lat_a[:edge, :, lanes], lat_b[:edge, :, lanes])
-        lon = ordered(lon_odd, lon_a[:, :, lanes], lon_b[:, :, lanes])
+        lat = below_and_above([v[:edge, :, lanes] for v in turns])
+        lon = ordered(lon_odd, in_chip([v[:rows, :, lanes] for v in turns]), lon_b[:, :, lanes])
         inner = slice(REACH, rows - REACH)
         blank = jnp.zeros((REACH, CELLS, LANES), F32)
         for side in range(2):
@@ -393,7 +408,7 @@
 
 
 def corner_kernel(
-    x_ref, lat_a, lat_b, lon_b, lon_a, corner_b, corner_a, ends, rim_toeplitz, wide_toeplitz, one_ref, two_ref,
+    x_ref, turn_0, turn_1, turn_2, lon_b, corner_b, corner_a, ends, rim_toeplitz, wide_toeplitz, one_ref, two_ref,
     side_out, rim_out, begun_ref, out_ref, corner_out, sems,
 ):
     del begun_ref
@@ -411,13 +426,13 @@
     copies = [pltpu.make_async_copy(source, target, sems.at[i]) for i, (source, target) in enumerate(moves)]
     for copy in copies:
         copy.start()
-    lat_odd, lon_odd = parities()
+    turns, lon_odd = (turn_0, turn_1, turn_2), lax.axis_index("lon") % 2 == 1
     one, two = lane_weights(one_ref, 0.5), lane_weights(two_ref)
 
     def first(c):
         lanes = lanes_of(c)
-        lat = ordered(lat_odd, lat_a[:edge, :, lanes], lat_b[:edge, :, lanes])
-        lon = ordered(lon_odd, lon_a[:, :, lanes], lon_b[:, :, lanes])
+        lat = below_and_above([v[:edge, :, lanes] for v in turns])
+        lon = ordered(lon_odd, in_chip([v[:rows, :, lanes] for v in turns]), lon_b[:, :, lanes])
         corner = ordered(lon_odd, corner_a[:, lanes], corner_b[:, lanes])
         tall = []
         for side in range(2):
@@ -427,8 +442,7 @@
             half = slice(side * (TILE - CELLS), side * (TILE - CELLS) + CELLS)
             mine = [x_ref[r : r + REACH, tiles, lanes].astype(F32)[:, half] for r in (0, rows - REACH)]
             near = lon[side]
-            far = ordered(lat_odd, corner[side][: REACH * CELLS], corner[side][REACH * CELLS :])
-            far = [v.reshape(REACH, CELLS, LANES) for v in far]
+            far = corner[side].reshape(2, REACH, CELLS, LANES)
             own = jnp.concatenate([above[0], mine[0], mine[1], above[1]], 0)
             other = jnp.concatenate([far[0], near[:REACH], near[rows - REACH :], far[1]], 0)
             tall.append(jnp.concatenate([own, other] if side else [other, own], 1))
@@ -471,7 +485,7 @@
     chunks = channels // LANES
     block = max(b for b in range(2, rows + 1, 2) if rows % b == 0 and (b + REACH) * WINDOW <= DEPTH)
     lat_peers, lon_peers = lax.axis_size("lat"), lax.axis_size("lon")
-    lon = lax.axis_index("lon")
+    turn, lon = lax.axis_index("lat") % TURNS, lax.axis_index("lon")
 
     anywhere = pl.BlockSpec(memory_space=pl.ANY)
     vmem = pl.BlockSpec(memory_space=pltpu.VMEM)
@@ -487,17 +501,17 @@
     across = cells // CELLS
     edge = REACH * across
     filter_args = (filters.transpose(1, 3, 2, 0), band_edges.T, basis_mask.T)
-    lat_a, lat_b, lon_a, lon_b = pl.pallas_call(
+    *turns, lon_b = pl.pallas_call(
         prep_kernel,
-        out_shape=(array(edge + 1, CELLS, channels),) * 2 + (array(rows, CELLS, channels),) * 2,
+        out_shape=(array(edge + 1, CELLS, channels),) * TURNS + (array(rows, CELLS, channels),),
         in_specs=[anywhere] * 5,
-        out_specs=(anywhere,) * 4,
+        out_specs=(anywhere,) * (TURNS + 1),
         scratch_shapes=[
             scratch(bases, filters.shape[3], BANDS, rows, dtype=F32),
             scratch(2, rows, dtype=jnp.int32), scratch(bases, rows, dtype=jnp.int32),
-            scratch(2, edge, CELLS, channels), scratch(2, rows, CELLS, channels),
+            scratch(TURNS, edge + 1, CELLS, channels), scratch(rows, CELLS, channels),
             scratch(bases, LANES, LANES, dtype=F32), scratch(2, CELLS, channels, dtype=F32),
-            scratch(2, CELLS, channels), dma((7,)), dma((6,)),
+            dma((7,)), dma((2 * TURNS + 1,)),
         ],
         compiler_params=pltpu.CompilerParams(vmem_limit_bytes=60 * 1024 * 1024),
         cost_estimate=pl.CostEstimate(flops=0, bytes_accessed=8 * REACH * cells * channels, transcendentals=0),
@@ -507,10 +521,8 @@
         *filter_args,
     )
     both = ("lat", "lon")
-    lat_a = lax.ppermute(lat_a, both, lat_swaps(lat_peers, lon_peers, False))
-    lat_b = lax.ppermute(lat_b, both, lat_swaps(lat_peers, lon_peers, True))
+    turns = [lax.ppermute(v, both, turn_swaps(lat_peers, lon_peers, j)) for j, v in enumerate(turns)]
     lon_b = lax.ppermute(lon_b, "lon", swaps(lon_peers, True))
-    lon_a = lax.ppermute(lon_a, "lon", swaps(lon_peers, False))
 
     middle = rows - 2 * REACH
     flops = 2 * (2 * rows - 3 * REACH) * (cells - 2 * CELLS) * bases * DEPTH * channels
@@ -535,14 +547,17 @@
         name="inner",
     )(state_field, *filter_args, weights_one, weights_two)
 
+    *turns, sides = lax.optimization_barrier((*turns, sides))
+
     def corner_send(leading, second):
         start = jnp.where(leading, 0, cells - CELLS)
-        joined = [v[:edge].reshape(REACH, cells, channels) for v in (lat_a, lat_b)]
-        parts = [lax.dynamic_slice_in_dim(v, start, CELLS, 1) for v in joined]
-        sent = jnp.concatenate(parts, 0).reshape(2 * REACH * CELLS, channels)
+        parts = [v[:edge].reshape(REACH, cells, channels) for v in turns]
+        parts = [lax.dynamic_slice_in_dim(v, start, CELLS, 1) for v in parts]
+        below = jnp.where(turn == 1, parts[0], jnp.where(turn == 2, parts[1], parts[2]))
+        above = jnp.where(turn == 0, parts[0], jnp.where(turn == 1, parts[1], parts[2]))
+        sent = jnp.concatenate([below, above], 0).reshape(2 * REACH * CELLS, channels)
         return lax.ppermute(sent, "lon", swaps(lon_peers, second))
 
-    lat_a, lat_b, sides = lax.optimization_barrier((lat_a, lat_b, sides))
     corner_b = corner_send(lon % 2 == 0, True)
     corner_a = corner_send(lon % 2 == 1, False)
     rim_toeplitz, rim_out, side_out, ends = pl.pallas_call(
@@ -561,7 +576,7 @@
         cost_estimate=cost,
         name="rim",
     )(
-        state_field, lat_a, lat_b, lon_b, lon_a, edge_rows, edge_cells, sides,
+        state_field, *turns, lon_b, edge_rows, edge_cells, sides,
         toeplitz, known, wide, weights_one, weights_two,
     )
     return pl.pallas_call(
@@ -575,7 +590,7 @@
         cost_estimate=cost,
         name="corner",
     )(
-        state_field, lat_a, lat_b, lon_b, lon_a, corner_b, corner_a, ends, rim_toeplitz, wide,
+        state_field, *turns, lon_b, corner_b, corner_a, ends, rim_toeplitz, wide,
         weights_one, weights_two, side_out, rim_out, begun,
     )
 

time: 21.3 us -> 21.3 us (level)
    ppermute x1, starting transfers between devices: 2.56 us -> 2.05 us  [per_device(): lon_b = lax.ppermute(lon_b, 'lon', swaps(lon_peers, True))]
    ppermute x3, starting transfers between devices: 3.11 us -> 3.61 us  [per_device(): lax.ppermute(v, both, turn_swaps(lat_peers, lon_peers, j))]
where the time goes in v7:
time: 21.3 us; the launch traced here: 21.2 us
  Pallas kernels  12.9 us (61%)
  starting transfers between devices  7.57 us (36%)
  waiting for transfers between devices  0.39 us (2%)
    pallas_call x1, Pallas kernels, per_device(): pl.pallas_call(functools.partial(inner_kernel, block), out_shape=(array(r...  5.36 us
    ppermute x3, starting transfers between devices, per_device(): lax.ppermute(v, both, turn_swaps(lat_peers, lon_peers, j))  3.61 us
    pallas_call x1, Pallas kernels, per_device(): pl.pallas_call(functools.partial(rim_kernel, block), out_shape=(array(2 *...  3.31 us
    pallas_call x1, Pallas kernels, per_device(): pl.pallas_call(prep_kernel, out_shape=(array(edge + 1, CELLS, channels),)...  2.53 us
    ppermute x1, starting transfers between devices, per_device(): lon_b = lax.ppermute(lon_b, 'lon', swaps(lon_peers, True))  2.05 us
    ppermute x2, starting transfers between devices, corner_send(): return lax.ppermute(sent, 'lon', swaps(lon_peers, second))  1.9 us
    pallas_call x1, Pallas kernels, per_device(): pl.pallas_call(corner_kernel, out_shape=array(rows, cells, channels), in_...  1.71 us
  transfers between devices with their start and end apart: 6, of which 2 were waited for; matrix products, arithmetic and copies ran while one was open for 1% of the time, Pallas kernels for 41%

profile of v7, /device:TPU:0, one launch (start us, length us, event | category | flops | bytes accessed | tf_op | source)
XLA Modules:
  0.0 21.2 jit_solution(7287470081695026219)
XLA Ops:
  0.0 0.0 copy-start
  0.0 0.0 copy-start.1
  0.0 0.0 copy-start.2
  0.0 0.0 copy-start.3
  0.0 0.0 copy-start.4
  0.0 0.0 copy-start.5
  0.0 2.5 %prep.1 = (bf16[33,8,640]{2,1,0:T(8,128)(2,1)}, bf16[33,8,640]{2,1,0:T(8,128)(2,1)}, bf16[33,8,640]{2,1,0:T(8,128)(2,1)}, bf16[24,8,640]{2,1,0:T(8,128)(2,1)}) custom-call(bf16[192,8,640]{2,1,0:T(8,128)(2,1)} %bitcast.12, bf16[24,8,8,640]{3,2,1,0:T(8,128)(2,1)} %bitcast.13, f32[5,9,5,24]{3,2,1,0:T(8,128)} %bitcast.14, s32[2,24]{1,0:T(2,128)} %bitcast.18, ...), custom_call_target="tpu_custom_call" | custom-call | bytes 1310720 | tf_op jit(solution)/shard_map/prep/pallas_call | solution.py:504
  2.6 3.1 %collective-permute-start = (bf16[33,8,640]{2,1,0:T(8,128)(2,1)}, bf16[33,8,640]{2,1,0:T(8,128)(2,1)S(1)}, u32[]{:S(2)}, u32[]{:S(2)}) collective-permute-start(bf16[33,8,640]{2,1,0:T(8,128)(2,1)} %get-tuple-element.24), channel_id=1, source_target_pairs={{0,8},{1,9},{2,10},{3,11},{4,12},{5,13},{6,14},{7,15},{8,0},{9,1},... | collective-permute-start | bytes 1013768 | tf_op jit(solution)/shard_map/ppermute | solution.py:524
  5.7 0.0 collective-permute-start.1
  5.7 0.5 %collective-permute-start.2 = (bf16[33,8,640]{2,1,0:T(8,128)(2,1)}, bf16[33,8,640]{2,1,0:T(8,128)(2,1)S(1)}, u32[]{:S(2)}, u32[]{:S(2)}) collective-permute-start(bf16[33,8,640]{2,1,0:T(8,128)(2,1)} %get-tuple-element.26), channel_id=1, source_target_pairs={{16,24},{17,25},{18,26},{19,27},{20,28},{21,29},{22,30},{23,31},{2... | collective-permute-start | bytes 1013768 | tf_op jit(solution)/shard_map/ppermute | solution.py:524
  6.2 2.1 %collective-permute-start.3 = (bf16[24,8,640]{2,1,0:T(8,128)(2,1)}, bf16[24,8,640]{2,1,0:T(8,128)(2,1)S(1)}, u32[]{:S(2)}, u32[]{:S(2)}) collective-permute-start(bf16[24,8,640]{2,1,0:T(8,128)(2,1)} %get-tuple-element.31), channel_id=1, source_target_pairs={{1,2},{3,4},{5,6},{7,0},{2,1},{4,3},{6,5},{0,7},{9,10},{11,12},{13... | collective-permute-start | bytes 737288 | tf_op jit(solution)/shard_map/ppermute | solution.py:525
  8.2 0.0 copy-done
  8.2 0.0 copy-done.1
  8.2 0.0 copy-done.2
  8.2 0.0 copy-done.3
  8.2 0.0 copy-done.4
  8.2 0.0 copy-done.5
  8.3 5.4 %inner.1 = (bf16[960,256]{1,0:T(8,128)(2,1)S(1)}, bf16[320,256]{1,0:T(8,128)(2,1)S(1)}, bf16[320,256]{1,0:T(8,128)(2,1)S(1)}, bf16[8,64,640]{2,1,0:T(8,128)(2,1)...) custom-call(bf16[24,64,640]{2,1,0:T(8,128)(2,1)S(1)} %copy-done, ...), custom_call_target="tpu_custom_call" | custom-call | flops 2831155200 | bytes 3932160 | tf_op jit(solution)/shard_map/inner/pallas_call | solution.py:530
  13.6 0.2 collective-permute-done.turn_0
  13.8 0.0 collective-permute-done.1.turn_1
  13.8 0.0 collective-permute-done.2.turn_2
  13.9 0.1 select_select_fusion.1
  14.0 1.2 %collective-permute-start.4 = (bf16[64,640]{1,0:T(8,128)(2,1)S(1)}, bf16[64,640]{1,0:T(8,128)(2,1)S(1)}, u32[]{:S(2)}, u32[]{:S(2)}) collective-permute-start(bf16[64,640]{1,0:T(8,128)(2,1)S(1)} %maximum_bitcast_fusion), channel_id=1, source_target_pairs={{1,2},{3,4},{5,6},{7,0},{2,1},{4,3},{6,5},{0,7},{9,10},{11,12},{13... | collective-permute-start | bytes 245768 | tf_op jit(solution)/shard_map/ppermute | solution.py:559
  15.3 0.7 %collective-permute-start.5 = (bf16[64,640]{1,0:T(8,128)(2,1)S(1)}, bf16[64,640]{1,0:T(8,128)(2,1)S(1)}, u32[]{:S(2)}, u32[]{:S(2)}) collective-permute-start(bf16[64,640]{1,0:T(8,128)(2,1)S(1)} %maximum_bitcast_fusion.1), channel_id=1, source_target_pairs={{0,1},{2,3},{4,5},{6,7},{1,0},{3,2},{5,4},{7,6},{8,9},{10,11},{12,... | collective-permute-start | bytes 245768 | tf_op jit(solution)/shard_map/ppermute | solution.py:559
  15.9 0.0 collective-permute-done.3.lon_b
  15.9 3.3 %rim.1 = (bf16[320,256]{1,0:T(8,128)(2,1)S(1)}, bf16[8,64,640]{2,1,0:T(8,128)(2,1)S(1)}, bf16[2,16,16,640]{3,2,1,0:T(8,128)(2,1)S(1)}, bf16[2,16,16,640]{3,2,1,0:T(8,128)(2,1)S(1)}) custom-call(bf16[24,64,640]{2,1,0:T(8,128)(2,1)S(1)} %copy-done, bf16[33,8,640]{2,1,0:T(8,128)(2,1)S(1)} %collective-permute-done.turn_0, ...), custom_call_target="tpu_custom_call" | custom-call | flops 2831155200 | bytes 3932160 | tf_op jit(solution)/shard_map/rim/pallas_call | solution.py:563
  19.2 0.2 collective-permute-done.4.corner_b
  19.4 0.0 collective-permute-done.5.corner_a
  19.4 1.7 %corner.1 = bf16[24,64,640]{2,1,0:T(8,128)(2,1)} custom-call(bf16[24,64,640]{2,1,0:T(8,128)(2,1)S(1)} %copy-done, bf16[33,8,640]{2,1,0:T(8,128)(2,1)S(1)} %collective-permute-done.turn_0, bf16[33,8,640]{2,1,0:T(8,128)(2,1)S(1)} %collective-permute-done.1.turn_1, ...), custom_call_target="tpu_custom_call", output_to_operand_aliasing={{}: (14, {})} | custom-call | flops 2831155200 | bytes 3932160 | tf_op jit(solution)/shard_map/corner/pallas_call | solution.py:582
  (5 shorter events, 0.1 us)
Async XLA Ops:
  0.0 8.2 %copy-start = (bf16[24,64,640]{2,1,0:T(8,128)(2,1)S(1)}, bf16[24,64,640]{2,1,0:T(8,128)(2,1)}, u32[]{:S(2)}) copy-start(bf16[24,64,640]{2,1,0:T(8,128)(2,1)} %x_ref.5) | copy-start | bytes 5898244
  0.0 8.2 %copy-start.1 = (f32[24,5,5,9]{0,2,3,1:T(8,128)S(1)}, f32[24,5,5,9]{0,2,3,1:T(8,128)}, u32[]{:S(2)}) copy-start(f32[24,5,5,9]{0,2,3,1:T(8,128)} %param.7) | copy-start | bytes 64804
  0.0 8.2 %copy-start.2 = (s32[24,5]{0,1:T(8,128)S(1)}, s32[24,5]{0,1:T(8,128)}, u32[]{:S(2)}) copy-start(s32[24,5]{0,1:T(8,128)} %param.9) | copy-start | bytes 1444
  0.0 8.2 %copy-start.3 = (s32[24,2]{0,1:T(2,128)S(1)}, s32[24,2]{0,1:T(2,128)}, u32[]{:S(2)}) copy-start(s32[24,2]{0,1:T(2,128)} %param.8) | copy-start | bytes 580
  0.0 8.2 %copy-start.4 = (f32[5,640]{1,0:T(8,128)S(1)}, f32[5,640]{1,0:T(8,128)}, u32[]{:S(2)}) copy-start(f32[5,640]{1,0:T(8,128)} %one_ref.5) | copy-start | bytes 38404
  0.0 8.2 %copy-start.5 = (f32[5,640]{1,0:T(8,128)S(1)}, f32[5,640]{1,0:T(8,128)}, u32[]{:S(2)}) copy-start(f32[5,640]{1,0:T(8,128)} %two_ref.5) | copy-start | bytes 38404
  2.6 11.2 %collective-permute-start = (bf16[33,8,640]{2,1,0:T(8,128)(2,1)}, bf16[33,8,640]{2,1,0:T(8,128)(2,1)S(1)}, u32[]{:S(2)}, u32[]{:S(2)}) collective-permute-start(bf16[33,8,640]{2,1,0:T(8,128)(2,1)} %get-tuple-element.24), channel_id=1, source_target_pairs={{0,8},{1,9},{2,10},{3,11},{4,12},{5,13},{6,14},{7,15},{8,0},{9,1},... | collective-permute-start | bytes 1013768 | tf_op jit(solution)/shard_map/ppermute | solution.py:524
  5.7 8.1 %collective-permute-start.1 = (bf16[33,8,640]{2,1,0:T(8,128)(2,1)}, bf16[33,8,640]{2,1,0:T(8,128)(2,1)S(1)}, u32[]{:S(2)}, u32[]{:S(2)}) collective-permute-start(bf16[33,8,640]{2,1,0:T(8,128)(2,1)} %get-tuple-element.25), channel_id=1, source_target_pairs={{8,16},{9,17},{10,18},{11,19},{12,20},{13,21},{14,22},{15,23},{16,... | collective-permute-start | bytes 1013768 | tf_op jit(solution)/shard_map/ppermute | solution.py:524
  5.7 8.1 %collective-permute-start.2 = (bf16[33,8,640]{2,1,0:T(8,128)(2,1)}, bf16[33,8,640]{2,1,0:T(8,128)(2,1)S(1)}, u32[]{:S(2)}, u32[]{:S(2)}) collective-permute-start(bf16[33,8,640]{2,1,0:T(8,128)(2,1)} %get-tuple-element.26), channel_id=1, source_target_pairs={{16,24},{17,25},{18,26},{19,27},{20,28},{21,29},{22,30},{23,31},{2... | collective-permute-start | bytes 1013768 | tf_op jit(solution)/shard_map/ppermute | solution.py:524
  6.2 9.8 %collective-permute-start.3 = (bf16[24,8,640]{2,1,0:T(8,128)(2,1)}, bf16[24,8,640]{2,1,0:T(8,128)(2,1)S(1)}, u32[]{:S(2)}, u32[]{:S(2)}) collective-permute-start(bf16[24,8,640]{2,1,0:T(8,128)(2,1)} %get-tuple-element.31), channel_id=1, source_target_pairs={{1,2},{3,4},{5,6},{7,0},{2,1},{4,3},{6,5},{0,7},{9,10},{11,12},{13... | collective-permute-start | bytes 737288 | tf_op jit(solution)/shard_map/ppermute | solution.py:525
  14.0 5.4 %collective-permute-start.4 = (bf16[64,640]{1,0:T(8,128)(2,1)S(1)}, bf16[64,640]{1,0:T(8,128)(2,1)S(1)}, u32[]{:S(2)}, u32[]{:S(2)}) collective-permute-start(bf16[64,640]{1,0:T(8,128)(2,1)S(1)} %maximum_bitcast_fusion), channel_id=1, source_target_pairs={{1,2},{3,4},{5,6},{7,0},{2,1},{4,3},{6,5},{0,7},{9,10},{11,12},{13... | collective-permute-start | bytes 245768 | tf_op jit(solution)/shard_map/ppermute | solution.py:559
  15.3 4.2 %collective-permute-start.5 = (bf16[64,640]{1,0:T(8,128)(2,1)S(1)}, bf16[64,640]{1,0:T(8,128)(2,1)S(1)}, u32[]{:S(2)}, u32[]{:S(2)}) collective-permute-start(bf16[64,640]{1,0:T(8,128)(2,1)S(1)} %maximum_bitcast_fusion.1), channel_id=1, source_target_pairs={{0,1},{2,3},{4,5},{6,7},{1,0},{3,2},{5,4},{7,6},{8,9},{10,11},{12,... | collective-permute-start | bytes 245768 | tf_op jit(solution)/shard_map/ppermute | solution.py:559

commit v8 on v7

--- a/solution.py
+++ b/solution.py
@@ -101,11 +101,12 @@
 def run_mixed(steps):
     waiting = []
     for first, second in steps:
-        share = -(-len(waiting) // max(len(first), 1))
-        for unit in first:
+        total, done = len(waiting), 0
+        for i, unit in enumerate(first):
             unit()
-            for _ in range(min(share, len(waiting))):
+            while done * len(first) < total * (i + 1):
                 waiting.pop(0)()
+                done += 1
         for unit in waiting:
             unit()
         waiting = list(second)
@@ -271,20 +272,19 @@
 
 
 def ordered(odd, a, b):
-    a, b = a.astype(F32), b.astype(F32)
-    return jnp.where(odd, a, b), jnp.where(odd, b, a)
+    return jnp.where(odd, a, b).astype(F32), jnp.where(odd, b, a).astype(F32)
 
 
 def pick(received, turn):
-    value = received[-1].astype(F32)
+    value = received[-1]
     for j in range(TURNS - 1):
-        value = jnp.where(turn == j, received[j].astype(F32), value)
+        value = jnp.where(turn == j, received[j], value)
     return value
 
 
 def below_and_above(received):
     turn = lax.axis_index("lat") % TURNS
-    return pick(received, (turn + TURNS - 1) % TURNS), pick(received, turn)
+    return pick(received, (turn + TURNS - 1) % TURNS).astype(F32), pick(received, turn).astype(F32)
 
 
 def in_chip(received):

time: 21.3 us -> 21.3 us (level)
  no operation moved by 1% of the time
where the time goes in v8:
time: 21.3 us; the launch traced here: 21.1 us
  Pallas kernels  12.8 us (60%)
  starting transfers between devices  7.57 us (36%)
  waiting for transfers between devices  0.49 us (2%)
    pallas_call x1, Pallas kernels, per_device(): pl.pallas_call(functools.partial(inner_kernel, block), out_shape=(array(r...  5.31 us
    ppermute x3, starting transfers between devices, per_device(): lax.ppermute(v, both, turn_swaps(lat_peers, lon_peers, j))  3.61 us
    pallas_call x1, Pallas kernels, per_device(): pl.pallas_call(functools.partial(rim_kernel, block), out_shape=(array(2 *...  3.25 us
    pallas_call x1, Pallas kernels, per_device(): pl.pallas_call(prep_kernel, out_shape=(array(edge + 1, CELLS, channels),)...  2.53 us
    ppermute x1, starting transfers between devices, per_device(): lon_b = lax.ppermute(lon_b, 'lon', swaps(lon_peers, True))  2.05 us
    ppermute x2, starting transfers between devices, corner_send(): return lax.ppermute(sent, 'lon', swaps(lon_peers, second))  1.9 us
    pallas_call x1, Pallas kernels, per_device(): pl.pallas_call(corner_kernel, out_shape=array(rows, cells, channels), in_...  1.69 us
  transfers between devices with their start and end apart: 6, of which 2 were waited for; matrix products, arithmetic and copies ran while one was open for 1% of the time, Pallas kernels for 41%

profile of v8, /device:TPU:0, one launch (start us, length us, event | category | flops | bytes accessed | tf_op | source)
XLA Modules:
  0.0 21.1 jit_solution(8425913551060916010)
XLA Ops:
  0.0 0.0 copy-start
  0.0 0.0 copy-start.1
  0.0 0.0 copy-start.2
  0.0 0.0 copy-start.3
  0.0 0.0 copy-start.4
  0.0 0.0 copy-start.5
  0.0 2.5 %prep.1 = (bf16[33,8,640]{2,1,0:T(8,128)(2,1)}, bf16[33,8,640]{2,1,0:T(8,128)(2,1)}, bf16[33,8,640]{2,1,0:T(8,128)(2,1)}, bf16[24,8,640]{2,1,0:T(8,128)(2,1)}) custom-call(bf16[192,8,640]{2,1,0:T(8,128)(2,1)} %bitcast.12, bf16[24,8,8,640]{3,2,1,0:T(8,128)(2,1)} %bitcast.13, f32[5,9,5,24]{3,2,1,0:T(8,128)} %bitcast.14, s32[2,24]{1,0:T(2,128)} %bitcast.18, ...), custom_call_target="tpu_custom_call" | custom-call | bytes 1310720 | tf_op jit(solution)/shard_map/prep/pallas_call | solution.py:504
  2.6 3.1 %collective-permute-start = (bf16[33,8,640]{2,1,0:T(8,128)(2,1)}, bf16[33,8,640]{2,1,0:T(8,128)(2,1)S(1)}, u32[]{:S(2)}, u32[]{:S(2)}) collective-permute-start(bf16[33,8,640]{2,1,0:T(8,128)(2,1)} %get-tuple-element.24), channel_id=1, source_target_pairs={{0,8},{1,9},{2,10},{3,11},{4,12},{5,13},{6,14},{7,15},{8,0},{9,1},... | collective-permute-start | bytes 1013768 | tf_op jit(solution)/shard_map/ppermute | solution.py:524
  5.7 0.0 collective-permute-start.1
  5.7 0.5 %collective-permute-start.2 = (bf16[33,8,640]{2,1,0:T(8,128)(2,1)}, bf16[33,8,640]{2,1,0:T(8,128)(2,1)S(1)}, u32[]{:S(2)}, u32[]{:S(2)}) collective-permute-start(bf16[33,8,640]{2,1,0:T(8,128)(2,1)} %get-tuple-element.26), channel_id=1, source_target_pairs={{16,24},{17,25},{18,26},{19,27},{20,28},{21,29},{22,30},{23,31},{2... | collective-permute-start | bytes 1013768 | tf_op jit(solution)/shard_map/ppermute | solution.py:524
  6.2 2.1 %collective-permute-start.3 = (bf16[24,8,640]{2,1,0:T(8,128)(2,1)}, bf16[24,8,640]{2,1,0:T(8,128)(2,1)S(1)}, u32[]{:S(2)}, u32[]{:S(2)}) collective-permute-start(bf16[24,8,640]{2,1,0:T(8,128)(2,1)} %get-tuple-element.31), channel_id=1, source_target_pairs={{1,2},{3,4},{5,6},{7,0},{2,1},{4,3},{6,5},{0,7},{9,10},{11,12},{13... | collective-permute-start | bytes 737288 | tf_op jit(solution)/shard_map/ppermute | solution.py:525
  8.2 0.0 copy-done
  8.2 0.0 copy-done.1
  8.2 0.0 copy-done.2
  8.2 0.0 copy-done.3
  8.2 0.0 copy-done.4
  8.2 0.0 copy-done.5
  8.3 5.3 %inner.1 = (bf16[960,256]{1,0:T(8,128)(2,1)S(1)}, bf16[320,256]{1,0:T(8,128)(2,1)S(1)}, bf16[320,256]{1,0:T(8,128)(2,1)S(1)}, bf16[8,64,640]{2,1,0:T(8,128)(2,1)...) custom-call(bf16[24,64,640]{2,1,0:T(8,128)(2,1)S(1)} %copy-done, ...), custom_call_target="tpu_custom_call" | custom-call | flops 2831155200 | bytes 3932160 | tf_op jit(solution)/shard_map/inner/pallas_call | solution.py:530
  13.6 0.2 %collective-permute-done.turn_0 = bf16[33,8,640]{2,1,0:T(8,128)(2,1)S(1)} collective-permute-done((bf16[33,8,640]{2,1,0:T(8,128)(2,1)}, bf16[33,8,640]{2,1,0:T(8,128)(2,1)S(1)}, u32[]{:S(2)}, u32[]{:S(2)}) %collective-permute-start) | collective-permute-done | bytes 337952 | tf_op jit(solution)/shard_map/ppermute | solution.py:524
  13.8 0.0 collective-permute-done.1.turn_1
  13.8 0.0 collective-permute-done.2.turn_2
  13.9 0.1 select_select_fusion.1
  14.0 1.2 %collective-permute-start.4 = (bf16[64,640]{1,0:T(8,128)(2,1)S(1)}, bf16[64,640]{1,0:T(8,128)(2,1)S(1)}, u32[]{:S(2)}, u32[]{:S(2)}) collective-permute-start(bf16[64,640]{1,0:T(8,128)(2,1)S(1)} %maximum_bitcast_fusion), channel_id=1, source_target_pairs={{1,2},{3,4},{5,6},{7,0},{2,1},{4,3},{6,5},{0,7},{9,10},{11,12},{13... | collective-permute-start | bytes 245768 | tf_op jit(solution)/shard_map/ppermute | solution.py:559
  15.3 0.7 %collective-permute-start.5 = (bf16[64,640]{1,0:T(8,128)(2,1)S(1)}, bf16[64,640]{1,0:T(8,128)(2,1)S(1)}, u32[]{:S(2)}, u32[]{:S(2)}) collective-permute-start(bf16[64,640]{1,0:T(8,128)(2,1)S(1)} %maximum_bitcast_fusion.1), channel_id=1, source_target_pairs={{0,1},{2,3},{4,5},{6,7},{1,0},{3,2},{5,4},{7,6},{8,9},{10,11},{12,... | collective-permute-start | bytes 245768 | tf_op jit(solution)/shard_map/ppermute | solution.py:559
  15.9 0.0 collective-permute-done.3.lon_b
  15.9 3.3 %rim.1 = (bf16[320,256]{1,0:T(8,128)(2,1)S(1)}, bf16[8,64,640]{2,1,0:T(8,128)(2,1)S(1)}, bf16[2,16,16,640]{3,2,1,0:T(8,128)(2,1)S(1)}, bf16[2,16,16,640]{3,2,1,0:T(8,128)(2,1)S(1)}) custom-call(bf16[24,64,640]{2,1,0:T(8,128)(2,1)S(1)} %copy-done, bf16[33,8,640]{2,1,0:T(8,128)(2,1)S(1)} %collective-permute-done.turn_0, ...), custom_call_target="tpu_custom_call" | custom-call | flops 2831155200 | bytes 3932160 | tf_op jit(solution)/shard_map/rim/pallas_call | solution.py:563
  19.2 0.3 %collective-permute-done.4.corner_b = bf16[64,640]{1,0:T(8,128)(2,1)S(1)} collective-permute-done((bf16[64,640]{1,0:T(8,128)(2,1)S(1)}, bf16[64,640]{1,0:T(8,128)(2,1)S(1)}, u32[]{:S(2)}, u32[]{:S(2)}) %collective-permute-start.4) | collective-permute-done | bytes 81952 | tf_op jit(solution)/shard_map/ppermute | solution.py:559
  19.4 0.0 collective-permute-done.5.corner_a
  19.4 1.7 %corner.1 = bf16[24,64,640]{2,1,0:T(8,128)(2,1)} custom-call(bf16[24,64,640]{2,1,0:T(8,128)(2,1)S(1)} %copy-done, bf16[33,8,640]{2,1,0:T(8,128)(2,1)S(1)} %collective-permute-done.turn_0, bf16[33,8,640]{2,1,0:T(8,128)(2,1)S(1)} %collective-permute-done.1.turn_1, ...), custom_call_target="tpu_custom_call", output_to_operand_aliasing={{}: (14, {})} | custom-call | flops 2831155200 | bytes 3932160 | tf_op jit(solution)/shard_map/corner/pallas_call | solution.py:582
  (5 shorter events, 0.1 us)
Async XLA Ops:
  0.0 8.2 %copy-start = (bf16[24,64,640]{2,1,0:T(8,128)(2,1)S(1)}, bf16[24,64,640]{2,1,0:T(8,128)(2,1)}, u32[]{:S(2)}) copy-start(bf16[24,64,640]{2,1,0:T(8,128)(2,1)} %x_ref.5) | copy-start | bytes 5898244
  0.0 8.2 %copy-start.1 = (f32[24,5,5,9]{0,2,3,1:T(8,128)S(1)}, f32[24,5,5,9]{0,2,3,1:T(8,128)}, u32[]{:S(2)}) copy-start(f32[24,5,5,9]{0,2,3,1:T(8,128)} %param.7) | copy-start | bytes 64804
  0.0 8.2 %copy-start.2 = (s32[24,5]{0,1:T(8,128)S(1)}, s32[24,5]{0,1:T(8,128)}, u32[]{:S(2)}) copy-start(s32[24,5]{0,1:T(8,128)} %param.9) | copy-start | bytes 1444
  0.0 8.2 %copy-start.3 = (s32[24,2]{0,1:T(2,128)S(1)}, s32[24,2]{0,1:T(2,128)}, u32[]{:S(2)}) copy-start(s32[24,2]{0,1:T(2,128)} %param.8) | copy-start | bytes 580
  0.0 8.2 %copy-start.4 = (f32[5,640]{1,0:T(8,128)S(1)}, f32[5,640]{1,0:T(8,128)}, u32[]{:S(2)}) copy-start(f32[5,640]{1,0:T(8,128)} %one_ref.5) | copy-start | bytes 38404
  0.0 8.2 %copy-start.5 = (f32[5,640]{1,0:T(8,128)S(1)}, f32[5,640]{1,0:T(8,128)}, u32[]{:S(2)}) copy-start(f32[5,640]{1,0:T(8,128)} %two_ref.5) | copy-start | bytes 38404
  2.6 11.2 %collective-permute-start = (bf16[33,8,640]{2,1,0:T(8,128)(2,1)}, bf16[33,8,640]{2,1,0:T(8,128)(2,1)S(1)}, u32[]{:S(2)}, u32[]{:S(2)}) collective-permute-start(bf16[33,8,640]{2,1,0:T(8,128)(2,1)} %get-tuple-element.24), channel_id=1, source_target_pairs={{0,8},{1,9},{2,10},{3,11},{4,12},{5,13},{6,14},{7,15},{8,0},{9,1},... | collective-permute-start | bytes 1013768 | tf_op jit(solution)/shard_map/ppermute | solution.py:524
  5.7 8.1 %collective-permute-start.1 = (bf16[33,8,640]{2,1,0:T(8,128)(2,1)}, bf16[33,8,640]{2,1,0:T(8,128)(2,1)S(1)}, u32[]{:S(2)}, u32[]{:S(2)}) collective-permute-start(bf16[33,8,640]{2,1,0:T(8,128)(2,1)} %get-tuple-element.25), channel_id=1, source_target_pairs={{8,16},{9,17},{10,18},{11,19},{12,20},{13,21},{14,22},{15,23},{16,... | collective-permute-start | bytes 1013768 | tf_op jit(solution)/shard_map/ppermute | solution.py:524
  5.7 8.1 %collective-permute-start.2 = (bf16[33,8,640]{2,1,0:T(8,128)(2,1)}, bf16[33,8,640]{2,1,0:T(8,128)(2,1)S(1)}, u32[]{:S(2)}, u32[]{:S(2)}) collective-permute-start(bf16[33,8,640]{2,1,0:T(8,128)(2,1)} %get-tuple-element.26), channel_id=1, source_target_pairs={{16,24},{17,25},{18,26},{19,27},{20,28},{21,29},{22,30},{23,31},{2... | collective-permute-start | bytes 1013768 | tf_op jit(solution)/shard_map/ppermute | solution.py:524
  6.2 9.8 %collective-permute-start.3 = (bf16[24,8,640]{2,1,0:T(8,128)(2,1)}, bf16[24,8,640]{2,1,0:T(8,128)(2,1)S(1)}, u32[]{:S(2)}, u32[]{:S(2)}) collective-permute-start(bf16[24,8,640]{2,1,0:T(8,128)(2,1)} %get-tuple-element.31), channel_id=1, source_target_pairs={{1,2},{3,4},{5,6},{7,0},{2,1},{4,3},{6,5},{0,7},{9,10},{11,12},{13... | collective-permute-start | bytes 737288 | tf_op jit(solution)/shard_map/ppermute | solution.py:525
  14.0 5.4 %collective-permute-start.4 = (bf16[64,640]{1,0:T(8,128)(2,1)S(1)}, bf16[64,640]{1,0:T(8,128)(2,1)S(1)}, u32[]{:S(2)}, u32[]{:S(2)}) collective-permute-start(bf16[64,640]{1,0:T(8,128)(2,1)S(1)} %maximum_bitcast_fusion), channel_id=1, source_target_pairs={{1,2},{3,4},{5,6},{7,0},{2,1},{4,3},{6,5},{0,7},{9,10},{11,12},{13... | collective-permute-start | bytes 245768 | tf_op jit(solution)/shard_map/ppermute | solution.py:559
  15.3 4.2 %collective-permute-start.5 = (bf16[64,640]{1,0:T(8,128)(2,1)S(1)}, bf16[64,640]{1,0:T(8,128)(2,1)S(1)}, u32[]{:S(2)}, u32[]{:S(2)}) collective-permute-start(bf16[64,640]{1,0:T(8,128)(2,1)S(1)} %maximum_bitcast_fusion.1), channel_id=1, source_target_pairs={{0,1},{2,3},{4,5},{6,7},{1,0},{3,2},{5,4},{7,6},{8,9},{10,11},{12,... | collective-permute-start | bytes 245768 | tf_op jit(solution)/shard_map/ppermute | solution.py:559

commit v9 on v8

--- a/solution.py
+++ b/solution.py
@@ -550,9 +550,7 @@
     *turns, sides = lax.optimization_barrier((*turns, sides))
 
     def corner_send(leading, second):
-        start = jnp.where(leading, 0, cells - CELLS)
-        parts = [v[:edge].reshape(REACH, cells, channels) for v in turns]
-        parts = [lax.dynamic_slice_in_dim(v, start, CELLS, 1) for v in parts]
+        parts = [jnp.where(leading, v[:edge:across], v[across - 1 : edge : across]) for v in turns]
         below = jnp.where(turn == 1, parts[0], jnp.where(turn == 2, parts[1], parts[2]))
         above = jnp.where(turn == 0, parts[0], jnp.where(turn == 1, parts[1], parts[2]))
         sent = jnp.concatenate([below, above], 0).reshape(2 * REACH * CELLS, channels)

time: 21.3 us -> 21.2 us (level)
  transfers between devices with their start and end apart: 6 -> 6, of which waited for: 2 -> 2; matrix products, arithmetic and copies ran while one was open for 1% -> 0% of each run, Pallas kernels for 41% -> 41%
where the time goes in v9:
time: 21.2 us; the launch traced here: 21 us
  Pallas kernels  12.8 us (60%)
  starting transfers between devices  7.57 us (36%)
  waiting for transfers between devices  0.5 us (2%)
    pallas_call x1, Pallas kernels, per_device(): pl.pallas_call(functools.partial(inner_kernel, block), out_shape=(array(r...  5.31 us
    ppermute x3, starting transfers between devices, per_device(): lax.ppermute(v, both, turn_swaps(lat_peers, lon_peers, j))  3.61 us
    pallas_call x1, Pallas kernels, per_device(): pl.pallas_call(functools.partial(rim_kernel, block), out_shape=(array(2 *...  3.24 us
    pallas_call x1, Pallas kernels, per_device(): pl.pallas_call(prep_kernel, out_shape=(array(edge + 1, CELLS, channels),)...  2.52 us
    ppermute x1, starting transfers between devices, per_device(): lon_b = lax.ppermute(lon_b, 'lon', swaps(lon_peers, True))  2.05 us
    ppermute x2, starting transfers between devices, corner_send(): return lax.ppermute(sent, 'lon', swaps(lon_peers, second))  1.9 us
    pallas_call x1, Pallas kernels, per_device(): pl.pallas_call(corner_kernel, out_shape=array(rows, cells, channels), in_...  1.69 us
  transfers between devices with their start and end apart: 6, of which 2 were waited for; matrix products, arithmetic and copies ran while one was open for 0% of the time, Pallas kernels for 41%

profile of v9, /device:TPU:0, one launch (start us, length us, event | category | flops | bytes accessed | tf_op | source)
XLA Modules:
  0.0 21.0 jit_solution(10979035808274761724)
XLA Ops:
  0.0 0.0 copy-start
  0.0 0.0 copy-start.1
  0.0 0.0 copy-start.2
  0.0 0.0 copy-start.3
  0.0 0.0 copy-start.4
  0.0 0.0 copy-start.5
  0.0 2.5 %prep.1 = (bf16[33,8,640]{2,1,0:T(8,128)(2,1)}, bf16[33,8,640]{2,1,0:T(8,128)(2,1)}, bf16[33,8,640]{2,1,0:T(8,128)(2,1)}, bf16[24,8,640]{2,1,0:T(8,128)(2,1)}) custom-call(bf16[192,8,640]{2,1,0:T(8,128)(2,1)} %bitcast.9, bf16[24,8,8,640]{3,2,1,0:T(8,128)(2,1)} %bitcast.10, f32[5,9,5,24]{3,2,1,0:T(8,128)} %bitcast.11, s32[2,24]{1,0:T(2,128)} %bitcast.15, ...), custom_call_target="tpu_custom_call" | custom-call | bytes 1310720 | tf_op jit(solution)/shard_map/prep/pallas_call | solution.py:504
  2.5 3.1 %collective-permute-start = (bf16[33,8,640]{2,1,0:T(8,128)(2,1)}, bf16[33,8,640]{2,1,0:T(8,128)(2,1)S(1)}, u32[]{:S(2)}, u32[]{:S(2)}) collective-permute-start(bf16[33,8,640]{2,1,0:T(8,128)(2,1)} %get-tuple-element.24), channel_id=1, source_target_pairs={{0,8},{1,9},{2,10},{3,11},{4,12},{5,13},{6,14},{7,15},{8,0},{9,1},... | collective-permute-start | bytes 1013768 | tf_op jit(solution)/shard_map/ppermute | solution.py:524
  5.7 0.0 collective-permute-start.1
  5.7 0.5 %collective-permute-start.2 = (bf16[33,8,640]{2,1,0:T(8,128)(2,1)}, bf16[33,8,640]{2,1,0:T(8,128)(2,1)S(1)}, u32[]{:S(2)}, u32[]{:S(2)}) collective-permute-start(bf16[33,8,640]{2,1,0:T(8,128)(2,1)} %get-tuple-element.26), channel_id=1, source_target_pairs={{16,24},{17,25},{18,26},{19,27},{20,28},{21,29},{22,30},{23,31},{2... | collective-permute-start | bytes 1013768 | tf_op jit(solution)/shard_map/ppermute | solution.py:524
  6.2 2.1 %collective-permute-start.3 = (bf16[24,8,640]{2,1,0:T(8,128)(2,1)}, bf16[24,8,640]{2,1,0:T(8,128)(2,1)S(1)}, u32[]{:S(2)}, u32[]{:S(2)}) collective-permute-start(bf16[24,8,640]{2,1,0:T(8,128)(2,1)} %get-tuple-element.31), channel_id=1, source_target_pairs={{1,2},{3,4},{5,6},{7,0},{2,1},{4,3},{6,5},{0,7},{9,10},{11,12},{13... | collective-permute-start | bytes 737288 | tf_op jit(solution)/shard_map/ppermute | solution.py:525
  8.2 0.0 copy-done
  8.2 0.0 copy-done.1
  8.2 0.0 copy-done.2
  8.2 0.0 copy-done.3
  8.2 0.0 copy-done.4
  8.2 0.0 copy-done.5
  8.2 5.3 %inner.1 = (bf16[960,256]{1,0:T(8,128)(2,1)S(1)}, bf16[320,256]{1,0:T(8,128)(2,1)S(1)}, bf16[320,256]{1,0:T(8,128)(2,1)S(1)}, bf16[8,64,640]{2,1,0:T(8,128)(2,1)...) custom-call(bf16[24,64,640]{2,1,0:T(8,128)(2,1)S(1)} %copy-done, ...), custom_call_target="tpu_custom_call" | custom-call | flops 2831155200 | bytes 3932160 | tf_op jit(solution)/shard_map/inner/pallas_call | solution.py:530
  13.6 0.2 %collective-permute-done.turn_0 = bf16[33,8,640]{2,1,0:T(8,128)(2,1)S(1)} collective-permute-done((bf16[33,8,640]{2,1,0:T(8,128)(2,1)}, bf16[33,8,640]{2,1,0:T(8,128)(2,1)S(1)}, u32[]{:S(2)}, u32[]{:S(2)}) %collective-permute-start) | collective-permute-done | bytes 337952 | tf_op jit(solution)/shard_map/ppermute | solution.py:524
  13.8 0.0 collective-permute-done.1.turn_1
  13.8 0.0 collective-permute-done.2.turn_2
  13.9 1.2 %collective-permute-start.4 = (bf16[64,640]{1,0:T(8,128)(2,1)S(1)}, bf16[64,640]{1,0:T(8,128)(2,1)S(1)}, u32[]{:S(2)}, u32[]{:S(2)}) collective-permute-start(bf16[64,640]{1,0:T(8,128)(2,1)S(1)} %maximum_bitcast_fusion), channel_id=1, source_target_pairs={{1,2},{3,4},{5,6},{7,0},{2,1},{4,3},{6,5},{0,7},{9,10},{11,12},{13... | collective-permute-start | bytes 245768 | tf_op jit(solution)/shard_map/ppermute | solution.py:557
  15.2 0.7 %collective-permute-start.5 = (bf16[64,640]{1,0:T(8,128)(2,1)S(1)}, bf16[64,640]{1,0:T(8,128)(2,1)S(1)}, u32[]{:S(2)}, u32[]{:S(2)}) collective-permute-start(bf16[64,640]{1,0:T(8,128)(2,1)S(1)} %maximum_bitcast_fusion.1), channel_id=1, source_target_pairs={{0,1},{2,3},{4,5},{6,7},{1,0},{3,2},{5,4},{7,6},{8,9},{10,11},{12,... | collective-permute-start | bytes 245768 | tf_op jit(solution)/shard_map/ppermute | solution.py:557
  15.8 0.0 collective-permute-done.3.lon_b
  15.8 3.2 %rim.1 = (bf16[320,256]{1,0:T(8,128)(2,1)S(1)}, bf16[8,64,640]{2,1,0:T(8,128)(2,1)S(1)}, bf16[2,16,16,640]{3,2,1,0:T(8,128)(2,1)S(1)}, bf16[2,16,16,640]{3,2,1,0:T(8,128)(2,1)S(1)}) custom-call(bf16[24,64,640]{2,1,0:T(8,128)(2,1)S(1)} %copy-done, bf16[33,8,640]{2,1,0:T(8,128)(2,1)S(1)} %collective-permute-done.turn_0, ...), custom_call_target="tpu_custom_call" | custom-call | flops 2831155200 | bytes 3932160 | tf_op jit(solution)/shard_map/rim/pallas_call | solution.py:561
  19.1 0.3 %collective-permute-done.4.corner_b = bf16[64,640]{1,0:T(8,128)(2,1)S(1)} collective-permute-done((bf16[64,640]{1,0:T(8,128)(2,1)S(1)}, bf16[64,640]{1,0:T(8,128)(2,1)S(1)}, u32[]{:S(2)}, u32[]{:S(2)}) %collective-permute-start.4) | collective-permute-done | bytes 81952 | tf_op jit(solution)/shard_map/ppermute | solution.py:557
  19.3 0.0 collective-permute-done.5.corner_a
  19.3 1.7 %corner.1 = bf16[24,64,640]{2,1,0:T(8,128)(2,1)} custom-call(bf16[24,64,640]{2,1,0:T(8,128)(2,1)S(1)} %copy-done, bf16[33,8,640]{2,1,0:T(8,128)(2,1)S(1)} %collective-permute-done.turn_0, bf16[33,8,640]{2,1,0:T(8,128)(2,1)S(1)} %collective-permute-done.1.turn_1, ...), custom_call_target="tpu_custom_call", output_to_operand_aliasing={{}: (14, {})} | custom-call | flops 2831155200 | bytes 3932160 | tf_op jit(solution)/shard_map/corner/pallas_call | solution.py:580
  (4 shorter events, 0.1 us)
Async XLA Ops:
  0.0 8.2 %copy-start = (bf16[24,64,640]{2,1,0:T(8,128)(2,1)S(1)}, bf16[24,64,640]{2,1,0:T(8,128)(2,1)}, u32[]{:S(2)}) copy-start(bf16[24,64,640]{2,1,0:T(8,128)(2,1)} %x_ref.5) | copy-start | bytes 5898244
  0.0 8.2 %copy-start.1 = (f32[24,5,5,9]{0,2,3,1:T(8,128)S(1)}, f32[24,5,5,9]{0,2,3,1:T(8,128)}, u32[]{:S(2)}) copy-start(f32[24,5,5,9]{0,2,3,1:T(8,128)} %param.7) | copy-start | bytes 64804
  0.0 8.2 %copy-start.2 = (s32[24,5]{0,1:T(8,128)S(1)}, s32[24,5]{0,1:T(8,128)}, u32[]{:S(2)}) copy-start(s32[24,5]{0,1:T(8,128)} %param.9) | copy-start | bytes 1444
  0.0 8.2 %copy-start.3 = (s32[24,2]{0,1:T(2,128)S(1)}, s32[24,2]{0,1:T(2,128)}, u32[]{:S(2)}) copy-start(s32[24,2]{0,1:T(2,128)} %param.8) | copy-start | bytes 580
  0.0 8.2 %copy-start.4 = (f32[5,640]{1,0:T(8,128)S(1)}, f32[5,640]{1,0:T(8,128)}, u32[]{:S(2)}) copy-start(f32[5,640]{1,0:T(8,128)} %one_ref.5) | copy-start | bytes 38404
  0.0 8.2 %copy-start.5 = (f32[5,640]{1,0:T(8,128)S(1)}, f32[5,640]{1,0:T(8,128)}, u32[]{:S(2)}) copy-start(f32[5,640]{1,0:T(8,128)} %two_ref.5) | copy-start | bytes 38404
  2.5 11.2 %collective-permute-start = (bf16[33,8,640]{2,1,0:T(8,128)(2,1)}, bf16[33,8,640]{2,1,0:T(8,128)(2,1)S(1)}, u32[]{:S(2)}, u32[]{:S(2)}) collective-permute-start(bf16[33,8,640]{2,1,0:T(8,128)(2,1)} %get-tuple-element.24), channel_id=1, source_target_pairs={{0,8},{1,9},{2,10},{3,11},{4,12},{5,13},{6,14},{7,15},{8,0},{9,1},... | collective-permute-start | bytes 1013768 | tf_op jit(solution)/shard_map/ppermute | solution.py:524
  5.7 8.1 %collective-permute-start.1 = (bf16[33,8,640]{2,1,0:T(8,128)(2,1)}, bf16[33,8,640]{2,1,0:T(8,128)(2,1)S(1)}, u32[]{:S(2)}, u32[]{:S(2)}) collective-permute-start(bf16[33,8,640]{2,1,0:T(8,128)(2,1)} %get-tuple-element.25), channel_id=1, source_target_pairs={{8,16},{9,17},{10,18},{11,19},{12,20},{13,21},{14,22},{15,23},{16,... | collective-permute-start | bytes 1013768 | tf_op jit(solution)/shard_map/ppermute | solution.py:524
  5.7 8.1 %collective-permute-start.2 = (bf16[33,8,640]{2,1,0:T(8,128)(2,1)}, bf16[33,8,640]{2,1,0:T(8,128)(2,1)S(1)}, u32[]{:S(2)}, u32[]{:S(2)}) collective-permute-start(bf16[33,8,640]{2,1,0:T(8,128)(2,1)} %get-tuple-element.26), channel_id=1, source_target_pairs={{16,24},{17,25},{18,26},{19,27},{20,28},{21,29},{22,30},{23,31},{2... | collective-permute-start | bytes 1013768 | tf_op jit(solution)/shard_map/ppermute | solution.py:524
  6.2 9.6 %collective-permute-start.3 = (bf16[24,8,640]{2,1,0:T(8,128)(2,1)}, bf16[24,8,640]{2,1,0:T(8,128)(2,1)S(1)}, u32[]{:S(2)}, u32[]{:S(2)}) collective-permute-start(bf16[24,8,640]{2,1,0:T(8,128)(2,1)} %get-tuple-element.31), channel_id=1, source_target_pairs={{1,2},{3,4},{5,6},{7,0},{2,1},{4,3},{6,5},{0,7},{9,10},{11,12},{13... | collective-permute-start | bytes 737288 | tf_op jit(solution)/shard_map/ppermute | solution.py:525
  13.9 5.4 %collective-permute-start.4 = (bf16[64,640]{1,0:T(8,128)(2,1)S(1)}, bf16[64,640]{1,0:T(8,128)(2,1)S(1)}, u32[]{:S(2)}, u32[]{:S(2)}) collective-permute-start(bf16[64,640]{1,0:T(8,128)(2,1)S(1)} %maximum_bitcast_fusion), channel_id=1, source_target_pairs={{1,2},{3,4},{5,6},{7,0},{2,1},{4,3},{6,5},{0,7},{9,10},{11,12},{13... | collective-permute-start | bytes 245768 | tf_op jit(solution)/shard_map/ppermute | solution.py:557
  15.2 4.2 %collective-permute-start.5 = (bf16[64,640]{1,0:T(8,128)(2,1)S(1)}, bf16[64,640]{1,0:T(8,128)(2,1)S(1)}, u32[]{:S(2)}, u32[]{:S(2)}) collective-permute-start(bf16[64,640]{1,0:T(8,128)(2,1)S(1)} %maximum_bitcast_fusion.1), channel_id=1, source_target_pairs={{0,1},{2,3},{4,5},{6,7},{1,0},{3,2},{5,4},{7,6},{8,9},{10,11},{12,... | collective-permute-start | bytes 245768 | tf_op jit(solution)/shard_map/ppermute | solution.py:557

commit v10 on v9

--- a/solution.py
+++ b/solution.py
@@ -134,7 +134,7 @@
 
 
 def prep_kernel(
-    flat_ref, groups_ref, filter_in, edge_in, mask_in, turn_0, turn_1, turn_2, lon_b,
+    flat_ref, groups_ref, filter_in, edge_in, mask_in, turn_0, turn_1, turn_2, lon_b, lines_ref,
     filter_ref, edge_ref, mask_ref, payloads, far, padded, tags, sems, out_sems,
 ):
     bases, lags, bands, rows = filter_in.shape
@@ -176,6 +176,7 @@
     for copy in small:
         copy.wait()
     for k, line in enumerate(filter_lines(filter_ref, edge_ref, mask_ref, padded, chosen)):
+        lines_ref[k] = line[:rows]
         tags[0, :LAT_REACH, lanes_of(k)] = line[rows - LAT_REACH : rows]
         tags[1, :LAT_REACH, lanes_of(k)] = line[:LAT_REACH]
     payloads[0, edge] = tags[0].astype(BF16)
@@ -191,16 +192,14 @@
 
 
 def inner_kernel(
-    block, x_ref, filter_ref, edge_ref, mask_ref, one_ref, two_ref,
+    block, x_ref, lines_ref, one_ref, two_ref,
     toeplitz, rim_toeplitz, wide_toeplitz, edge_rows, edge_cells, sides, out_ref,
-    middle, padded, field, hidden, ends, sems,
+    middle, field, hidden, ends, sems,
 ):
     rows, cells, channels = x_ref.shape
     bases = one_ref.shape[0]
     chunks = channels // LANES
-    padded[...] = jnp.zeros_like(padded)
-    chosen = line_choice(filter_ref.shape[1])
-    lines = filter_lines(filter_ref, edge_ref, mask_ref, padded, chosen)
+    lines = [lines_ref[k] for k in range(bases)]
     fill_toeplitz(toeplitz, lambda r, k: lines[k][r : r + 1, :], rows, bases, lambda r: r % block)
     kept = list(range(REACH)) + list(range(rows - REACH, rows))
     fill_toeplitz(wide_toeplitz, lambda r, k: lines[k][kept[r] : kept[r] + 1, :], 2 * REACH, bases, place_of)
@@ -501,11 +500,12 @@
     across = cells // CELLS
     edge = REACH * across
     filter_args = (filters.transpose(1, 3, 2, 0), band_edges.T, basis_mask.T)
-    *turns, lon_b = pl.pallas_call(
+    *turns, lon_b, lines = pl.pallas_call(
         prep_kernel,
-        out_shape=(array(edge + 1, CELLS, channels),) * TURNS + (array(rows, CELLS, channels),),
+        out_shape=(array(edge + 1, CELLS, channels),) * TURNS
+        + (array(rows, CELLS, channels), scratch(bases, rows, LANES, dtype=F32)),
         in_specs=[anywhere] * 5,
-        out_specs=(anywhere,) * (TURNS + 1),
+        out_specs=(anywhere,) * (TURNS + 1) + (vmem,),
         scratch_shapes=[
             scratch(bases, filters.shape[3], BANDS, rows, dtype=F32),
             scratch(2, rows, dtype=jnp.int32), scratch(bases, rows, dtype=jnp.int32),
@@ -534,10 +534,10 @@
             array(2 * REACH, cells, channels), array(middle - REACH, TILE, channels),
             array(middle, TILE, channels), array(rows, cells, channels),
         ),
-        in_specs=[vmem] * 6,
+        in_specs=[vmem] * 4,
         out_specs=(vmem,) * 6 + (anywhere,),
         scratch_shapes=[
-            scratch(middle, cells - 2 * TILE, channels), scratch(bases, LANES, LANES, dtype=F32),
+            scratch(middle, cells - 2 * TILE, channels),
             scratch(chunks, rows + REACH, cells, LANES, dtype=F32),
             scratch(chunks, rows + REACH, cells - CELLS, LANES, dtype=F32),
             scratch(chunks, middle, TILE, LANES, dtype=F32), dma((1,)),
@@ -545,7 +545,7 @@
         compiler_params=params,
         cost_estimate=cost,
         name="inner",
-    )(state_field, *filter_args, weights_one, weights_two)
+    )(state_field, lines, weights_one, weights_two)
 
     *turns, sides = lax.optimization_barrier((*turns, sides))
 

time: 21.2 us -> 21.2 us (level)
  Pallas kernels: 12.8 us -> 12.5 us
  waiting for transfers between devices: 0.5 us -> 0.8 us
    ppermute x3, waiting for transfers between devices: 0.22 us -> 0.47 us  [per_device(): lax.ppermute(v, both, turn_swaps(lat_peers, lon_peers, j))]
    pallas_call x1, Pallas kernels: 5.31 us -> 5.1 us  [per_device(): pl.pallas_call(functools.partial(inner_kernel, block), out_shape=(array(r...]
  transfers between devices with their start and end apart: 6 -> 6, of which waited for: 2 -> 2; matrix products, arithmetic and copies ran while one was open for 0% -> 0% of each run, Pallas kernels for 41% -> 39%
where the time goes in v10:
time: 21.2 us; the launch traced here: 21 us
  Pallas kernels  12.5 us (59%)
  starting transfers between devices  7.56 us (36%)
  waiting for transfers between devices  0.8 us (4%)
    pallas_call x1, Pallas kernels, per_device(): pl.pallas_call(functools.partial(inner_kernel, block), out_shape=(array(r...  5.1 us
    ppermute x3, starting transfers between devices, per_device(): lax.ppermute(v, both, turn_swaps(lat_peers, lon_peers, j))  3.6 us
    pallas_call x1, Pallas kernels, per_device(): pl.pallas_call(functools.partial(rim_kernel, block), out_shape=(array(2 *...  3.19 us
    pallas_call x1, Pallas kernels, per_device(): pl.pallas_call(prep_kernel, out_shape=(array(edge + 1, CELLS, channels),)...  2.55 us
    ppermute x1, starting transfers between devices, per_device(): lon_b = lax.ppermute(lon_b, 'lon', swaps(lon_peers, True))  2.05 us
    ppermute x2, starting transfers between devices, corner_send(): return lax.ppermute(sent, 'lon', swaps(lon_peers, second))  1.9 us
    pallas_call x1, Pallas kernels, per_device(): pl.pallas_call(corner_kernel, out_shape=array(rows, cells, channels), in_...  1.7 us
    ppermute x3, waiting for transfers between devices, per_device(): lax.ppermute(v, both, turn_swaps(lat_peers, lon_peers, j))  0.47 us
  transfers between devices with their start and end apart: 6, of which 2 were waited for; matrix products, arithmetic and copies ran while one was open for 0% of the time, Pallas kernels for 39%

profile of v10, /device:TPU:0, one launch (start us, length us, event | category | flops | bytes accessed | tf_op | source)
XLA Modules:
  0.0 21.0 jit_solution(13648778153773843665)
XLA Ops:
  0.0 0.0 copy-start
  0.0 0.0 copy-start.1
  0.0 0.0 copy-start.2
  0.0 2.6 %prep.1 = (bf16[33,8,640]{2,1,0:T(8,128)(2,1)}, bf16[33,8,640]{2,1,0:T(8,128)(2,1)}, bf16[33,8,640]{2,1,0:T(8,128)(2,1)}, bf16[24,8,640]{2,1,0:T(8,128)(2,1)}, f32[5,24,128]{2,1,0:T(8,128)S(1)}) custom-call(bf16[192,8,640]{2,1,0:T(8,128)(2,1)} %bitcast.9, bf16[24,8,8,640]{3,2,1,0:T(8,128)(2,1)} %bitcast.10, f32[5,9,5,24]{3,2,1,0:T(8,128)} %bitcast.11, ...), custom_call_target="tpu_custom_call" | custom-call | bytes 1310720 | tf_op jit(solution)/shard_map/prep/pallas_call | solution.py:503
  2.6 3.1 %collective-permute-start = (bf16[33,8,640]{2,1,0:T(8,128)(2,1)}, bf16[33,8,640]{2,1,0:T(8,128)(2,1)S(1)}, u32[]{:S(2)}, u32[]{:S(2)}) collective-permute-start(bf16[33,8,640]{2,1,0:T(8,128)(2,1)} %get-tuple-element.25), channel_id=1, source_target_pairs={{0,8},{1,9},{2,10},{3,11},{4,12},{5,13},{6,14},{7,15},{8,0},{9,1},... | collective-permute-start | bytes 1013768 | tf_op jit(solution)/shard_map/ppermute | solution.py:524
  5.7 0.0 collective-permute-start.1
  5.7 0.5 %collective-permute-start.2 = (bf16[33,8,640]{2,1,0:T(8,128)(2,1)}, bf16[33,8,640]{2,1,0:T(8,128)(2,1)S(1)}, u32[]{:S(2)}, u32[]{:S(2)}) collective-permute-start(bf16[33,8,640]{2,1,0:T(8,128)(2,1)} %get-tuple-element.27), channel_id=1, source_target_pairs={{16,24},{17,25},{18,26},{19,27},{20,28},{21,29},{22,30},{23,31},{2... | collective-permute-start | bytes 1013768 | tf_op jit(solution)/shard_map/ppermute | solution.py:524
  6.2 2.1 %collective-permute-start.3 = (bf16[24,8,640]{2,1,0:T(8,128)(2,1)}, bf16[24,8,640]{2,1,0:T(8,128)(2,1)S(1)}, u32[]{:S(2)}, u32[]{:S(2)}) collective-permute-start(bf16[24,8,640]{2,1,0:T(8,128)(2,1)} %get-tuple-element.33), channel_id=1, source_target_pairs={{1,2},{3,4},{5,6},{7,0},{2,1},{4,3},{6,5},{0,7},{9,10},{11,12},{13... | collective-permute-start | bytes 737288 | tf_op jit(solution)/shard_map/ppermute | solution.py:525
  8.2 0.0 copy-done
  8.2 0.0 copy-done.1
  8.2 0.0 copy-done.2
  8.2 5.1 %inner.1 = (bf16[960,256]{1,0:T(8,128)(2,1)S(1)}, bf16[320,256]{1,0:T(8,128)(2,1)S(1)}, bf16[320,256]{1,0:T(8,128)(2,1)S(1)}, bf16[8,64,640]{2,1,0:T(8,128)(2,1)...) custom-call(bf16[24,64,640]{2,1,0:T(8,128)(2,1)S(1)} %copy-done, ...), custom_call_target="tpu_custom_call" | custom-call | flops 2831155200 | bytes 3932160 | tf_op jit(solution)/shard_map/inner/pallas_call | solution.py:530
  13.3 0.5 %collective-permute-done.turn_0 = bf16[33,8,640]{2,1,0:T(8,128)(2,1)S(1)} collective-permute-done((bf16[33,8,640]{2,1,0:T(8,128)(2,1)}, bf16[33,8,640]{2,1,0:T(8,128)(2,1)S(1)}, u32[]{:S(2)}, u32[]{:S(2)}) %collective-permute-start) | collective-permute-done | bytes 337952 | tf_op jit(solution)/shard_map/ppermute | solution.py:524
  13.8 0.0 collective-permute-done.1.turn_1
  13.8 0.0 collective-permute-done.2.turn_2
  13.9 1.2 %collective-permute-start.4 = (bf16[64,640]{1,0:T(8,128)(2,1)S(1)}, bf16[64,640]{1,0:T(8,128)(2,1)S(1)}, u32[]{:S(2)}, u32[]{:S(2)}) collective-permute-start(bf16[64,640]{1,0:T(8,128)(2,1)S(1)} %maximum_bitcast_fusion), channel_id=1, source_target_pairs={{1,2},{3,4},{5,6},{7,0},{2,1},{4,3},{6,5},{0,7},{9,10},{11,12},{13... | collective-permute-start | bytes 245768 | tf_op jit(solution)/shard_map/ppermute | solution.py:557
  15.2 0.7 %collective-permute-start.5 = (bf16[64,640]{1,0:T(8,128)(2,1)S(1)}, bf16[64,640]{1,0:T(8,128)(2,1)S(1)}, u32[]{:S(2)}, u32[]{:S(2)}) collective-permute-start(bf16[64,640]{1,0:T(8,128)(2,1)S(1)} %maximum_bitcast_fusion.1), channel_id=1, source_target_pairs={{0,1},{2,3},{4,5},{6,7},{1,0},{3,2},{5,4},{7,6},{8,9},{10,11},{12,... | collective-permute-start | bytes 245768 | tf_op jit(solution)/shard_map/ppermute | solution.py:557
  15.8 0.0 collective-permute-done.3.lon_b
  15.8 3.2 %rim.1 = (bf16[320,256]{1,0:T(8,128)(2,1)S(1)}, bf16[8,64,640]{2,1,0:T(8,128)(2,1)S(1)}, bf16[2,16,16,640]{3,2,1,0:T(8,128)(2,1)S(1)}, bf16[2,16,16,640]{3,2,1,0:T(8,128)(2,1)S(1)}) custom-call(bf16[24,64,640]{2,1,0:T(8,128)(2,1)S(1)} %copy-done, bf16[33,8,640]{2,1,0:T(8,128)(2,1)S(1)} %collective-permute-done.turn_0, ...), custom_call_target="tpu_custom_call" | custom-call | flops 2831155200 | bytes 3932160 | tf_op jit(solution)/shard_map/rim/pallas_call | solution.py:561
  19.0 0.3 %collective-permute-done.4.corner_b = bf16[64,640]{1,0:T(8,128)(2,1)S(1)} collective-permute-done((bf16[64,640]{1,0:T(8,128)(2,1)S(1)}, bf16[64,640]{1,0:T(8,128)(2,1)S(1)}, u32[]{:S(2)}, u32[]{:S(2)}) %collective-permute-start.4) | collective-permute-done | bytes 81952 | tf_op jit(solution)/shard_map/ppermute | solution.py:557
  19.3 0.0 collective-permute-done.5.corner_a
  19.3 1.7 %corner.1 = bf16[24,64,640]{2,1,0:T(8,128)(2,1)} custom-call(bf16[24,64,640]{2,1,0:T(8,128)(2,1)S(1)} %copy-done, bf16[33,8,640]{2,1,0:T(8,128)(2,1)S(1)} %collective-permute-done.turn_0, bf16[33,8,640]{2,1,0:T(8,128)(2,1)S(1)} %collective-permute-done.1.turn_1, ...), custom_call_target="tpu_custom_call", output_to_operand_aliasing={{}: (14, {})} | custom-call | flops 2831155200 | bytes 3932160 | tf_op jit(solution)/shard_map/corner/pallas_call | solution.py:580
  (4 shorter events, 0.1 us)
Async XLA Ops:
  0.0 8.2 %copy-start = (bf16[24,64,640]{2,1,0:T(8,128)(2,1)S(1)}, bf16[24,64,640]{2,1,0:T(8,128)(2,1)}, u32[]{:S(2)}) copy-start(bf16[24,64,640]{2,1,0:T(8,128)(2,1)} %x_ref.5) | copy-start | bytes 5898244
  0.0 8.2 %copy-start.1 = (f32[5,640]{1,0:T(8,128)S(1)}, f32[5,640]{1,0:T(8,128)}, u32[]{:S(2)}) copy-start(f32[5,640]{1,0:T(8,128)} %one_ref.5) | copy-start | bytes 38404
  0.0 8.2 %copy-start.2 = (f32[5,640]{1,0:T(8,128)S(1)}, f32[5,640]{1,0:T(8,128)}, u32[]{:S(2)}) copy-start(f32[5,640]{1,0:T(8,128)} %two_ref.5) | copy-start | bytes 38404
  2.6 11.2 %collective-permute-start = (bf16[33,8,640]{2,1,0:T(8,128)(2,1)}, bf16[33,8,640]{2,1,0:T(8,128)(2,1)S(1)}, u32[]{:S(2)}, u32[]{:S(2)}) collective-permute-start(bf16[33,8,640]{2,1,0:T(8,128)(2,1)} %get-tuple-element.25), channel_id=1, source_target_pairs={{0,8},{1,9},{2,10},{3,11},{4,12},{5,13},{6,14},{7,15},{8,0},{9,1},... | collective-permute-start | bytes 1013768 | tf_op jit(solution)/shard_map/ppermute | solution.py:524
  5.7 8.1 %collective-permute-start.1 = (bf16[33,8,640]{2,1,0:T(8,128)(2,1)}, bf16[33,8,640]{2,1,0:T(8,128)(2,1)S(1)}, u32[]{:S(2)}, u32[]{:S(2)}) collective-permute-start(bf16[33,8,640]{2,1,0:T(8,128)(2,1)} %get-tuple-element.26), channel_id=1, source_target_pairs={{8,16},{9,17},{10,18},{11,19},{12,20},{13,21},{14,22},{15,23},{16,... | collective-permute-start | bytes 1013768 | tf_op jit(solution)/shard_map/ppermute | solution.py:524
  5.7 8.1 %collective-permute-start.2 = (bf16[33,8,640]{2,1,0:T(8,128)(2,1)}, bf16[33,8,640]{2,1,0:T(8,128)(2,1)S(1)}, u32[]{:S(2)}, u32[]{:S(2)}) collective-permute-start(bf16[33,8,640]{2,1,0:T(8,128)(2,1)} %get-tuple-element.27), channel_id=1, source_target_pairs={{16,24},{17,25},{18,26},{19,27},{20,28},{21,29},{22,30},{23,31},{2... | collective-permute-start | bytes 1013768 | tf_op jit(solution)/shard_map/ppermute | solution.py:524
  6.2 9.6 %collective-permute-start.3 = (bf16[24,8,640]{2,1,0:T(8,128)(2,1)}, bf16[24,8,640]{2,1,0:T(8,128)(2,1)S(1)}, u32[]{:S(2)}, u32[]{:S(2)}) collective-permute-start(bf16[24,8,640]{2,1,0:T(8,128)(2,1)} %get-tuple-element.33), channel_id=1, source_target_pairs={{1,2},{3,4},{5,6},{7,0},{2,1},{4,3},{6,5},{0,7},{9,10},{11,12},{13... | collective-permute-start | bytes 737288 | tf_op jit(solution)/shard_map/ppermute | solution.py:525
  13.9 5.4 %collective-permute-start.4 = (bf16[64,640]{1,0:T(8,128)(2,1)S(1)}, bf16[64,640]{1,0:T(8,128)(2,1)S(1)}, u32[]{:S(2)}, u32[]{:S(2)}) collective-permute-start(bf16[64,640]{1,0:T(8,128)(2,1)S(1)} %maximum_bitcast_fusion), channel_id=1, source_target_pairs={{1,2},{3,4},{5,6},{7,0},{2,1},{4,3},{6,5},{0,7},{9,10},{11,12},{13... | collective-permute-start | bytes 245768 | tf_op jit(solution)/shard_map/ppermute | solution.py:557
  15.2 4.2 %collective-permute-start.5 = (bf16[64,640]{1,0:T(8,128)(2,1)S(1)}, bf16[64,640]{1,0:T(8,128)(2,1)S(1)}, u32[]{:S(2)}, u32[]{:S(2)}) collective-permute-start(bf16[64,640]{1,0:T(8,128)(2,1)S(1)} %maximum_bitcast_fusion.1), channel_id=1, source_target_pairs={{0,1},{2,3},{4,5},{6,7},{1,0},{3,2},{5,4},{7,6},{8,9},{10,11},{12,... | collective-permute-start | bytes 245768 | tf_op jit(solution)/shard_map/ppermute | solution.py:557

commit v11 on v10

--- a/solution.py
+++ b/solution.py
@@ -463,17 +463,25 @@
             whole = [near, values[side]] if side else [values[side], near]
             corner_out[side, :, :, lanes] = jnp.concatenate(whole, 1).astype(BF16)
 
+    def leave(begin, end):
+        lanes = pl.ds(begin * LANES, (end - begin) * LANES)
+        for side in range(2):
+            for row in range(2):
+                source = corner_out.at[side, pl.ds(row * REACH, REACH), :, lanes]
+                target = out_ref.at[ends_at[row], sides_at[side], lanes]
+                copies.append(pltpu.make_async_copy(source, target, sems.at[len(copies)]))
+                copies[-1].start()
+
     hidden = [first(c) for c in range(chunks)]
-    for c in range(chunks):
+    early = max(chunks - 2, 1)
+    for c in range(early):
         second(c, hidden[c])
-    last = []
-    for side in range(2):
-        for end in range(2):
-            source = corner_out.at[side, pl.ds(end * REACH, REACH)]
-            target = out_ref.at[ends_at[end], sides_at[side]]
-            last.append(pltpu.make_async_copy(source, target, sems.at[len(copies) + len(last)]))
-            last[-1].start()
-    for copy in copies + last:
+    leave(0, early)
+    for c in range(early, chunks):
+        second(c, hidden[c])
+    if early < chunks:
+        leave(early, chunks)
+    for copy in copies:
         copy.wait()
 
 
@@ -583,7 +591,7 @@
         in_specs=[vmem] * 14 + [anywhere],
         out_specs=anywhere,
         input_output_aliases={14: 0},
-        scratch_shapes=[scratch(2, 2 * REACH, TILE, channels), dma((8,))],
+        scratch_shapes=[scratch(2, 2 * REACH, TILE, channels), dma((12,))],
         compiler_params=params,
         cost_estimate=cost,
         name="corner",

time: 21.2 us -> 21.1 us (level)
  no operation moved by 1% of the time
where the time goes in v11:
time: 21.1 us; the launch traced here: 21 us
  Pallas kernels  12.5 us (59%)
  starting transfers between devices  7.56 us (36%)
  waiting for transfers between devices  0.8 us (4%)
    pallas_call x1, Pallas kernels, per_device(): pl.pallas_call(functools.partial(inner_kernel, block), out_shape=(array(r...  5.1 us
    ppermute x3, starting transfers between devices, per_device(): lax.ppermute(v, both, turn_swaps(lat_peers, lon_peers, j))  3.6 us
    pallas_call x1, Pallas kernels, per_device(): pl.pallas_call(functools.partial(rim_kernel, block), out_shape=(array(2 *...  3.19 us
    pallas_call x1, Pallas kernels, per_device(): pl.pallas_call(prep_kernel, out_shape=(array(edge + 1, CELLS, channels),)...  2.55 us
    ppermute x1, starting transfers between devices, per_device(): lon_b = lax.ppermute(lon_b, 'lon', swaps(lon_peers, True))  2.05 us
    ppermute x2, starting transfers between devices, corner_send(): return lax.ppermute(sent, 'lon', swaps(lon_peers, second))  1.9 us
    pallas_call x1, Pallas kernels, per_device(): pl.pallas_call(corner_kernel, out_shape=array(rows, cells, channels), in_...  1.63 us
    ppermute x3, waiting for transfers between devices, per_device(): lax.ppermute(v, both, turn_swaps(lat_peers, lon_peers, j))  0.47 us
  transfers between devices with their start and end apart: 6, of which 2 were waited for; matrix products, arithmetic and copies ran while one was open for 0% of the time, Pallas kernels for 39%

profile of v11, /device:TPU:0, one launch (start us, length us, event | category | flops | bytes accessed | tf_op | source)
XLA Modules:
  0.0 21.0 jit_solution(4976108350750784235)
XLA Ops:
  0.0 0.0 copy-start
  0.0 0.0 copy-start.1
  0.0 0.0 copy-start.2
  0.0 2.6 %prep.1 = (bf16[33,8,640]{2,1,0:T(8,128)(2,1)}, bf16[33,8,640]{2,1,0:T(8,128)(2,1)}, bf16[33,8,640]{2,1,0:T(8,128)(2,1)}, bf16[24,8,640]{2,1,0:T(8,128)(2,1)}, f32[5,24,128]{2,1,0:T(8,128)S(1)}) custom-call(bf16[192,8,640]{2,1,0:T(8,128)(2,1)} %bitcast.9, bf16[24,8,8,640]{3,2,1,0:T(8,128)(2,1)} %bitcast.10, f32[5,9,5,24]{3,2,1,0:T(8,128)} %bitcast.11, ...), custom_call_target="tpu_custom_call" | custom-call | bytes 1310720 | tf_op jit(solution)/shard_map/prep/pallas_call | solution.py:511
  2.6 3.1 %collective-permute-start = (bf16[33,8,640]{2,1,0:T(8,128)(2,1)}, bf16[33,8,640]{2,1,0:T(8,128)(2,1)S(1)}, u32[]{:S(2)}, u32[]{:S(2)}) collective-permute-start(bf16[33,8,640]{2,1,0:T(8,128)(2,1)} %get-tuple-element.25), channel_id=1, source_target_pairs={{0,8},{1,9},{2,10},{3,11},{4,12},{5,13},{6,14},{7,15},{8,0},{9,1},... | collective-permute-start | bytes 1013768 | tf_op jit(solution)/shard_map/ppermute | solution.py:532
  5.7 0.0 collective-permute-start.1
  5.7 0.5 %collective-permute-start.2 = (bf16[33,8,640]{2,1,0:T(8,128)(2,1)}, bf16[33,8,640]{2,1,0:T(8,128)(2,1)S(1)}, u32[]{:S(2)}, u32[]{:S(2)}) collective-permute-start(bf16[33,8,640]{2,1,0:T(8,128)(2,1)} %get-tuple-element.27), channel_id=1, source_target_pairs={{16,24},{17,25},{18,26},{19,27},{20,28},{21,29},{22,30},{23,31},{2... | collective-permute-start | bytes 1013768 | tf_op jit(solution)/shard_map/ppermute | solution.py:532
  6.2 2.1 %collective-permute-start.3 = (bf16[24,8,640]{2,1,0:T(8,128)(2,1)}, bf16[24,8,640]{2,1,0:T(8,128)(2,1)S(1)}, u32[]{:S(2)}, u32[]{:S(2)}) collective-permute-start(bf16[24,8,640]{2,1,0:T(8,128)(2,1)} %get-tuple-element.33), channel_id=1, source_target_pairs={{1,2},{3,4},{5,6},{7,0},{2,1},{4,3},{6,5},{0,7},{9,10},{11,12},{13... | collective-permute-start | bytes 737288 | tf_op jit(solution)/shard_map/ppermute | solution.py:533
  8.2 0.0 copy-done
  8.2 0.0 copy-done.1
  8.2 0.0 copy-done.2
  8.2 5.1 %inner.1 = (bf16[960,256]{1,0:T(8,128)(2,1)S(1)}, bf16[320,256]{1,0:T(8,128)(2,1)S(1)}, bf16[320,256]{1,0:T(8,128)(2,1)S(1)}, bf16[8,64,640]{2,1,0:T(8,128)(2,1)...) custom-call(bf16[24,64,640]{2,1,0:T(8,128)(2,1)S(1)} %copy-done, ...), custom_call_target="tpu_custom_call" | custom-call | flops 2831155200 | bytes 3932160 | tf_op jit(solution)/shard_map/inner/pallas_call | solution.py:538
  13.3 0.5 %collective-permute-done.turn_0 = bf16[33,8,640]{2,1,0:T(8,128)(2,1)S(1)} collective-permute-done((bf16[33,8,640]{2,1,0:T(8,128)(2,1)}, bf16[33,8,640]{2,1,0:T(8,128)(2,1)S(1)}, u32[]{:S(2)}, u32[]{:S(2)}) %collective-permute-start) | collective-permute-done | bytes 337952 | tf_op jit(solution)/shard_map/ppermute | solution.py:532
  13.8 0.0 collective-permute-done.1.turn_1
  13.8 0.0 collective-permute-done.2.turn_2
  13.9 1.2 %collective-permute-start.4 = (bf16[64,640]{1,0:T(8,128)(2,1)S(1)}, bf16[64,640]{1,0:T(8,128)(2,1)S(1)}, u32[]{:S(2)}, u32[]{:S(2)}) collective-permute-start(bf16[64,640]{1,0:T(8,128)(2,1)S(1)} %maximum_bitcast_fusion), channel_id=1, source_target_pairs={{1,2},{3,4},{5,6},{7,0},{2,1},{4,3},{6,5},{0,7},{9,10},{11,12},{13... | collective-permute-start | bytes 245768 | tf_op jit(solution)/shard_map/ppermute | solution.py:565
  15.2 0.7 %collective-permute-start.5 = (bf16[64,640]{1,0:T(8,128)(2,1)S(1)}, bf16[64,640]{1,0:T(8,128)(2,1)S(1)}, u32[]{:S(2)}, u32[]{:S(2)}) collective-permute-start(bf16[64,640]{1,0:T(8,128)(2,1)S(1)} %maximum_bitcast_fusion.1), channel_id=1, source_target_pairs={{0,1},{2,3},{4,5},{6,7},{1,0},{3,2},{5,4},{7,6},{8,9},{10,11},{12,... | collective-permute-start | bytes 245768 | tf_op jit(solution)/shard_map/ppermute | solution.py:565
  15.8 0.0 collective-permute-done.3.lon_b
  15.8 3.2 %rim.1 = (bf16[320,256]{1,0:T(8,128)(2,1)S(1)}, bf16[8,64,640]{2,1,0:T(8,128)(2,1)S(1)}, bf16[2,16,16,640]{3,2,1,0:T(8,128)(2,1)S(1)}, bf16[2,16,16,640]{3,2,1,0:T(8,128)(2,1)S(1)}) custom-call(bf16[24,64,640]{2,1,0:T(8,128)(2,1)S(1)} %copy-done, bf16[33,8,640]{2,1,0:T(8,128)(2,1)S(1)} %collective-permute-done.turn_0, ...), custom_call_target="tpu_custom_call" | custom-call | flops 2831155200 | bytes 3932160 | tf_op jit(solution)/shard_map/rim/pallas_call | solution.py:569
  19.0 0.3 %collective-permute-done.4.corner_b = bf16[64,640]{1,0:T(8,128)(2,1)S(1)} collective-permute-done((bf16[64,640]{1,0:T(8,128)(2,1)S(1)}, bf16[64,640]{1,0:T(8,128)(2,1)S(1)}, u32[]{:S(2)}, u32[]{:S(2)}) %collective-permute-start.4) | collective-permute-done | bytes 81952 | tf_op jit(solution)/shard_map/ppermute | solution.py:565
  19.3 0.0 collective-permute-done.5.corner_a
  19.3 1.6 %corner.1 = bf16[24,64,640]{2,1,0:T(8,128)(2,1)} custom-call(bf16[24,64,640]{2,1,0:T(8,128)(2,1)S(1)} %copy-done, bf16[33,8,640]{2,1,0:T(8,128)(2,1)S(1)} %collective-permute-done.turn_0, bf16[33,8,640]{2,1,0:T(8,128)(2,1)S(1)} %collective-permute-done.1.turn_1, ...), custom_call_target="tpu_custom_call", output_to_operand_aliasing={{}: (14, {})} | custom-call | flops 2831155200 | bytes 3932160 | tf_op jit(solution)/shard_map/corner/pallas_call | solution.py:588
  (4 shorter events, 0.1 us)
Async XLA Ops:
  0.0 8.2 %copy-start = (bf16[24,64,640]{2,1,0:T(8,128)(2,1)S(1)}, bf16[24,64,640]{2,1,0:T(8,128)(2,1)}, u32[]{:S(2)}) copy-start(bf16[24,64,640]{2,1,0:T(8,128)(2,1)} %x_ref.5) | copy-start | bytes 5898244
  0.0 8.2 %copy-start.1 = (f32[5,640]{1,0:T(8,128)S(1)}, f32[5,640]{1,0:T(8,128)}, u32[]{:S(2)}) copy-start(f32[5,640]{1,0:T(8,128)} %one_ref.5) | copy-start | bytes 38404
  0.0 8.2 %copy-start.2 = (f32[5,640]{1,0:T(8,128)S(1)}, f32[5,640]{1,0:T(8,128)}, u32[]{:S(2)}) copy-start(f32[5,640]{1,0:T(8,128)} %two_ref.5) | copy-start | bytes 38404
  2.6 11.2 %collective-permute-start = (bf16[33,8,640]{2,1,0:T(8,128)(2,1)}, bf16[33,8,640]{2,1,0:T(8,128)(2,1)S(1)}, u32[]{:S(2)}, u32[]{:S(2)}) collective-permute-start(bf16[33,8,640]{2,1,0:T(8,128)(2,1)} %get-tuple-element.25), channel_id=1, source_target_pairs={{0,8},{1,9},{2,10},{3,11},{4,12},{5,13},{6,14},{7,15},{8,0},{9,1},... | collective-permute-start | bytes 1013768 | tf_op jit(solution)/shard_map/ppermute | solution.py:532
  5.7 8.1 %collective-permute-start.1 = (bf16[33,8,640]{2,1,0:T(8,128)(2,1)}, bf16[33,8,640]{2,1,0:T(8,128)(2,1)S(1)}, u32[]{:S(2)}, u32[]{:S(2)}) collective-permute-start(bf16[33,8,640]{2,1,0:T(8,128)(2,1)} %get-tuple-element.26), channel_id=1, source_target_pairs={{8,16},{9,17},{10,18},{11,19},{12,20},{13,21},{14,22},{15,23},{16,... | collective-permute-start | bytes 1013768 | tf_op jit(solution)/shard_map/ppermute | solution.py:532
  5.7 8.1 %collective-permute-start.2 = (bf16[33,8,640]{2,1,0:T(8,128)(2,1)}, bf16[33,8,640]{2,1,0:T(8,128)(2,1)S(1)}, u32[]{:S(2)}, u32[]{:S(2)}) collective-permute-start(bf16[33,8,640]{2,1,0:T(8,128)(2,1)} %get-tuple-element.27), channel_id=1, source_target_pairs={{16,24},{17,25},{18,26},{19,27},{20,28},{21,29},{22,30},{23,31},{2... | collective-permute-start | bytes 1013768 | tf_op jit(solution)/shard_map/ppermute | solution.py:532
  6.2 9.6 %collective-permute-start.3 = (bf16[24,8,640]{2,1,0:T(8,128)(2,1)}, bf16[24,8,640]{2,1,0:T(8,128)(2,1)S(1)}, u32[]{:S(2)}, u32[]{:S(2)}) collective-permute-start(bf16[24,8,640]{2,1,0:T(8,128)(2,1)} %get-tuple-element.33), channel_id=1, source_target_pairs={{1,2},{3,4},{5,6},{7,0},{2,1},{4,3},{6,5},{0,7},{9,10},{11,12},{13... | collective-permute-start | bytes 737288 | tf_op jit(solution)/shard_map/ppermute | solution.py:533
  13.9 5.4 %collective-permute-start.4 = (bf16[64,640]{1,0:T(8,128)(2,1)S(1)}, bf16[64,640]{1,0:T(8,128)(2,1)S(1)}, u32[]{:S(2)}, u32[]{:S(2)}) collective-permute-start(bf16[64,640]{1,0:T(8,128)(2,1)S(1)} %maximum_bitcast_fusion), channel_id=1, source_target_pairs={{1,2},{3,4},{5,6},{7,0},{2,1},{4,3},{6,5},{0,7},{9,10},{11,12},{13... | collective-permute-start | bytes 245768 | tf_op jit(solution)/shard_map/ppermute | solution.py:565
  15.2 4.2 %collective-permute-start.5 = (bf16[64,640]{1,0:T(8,128)(2,1)S(1)}, bf16[64,640]{1,0:T(8,128)(2,1)S(1)}, u32[]{:S(2)}, u32[]{:S(2)}) collective-permute-start(bf16[64,640]{1,0:T(8,128)(2,1)S(1)} %maximum_bitcast_fusion.1), channel_id=1, source_target_pairs={{0,1},{2,3},{4,5},{6,7},{1,0},{3,2},{5,4},{7,6},{8,9},{10,11},{12,... | collective-permute-start | bytes 245768 | tf_op jit(solution)/shard_map/ppermute | solution.py:565

commit v12 on v11

--- a/solution.py
+++ b/solution.py
@@ -154,7 +154,7 @@
         pltpu.make_async_copy(groups_ref.at[:, near_at], payloads.at[2, pl.ds(0, rows)], sems.at[5]),
         pltpu.make_async_copy(groups_ref.at[:, far_at], far, sems.at[6]),
     ]
-    for copy in copies[:2] + small + copies[2:]:
+    for copy in copies + small:
         copy.start()
     padded[...] = jnp.zeros_like(padded)
     tags[...] = jnp.zeros_like(tags)

time: 21.1 us -> 21 us (level)
  transfers between devices with their start and end apart: 6 -> 6, of which waited for: 2 -> 2; matrix products, arithmetic and copies ran while one was open for 0% -> 0% of each run, Pallas kernels for 39% -> 40%
where the time goes in v12:
time: 21 us; the launch traced here: 20.9 us
  Pallas kernels  12.4 us (59%)
  starting transfers between devices  7.56 us (36%)
  waiting for transfers between devices  0.79 us (4%)
    pallas_call x1, Pallas kernels, per_device(): pl.pallas_call(functools.partial(inner_kernel, block), out_shape=(array(r...  5.1 us
    ppermute x3, starting transfers between devices, per_device(): lax.ppermute(v, both, turn_swaps(lat_peers, lon_peers, j))  3.6 us
    pallas_call x1, Pallas kernels, per_device(): pl.pallas_call(functools.partial(rim_kernel, block), out_shape=(array(2 *...  3.18 us
    pallas_call x1, Pallas kernels, per_device(): pl.pallas_call(prep_kernel, out_shape=(array(edge + 1, CELLS, channels),)...  2.49 us
    ppermute x1, starting transfers between devices, per_device(): lon_b = lax.ppermute(lon_b, 'lon', swaps(lon_peers, True))  2.05 us
    ppermute x2, starting transfers between devices, corner_send(): return lax.ppermute(sent, 'lon', swaps(lon_peers, second))  1.9 us
    pallas_call x1, Pallas kernels, per_device(): pl.pallas_call(corner_kernel, out_shape=array(rows, cells, channels), in_...  1.63 us
    ppermute x3, waiting for transfers between devices, per_device(): lax.ppermute(v, both, turn_swaps(lat_peers, lon_peers, j))  0.46 us
  transfers between devices with their start and end apart: 6, of which 2 were waited for; matrix products, arithmetic and copies ran while one was open for 0% of the time, Pallas kernels for 40%

profile of v12, /device:TPU:0, one launch (start us, length us, event | category | flops | bytes accessed | tf_op | source)
XLA Modules:
  0.0 20.9 jit_solution(2518271782826557287)
XLA Ops:
  0.0 0.0 copy-start
  0.0 0.0 copy-start.1
  0.0 0.0 copy-start.2
  0.0 2.5 %prep.1 = (bf16[33,8,640]{2,1,0:T(8,128)(2,1)}, bf16[33,8,640]{2,1,0:T(8,128)(2,1)}, bf16[33,8,640]{2,1,0:T(8,128)(2,1)}, bf16[24,8,640]{2,1,0:T(8,128)(2,1)}, f32[5,24,128]{2,1,0:T(8,128)S(1)}) custom-call(bf16[192,8,640]{2,1,0:T(8,128)(2,1)} %bitcast.9, bf16[24,8,8,640]{3,2,1,0:T(8,128)(2,1)} %bitcast.10, f32[5,9,5,24]{3,2,1,0:T(8,128)} %bitcast.11, ...), custom_call_target="tpu_custom_call" | custom-call | bytes 1310720 | tf_op jit(solution)/shard_map/prep/pallas_call | solution.py:511
  2.5 3.1 %collective-permute-start = (bf16[33,8,640]{2,1,0:T(8,128)(2,1)}, bf16[33,8,640]{2,1,0:T(8,128)(2,1)S(1)}, u32[]{:S(2)}, u32[]{:S(2)}) collective-permute-start(bf16[33,8,640]{2,1,0:T(8,128)(2,1)} %get-tuple-element.25), channel_id=1, source_target_pairs={{0,8},{1,9},{2,10},{3,11},{4,12},{5,13},{6,14},{7,15},{8,0},{9,1},... | collective-permute-start | bytes 1013768 | tf_op jit(solution)/shard_map/ppermute | solution.py:532
  5.6 0.0 collective-permute-start.1
  5.6 0.5 %collective-permute-start.2 = (bf16[33,8,640]{2,1,0:T(8,128)(2,1)}, bf16[33,8,640]{2,1,0:T(8,128)(2,1)S(1)}, u32[]{:S(2)}, u32[]{:S(2)}) collective-permute-start(bf16[33,8,640]{2,1,0:T(8,128)(2,1)} %get-tuple-element.27), channel_id=1, source_target_pairs={{16,24},{17,25},{18,26},{19,27},{20,28},{21,29},{22,30},{23,31},{2... | collective-permute-start | bytes 1013768 | tf_op jit(solution)/shard_map/ppermute | solution.py:532
  6.1 2.1 %collective-permute-start.3 = (bf16[24,8,640]{2,1,0:T(8,128)(2,1)}, bf16[24,8,640]{2,1,0:T(8,128)(2,1)S(1)}, u32[]{:S(2)}, u32[]{:S(2)}) collective-permute-start(bf16[24,8,640]{2,1,0:T(8,128)(2,1)} %get-tuple-element.33), channel_id=1, source_target_pairs={{1,2},{3,4},{5,6},{7,0},{2,1},{4,3},{6,5},{0,7},{9,10},{11,12},{13... | collective-permute-start | bytes 737288 | tf_op jit(solution)/shard_map/ppermute | solution.py:533
  8.2 0.0 copy-done
  8.2 0.0 copy-done.1
  8.2 0.0 copy-done.2
  8.2 5.1 %inner.1 = (bf16[960,256]{1,0:T(8,128)(2,1)S(1)}, bf16[320,256]{1,0:T(8,128)(2,1)S(1)}, bf16[320,256]{1,0:T(8,128)(2,1)S(1)}, bf16[8,64,640]{2,1,0:T(8,128)(2,1)...) custom-call(bf16[24,64,640]{2,1,0:T(8,128)(2,1)S(1)} %copy-done, ...), custom_call_target="tpu_custom_call" | custom-call | flops 2831155200 | bytes 3932160 | tf_op jit(solution)/shard_map/inner/pallas_call | solution.py:538
  13.3 0.5 %collective-permute-done.turn_0 = bf16[33,8,640]{2,1,0:T(8,128)(2,1)S(1)} collective-permute-done((bf16[33,8,640]{2,1,0:T(8,128)(2,1)}, bf16[33,8,640]{2,1,0:T(8,128)(2,1)S(1)}, u32[]{:S(2)}, u32[]{:S(2)}) %collective-permute-start) | collective-permute-done | bytes 337952 | tf_op jit(solution)/shard_map/ppermute | solution.py:532
  13.7 0.0 collective-permute-done.1.turn_1
  13.7 0.0 collective-permute-done.2.turn_2
  13.8 1.2 %collective-permute-start.4 = (bf16[64,640]{1,0:T(8,128)(2,1)S(1)}, bf16[64,640]{1,0:T(8,128)(2,1)S(1)}, u32[]{:S(2)}, u32[]{:S(2)}) collective-permute-start(bf16[64,640]{1,0:T(8,128)(2,1)S(1)} %maximum_bitcast_fusion), channel_id=1, source_target_pairs={{1,2},{3,4},{5,6},{7,0},{2,1},{4,3},{6,5},{0,7},{9,10},{11,12},{13... | collective-permute-start | bytes 245768 | tf_op jit(solution)/shard_map/ppermute | solution.py:565
  15.1 0.7 %collective-permute-start.5 = (bf16[64,640]{1,0:T(8,128)(2,1)S(1)}, bf16[64,640]{1,0:T(8,128)(2,1)S(1)}, u32[]{:S(2)}, u32[]{:S(2)}) collective-permute-start(bf16[64,640]{1,0:T(8,128)(2,1)S(1)} %maximum_bitcast_fusion.1), channel_id=1, source_target_pairs={{0,1},{2,3},{4,5},{6,7},{1,0},{3,2},{5,4},{7,6},{8,9},{10,11},{12,... | collective-permute-start | bytes 245768 | tf_op jit(solution)/shard_map/ppermute | solution.py:565
  15.8 0.0 collective-permute-done.3.lon_b
  15.8 3.2 %rim.1 = (bf16[320,256]{1,0:T(8,128)(2,1)S(1)}, bf16[8,64,640]{2,1,0:T(8,128)(2,1)S(1)}, bf16[2,16,16,640]{3,2,1,0:T(8,128)(2,1)S(1)}, bf16[2,16,16,640]{3,2,1,0:T(8,128)(2,1)S(1)}) custom-call(bf16[24,64,640]{2,1,0:T(8,128)(2,1)S(1)} %copy-done, bf16[33,8,640]{2,1,0:T(8,128)(2,1)S(1)} %collective-permute-done.turn_0, ...), custom_call_target="tpu_custom_call" | custom-call | flops 2831155200 | bytes 3932160 | tf_op jit(solution)/shard_map/rim/pallas_call | solution.py:569
  18.9 0.3 %collective-permute-done.4.corner_b = bf16[64,640]{1,0:T(8,128)(2,1)S(1)} collective-permute-done((bf16[64,640]{1,0:T(8,128)(2,1)S(1)}, bf16[64,640]{1,0:T(8,128)(2,1)S(1)}, u32[]{:S(2)}, u32[]{:S(2)}) %collective-permute-start.4) | collective-permute-done | bytes 81952 | tf_op jit(solution)/shard_map/ppermute | solution.py:565
  19.3 0.0 collective-permute-done.5.corner_a
  19.3 1.6 %corner.1 = bf16[24,64,640]{2,1,0:T(8,128)(2,1)} custom-call(bf16[24,64,640]{2,1,0:T(8,128)(2,1)S(1)} %copy-done, bf16[33,8,640]{2,1,0:T(8,128)(2,1)S(1)} %collective-permute-done.turn_0, bf16[33,8,640]{2,1,0:T(8,128)(2,1)S(1)} %collective-permute-done.1.turn_1, ...), custom_call_target="tpu_custom_call", output_to_operand_aliasing={{}: (14, {})} | custom-call | flops 2831155200 | bytes 3932160 | tf_op jit(solution)/shard_map/corner/pallas_call | solution.py:588
  (4 shorter events, 0.1 us)
Async XLA Ops:
  0.0 8.2 %copy-start = (bf16[24,64,640]{2,1,0:T(8,128)(2,1)S(1)}, bf16[24,64,640]{2,1,0:T(8,128)(2,1)}, u32[]{:S(2)}) copy-start(bf16[24,64,640]{2,1,0:T(8,128)(2,1)} %x_ref.5) | copy-start | bytes 5898244
  0.0 8.2 %copy-start.1 = (f32[5,640]{1,0:T(8,128)S(1)}, f32[5,640]{1,0:T(8,128)}, u32[]{:S(2)}) copy-start(f32[5,640]{1,0:T(8,128)} %one_ref.5) | copy-start | bytes 38404
  0.0 8.2 %copy-start.2 = (f32[5,640]{1,0:T(8,128)S(1)}, f32[5,640]{1,0:T(8,128)}, u32[]{:S(2)}) copy-start(f32[5,640]{1,0:T(8,128)} %two_ref.5) | copy-start | bytes 38404
  2.5 11.2 %collective-permute-start = (bf16[33,8,640]{2,1,0:T(8,128)(2,1)}, bf16[33,8,640]{2,1,0:T(8,128)(2,1)S(1)}, u32[]{:S(2)}, u32[]{:S(2)}) collective-permute-start(bf16[33,8,640]{2,1,0:T(8,128)(2,1)} %get-tuple-element.25), channel_id=1, source_target_pairs={{0,8},{1,9},{2,10},{3,11},{4,12},{5,13},{6,14},{7,15},{8,0},{9,1},... | collective-permute-start | bytes 1013768 | tf_op jit(solution)/shard_map/ppermute | solution.py:532
  5.6 8.1 %collective-permute-start.1 = (bf16[33,8,640]{2,1,0:T(8,128)(2,1)}, bf16[33,8,640]{2,1,0:T(8,128)(2,1)S(1)}, u32[]{:S(2)}, u32[]{:S(2)}) collective-permute-start(bf16[33,8,640]{2,1,0:T(8,128)(2,1)} %get-tuple-element.26), channel_id=1, source_target_pairs={{8,16},{9,17},{10,18},{11,19},{12,20},{13,21},{14,22},{15,23},{16,... | collective-permute-start | bytes 1013768 | tf_op jit(solution)/shard_map/ppermute | solution.py:532
  5.6 8.1 %collective-permute-start.2 = (bf16[33,8,640]{2,1,0:T(8,128)(2,1)}, bf16[33,8,640]{2,1,0:T(8,128)(2,1)S(1)}, u32[]{:S(2)}, u32[]{:S(2)}) collective-permute-start(bf16[33,8,640]{2,1,0:T(8,128)(2,1)} %get-tuple-element.27), channel_id=1, source_target_pairs={{16,24},{17,25},{18,26},{19,27},{20,28},{21,29},{22,30},{23,31},{2... | collective-permute-start | bytes 1013768 | tf_op jit(solution)/shard_map/ppermute | solution.py:532
  6.1 9.6 %collective-permute-start.3 = (bf16[24,8,640]{2,1,0:T(8,128)(2,1)}, bf16[24,8,640]{2,1,0:T(8,128)(2,1)S(1)}, u32[]{:S(2)}, u32[]{:S(2)}) collective-permute-start(bf16[24,8,640]{2,1,0:T(8,128)(2,1)} %get-tuple-element.33), channel_id=1, source_target_pairs={{1,2},{3,4},{5,6},{7,0},{2,1},{4,3},{6,5},{0,7},{9,10},{11,12},{13... | collective-permute-start | bytes 737288 | tf_op jit(solution)/shard_map/ppermute | solution.py:533
  13.8 5.4 %collective-permute-start.4 = (bf16[64,640]{1,0:T(8,128)(2,1)S(1)}, bf16[64,640]{1,0:T(8,128)(2,1)S(1)}, u32[]{:S(2)}, u32[]{:S(2)}) collective-permute-start(bf16[64,640]{1,0:T(8,128)(2,1)S(1)} %maximum_bitcast_fusion), channel_id=1, source_target_pairs={{1,2},{3,4},{5,6},{7,0},{2,1},{4,3},{6,5},{0,7},{9,10},{11,12},{13... | collective-permute-start | bytes 245768 | tf_op jit(solution)/shard_map/ppermute | solution.py:565
  15.1 4.2 %collective-permute-start.5 = (bf16[64,640]{1,0:T(8,128)(2,1)S(1)}, bf16[64,640]{1,0:T(8,128)(2,1)S(1)}, u32[]{:S(2)}, u32[]{:S(2)}) collective-permute-start(bf16[64,640]{1,0:T(8,128)(2,1)S(1)} %maximum_bitcast_fusion.1), channel_id=1, source_target_pairs={{0,1},{2,3},{4,5},{6,7},{1,0},{3,2},{5,4},{7,6},{8,9},{10,11},{12,... | collective-permute-start | bytes 245768 | tf_op jit(solution)/shard_map/ppermute | solution.py:565
